TPU v7x, 256 devices: a whole 4x4x8 slice. The times are simulated.
256 devices in a mesh: dom: 64 (over x, z, core), mp: 4 (over y).
Axes of the slice: x: 4, y: 4, z: 8, core: 2. Of those that a mesh axis runs over, the one named last changes fastest.
Arguments:
- hidden_states: bfloat16 [32768, 768], P('dom'), may hold values from -6.5 to 6.5
- text_len: int32 [256], P('dom'), may hold values from 16 to 128
- w_qkv: bfloat16 [768, 3, 768], P(None, None, 'mp'), may hold values from -8 to 8
- w_out: bfloat16 [768, 768], P('mp'), may hold values from -0.21875 to 0.21875
- w_up: bfloat16 [768, 3072], P(None, 'mp'), may hold values from -0.21875 to 0.21875
- w_down: bfloat16 [3072, 768], P('mp'), may hold values from -0.109375 to 0.109375
- hist: bfloat16 [16384, 768], P('dom'), may hold values from -16 to 16
- nbr: int32 [16384, 10], P('dom'), may hold values from 0 to 1279, as said below
- send_rows: int32 [64, 64, 16], P('dom'), may hold values from -1 to 255, as said below
- fresh_target: int32 [256], replicated, may hold values from 0 to 16383, as said below
- w_self: bfloat16 [768, 768], P(None, 'mp'), may hold values from -0.21875 to 0.21875
- w_neigh: bfloat16 [768, 768], P(None, 'mp'), may hold values from -0.21875 to 0.21875
- upstream: bfloat16 [16384, 768], P('dom', 'mp'), may hold values from -6 to 6
Outputs:
- sage_out: bfloat16 [16384, 768], P('dom', 'mp')
- grad_fresh: float32 [256, 768], P('dom', 'mp')
- grad_self_w: float32 [768, 768], P('dom', 'mp')
- grad_neigh_w: float32 [768, 768], P('dom', 'mp')
Inputs may be any that keep to these rules, and one draw needn't show every extreme that they name: `send_rows`: within each list the filled slots come first and -1 marks the unused ones; no partition lists rows for itself; every partition sends one row or more to every other, and for every partition some list to another partition fills all 16 slots. `nbr`: an entry below 256 is a local row of the node's partition; an entry 256 + q * 16 + c reads slot c of the list partition q sends to the node's partition, always a filled slot of another partition's list. `fresh_target`: distinct rows; each partition owns exactly 4 of them.
All inputs are finite; a program needn't handle non-finite values.
Results may differ from a plain program's by a relative error of at most 0.015.
Values may be sent and summed in bfloat16 or wider, within the bound.
No kernel may reach another device: no remote copies, remote signals or barrier semaphores. Data moves between devices by JAX's collectives and lax.ppermute only.
A program may use at most 64 MiB of HBM per device.

v0:
```python
import math

import jax
import jax.numpy as jnp
from jax import lax
from jax.sharding import PartitionSpec as P

HEADS = 12


EPSILON = 1e-05


def layer_norm(values):
    center = values - jnp.mean(values, axis=-1, keepdims=True)
    spread = jnp.mean(center * center, axis=-1, keepdims=True)
    return center * lax.rsqrt(spread + EPSILON)


def exact_gelu(values):
    return jax.nn.gelu(values, approximate=False)


def attend(rows, lengths, weights_qkv):
    model_width = rows.shape[1]
    text_count = lengths.shape[0]
    length = rows.shape[0] // text_count
    local_width = weights_qkv.shape[2]
    head_dim = model_width // HEADS
    head_count = local_width // head_dim
    packed = jnp.dot(
        rows, weights_qkv.reshape(model_width, 3 * local_width), preferred_element_type=jnp.float32
    ).astype(jnp.bfloat16)
    packed = packed.reshape(text_count, length, 3, head_count, head_dim)
    scores = jnp.einsum(
        "tqhc,tkhc->thqk", packed[:, :, 0], packed[:, :, 1], preferred_element_type=jnp.float32
    ) / math.sqrt(head_dim)
    live_keys = jnp.arange(length)[None, :] < lengths[:, None]
    scores = jnp.where(live_keys[:, None, None, :], scores, -1e30)
    row_peak = jnp.max(scores, axis=-1, keepdims=True)
    weights = jnp.exp(scores - row_peak)
    attention_probs = (weights / jnp.sum(weights, axis=-1, keepdims=True)).astype(jnp.bfloat16)
    context = jnp.einsum(
        "thqk,tkhc->tqhc", attention_probs, packed[:, :, 2], preferred_element_type=jnp.float32
    )
    return context.astype(jnp.bfloat16).reshape(text_count * length, local_width)


def encode_block(hidden_states, text_len, w_qkv, w_out, w_up, w_down):
    model_width = hidden_states.shape[1]
    text_count = text_len.shape[0]
    length = hidden_states.shape[0] // text_count
    shares = lax.axis_size("mp")
    share_rows = text_count * length // shares
    position = lax.axis_index("mp")
    own_texts = share_rows // length
    own_len = lax.dynamic_slice_in_dim(text_len, position * own_texts, own_texts, 0)
    residual = lax.dynamic_slice_in_dim(hidden_states, position * share_rows, share_rows, 0)
    context = attend(hidden_states, text_len, w_qkv)
    attended = lax.psum_scatter(
        jnp.dot(context, w_out, preferred_element_type=jnp.float32).astype(jnp.bfloat16),
        "mp",
        scatter_dimension=0,
        tiled=True,
    ).astype(jnp.float32)
    first_norm = layer_norm(residual.astype(jnp.float32) + attended).astype(jnp.bfloat16)
    inner_act = exact_gelu(
        jnp.dot(
            lax.all_gather(first_norm, "mp", axis=0, tiled=True),
            w_up,
            preferred_element_type=jnp.float32,
        )
    ).astype(jnp.bfloat16)
    partial_sums = jnp.dot(inner_act, w_down, preferred_element_type=jnp.float32)
    summed = lax.psum_scatter(
        partial_sums.astype(jnp.bfloat16), "mp", scatter_dimension=0, tiled=True
    ).astype(jnp.float32)
    second_norm = layer_norm(first_norm.astype(jnp.float32) + summed)
    second_norm = second_norm.reshape(own_texts, length, model_width)
    own_live = jnp.arange(length)[None, :] < own_len[:, None]
    pooled = jnp.sum(jnp.where(own_live[:, :, None], second_norm, 0.0), axis=1) / own_len[
        :, None
    ].astype(jnp.float32)
    return pooled.astype(jnp.bfloat16)


def local(
    hidden_states,
    text_len,
    w_qkv,
    w_out,
    w_up,
    w_down,
    hist,
    nbr,
    send_rows,
    fresh_target,
    w_self,
    w_neigh,
    upstream,
):
    fresh_local = encode_block(hidden_states, text_len, w_qkv, w_out, w_up, w_down)
    fresh_all = lax.all_gather(fresh_local, ("dom", "mp"), axis=0, tiled=True)
    node_count = hist.shape[0]
    model_width = hist.shape[1]
    quarter = w_self.shape[1]
    first_node = lax.axis_index("dom") * node_count
    fresh_slot = fresh_target - first_node
    owned = (fresh_slot >= 0) & (fresh_slot < node_count)
    table = hist.at[jnp.where(owned, fresh_slot, node_count)].set(fresh_all, mode="drop")
    wanted = send_rows[0]
    filled = wanted >= 0
    source_rows = jnp.maximum(wanted, 0)
    peer_count = wanted.shape[0]
    slot_count = wanted.shape[1]
    outgoing = jnp.where(filled[:, :, None], table[source_rows], jnp.zeros((), table.dtype))
    received = lax.all_to_all(outgoing, "dom", split_axis=0, concat_axis=0, tiled=True)
    extended = jnp.concatenate(
        [table, received.reshape(peer_count * slot_count, model_width)], axis=0
    )
    fanout = nbr.shape[1]
    total = jnp.zeros((node_count, model_width), jnp.float32)
    for neighbour in range(fanout):
        total = total + extended[nbr[:, neighbour]].astype(jnp.float32)
    agg_rows = (total / fanout).astype(jnp.bfloat16)
    pre_act = jnp.dot(table, w_self, preferred_element_type=jnp.float32) + jnp.dot(
        agg_rows, w_neigh, preferred_element_type=jnp.float32
    )
    activated, pull_back = jax.vjp(exact_gelu, pre_act)
    sage_out = activated.astype(jnp.bfloat16)
    grad_pre = pull_back(upstream.astype(jnp.float32))[0].astype(jnp.bfloat16)
    contract = (((0,), (0,)), ((), ()))
    part_self = lax.dot_general(table, grad_pre, contract, preferred_element_type=jnp.float32)
    part_neigh = lax.dot_general(agg_rows, grad_pre, contract, preferred_element_type=jnp.float32)
    weight_grads = lax.psum_scatter(
        jnp.concatenate([part_self, part_neigh], axis=1), "dom", scatter_dimension=0, tiled=True
    )
    grad_self_w = weight_grads[:, :quarter]
    grad_neigh_w = weight_grads[:, quarter:]
    contract_out = (((1,), (1,)), ((), ()))
    self_terms = lax.dot_general(grad_pre, w_self, contract_out, preferred_element_type=jnp.float32)
    neigh_terms = lax.dot_general(
        grad_pre, w_neigh, contract_out, preferred_element_type=jnp.float32
    )
    grad_self, grad_agg = (
        lax.psum_scatter(
            self_terms.astype(jnp.bfloat16), "mp", scatter_dimension=1, tiled=True
        ).astype(jnp.float32),
        lax.psum_scatter(
            neigh_terms.astype(jnp.bfloat16), "mp", scatter_dimension=1, tiled=True
        ).astype(jnp.float32),
    )
    grad_total = grad_agg / fanout
    grad_extended = jnp.zeros((extended.shape[0], quarter), jnp.float32)
    for neighbour in range(fanout):
        grad_extended = grad_extended.at[nbr[:, neighbour]].add(grad_total)
    halo_grad = grad_extended[node_count:].reshape(peer_count, slot_count, quarter)
    returned = lax.all_to_all(
        halo_grad.astype(jnp.bfloat16), "dom", split_axis=0, concat_axis=0, tiled=True
    ).astype(halo_grad.dtype)
    target_rows = jnp.where(filled, wanted, node_count).reshape(peer_count * slot_count)
    grad_table = (
        (grad_self + grad_extended[:node_count])
        .at[target_rows]
        .add(returned.reshape(peer_count * slot_count, quarter), mode="drop")
    )
    fresh_terms = jnp.where(
        owned[:, None], grad_table[jnp.clip(fresh_slot, 0, node_count - 1)], 0.0
    )
    grad_fresh = lax.psum_scatter(fresh_terms, "dom", scatter_dimension=0, tiled=True)
    return (sage_out, grad_fresh, grad_self_w, grad_neigh_w)


def solution(mesh):
    in_specs = (
        P("dom", None),
        P("dom"),
        P(None, None, "mp"),
        P("mp", None),
        P(None, "mp"),
        P("mp", None),
        P("dom", None),
        P("dom", None),
        P("dom", None, None),
        P(),
        P(None, "mp"),
        P(None, "mp"),
        P("dom", "mp"),
    )
    out_specs = (P("dom", "mp"), P("dom", "mp"), P("dom", "mp"), P("dom", "mp"))
    return jax.shard_map(local, mesh=mesh, in_specs=in_specs, out_specs=out_specs, check_vma=False)
```

profile of v0, /device:TPU:32, one launch (start us, length us, event | category | flops | bytes accessed | tf_op | source)
XLA Modules:
  0.0 583.5 jit_solution(14225084938537878831)
XLA Ops:
  13.3 27.7 %reduce-scatter.7.cloned.1.call-done = bf16[128,768]{1,0:T(8,128)(2,1)} async-done(((bf16[512,768]{1,0:T(8,128)(2,1)}), bf16[128,768]{1,0:T(8,128)(2,1)}) %reduce-scatter.7.cloned.1.call-update) | async-done | bytes 196624 | tf_op jit(solution)/shard_map/reduce_scatter | solution.py:60
  44.2 13.9 %all_gather.6 = bf16[512,768]{1,0:T(8,128)(2,1)S(1)} all-gather(bf16[128,768]{1,0:T(8,128)(2,1)S(1)} %multiply_convert_fusion.1), channel_id=1, replica_groups=mesh['dom'=64,'mp'=4] {'mp'}, dimensions={0}, use_global_device_ids=true | all-gather | bytes 983040 | tf_op jit(solution)/shard_map/all_gather | solution.py:69
  58.2 6.7 %convolution_convert_fusion = bf16[512,768]{1,0:T(8,128)(2,1)} fusion(bf16[768,768]{1,0:T(8,128)(2,1)S(1)} %copy-done, bf16[512,768]{1,0:T(8,128)(2,1)S(1)} %all_gather.6, bf16[768,768]{1,0:T(8,128)(2,1)} %param.17), kind=kOutput, calls=%fused_computation.47 | convolution fusion | flops 1233911808 | bytes 3932160 | tf_op jit(solution)/shard_map/dot_general | solution.py:74
  67.7 22.1 %reduce-scatter.9.cloned.1.call-done = bf16[128,768]{1,0:T(8,128)(2,1)} async-done(((bf16[512,768]{1,0:T(8,128)(2,1)}), bf16[128,768]{1,0:T(8,128)(2,1)}) %reduce-scatter.9.cloned.1.call-update) | async-done | bytes 196624 | tf_op jit(solution)/shard_map/reduce_scatter | solution.py:75
  93.1 127.7 %all-gather.1 = bf16[256,1,768]{2,1,0:T(2,128)(2,1)S(1)} all-gather(bf16[1,1,768]{2,1,0:T(2,128)(2,1)S(1)} %reshape.359), channel_id=2, replica_groups=mesh['dom'=64,'mp'=4] {'dom','mp'}, dimensions={0}, use_global_device_ids=true | all-gather | bytes 394752 | tf_op jit(solution)/shard_map/all_gather | solution.py:103
  222.7 4.0 gather_fusion
  228.1 12.5 %all-to-all-start = ((bf16[64,16,768]{2,1,0:T(8,128)(2,1)}), bf16[64,16,768]{2,1,0:T(8,128)(2,1)S(1)}, u32[]{:S(2)}, u32[]{:S(2)}) async-start(bf16[64,16,768]{2,1,0:T(8,128)(2,1)} %broadcast_select_fusion), calls=%async_computation.2 | async-start | bytes 3145728 | tf_op jit(solution)/shard_map/all_to_all | solution.py:117
  248.3 31.4 %all-to-all-done = bf16[64,16,768]{2,1,0:T(8,128)(2,1)S(1)} async-done(((bf16[64,16,768]{2,1,0:T(8,128)(2,1)}), bf16[64,16,768]{2,1,0:T(8,128)(2,1)S(1)}, u32[]{:S(2)}, u32[]{:S(2)}) %all-to-all-start) | async-done | bytes 1572896 | tf_op jit(solution)/shard_map/all_to_all | solution.py:117
  303.2 2.6 multiply_convert_fusion
  309.7 18.5 %reduce-scatter.13.cloned.1.call-done = bf16[256,192]{0,1:T(8,128)(2,1)} async-done(((bf16[256,768]{0,1:T(8,128)(2,1)}), bf16[256,192]{0,1:T(8,128)(2,1)}) %reduce-scatter.13.cloned.1.call-update) | async-done | bytes 98320 | tf_op jit(solution)/shard_map/reduce_scatter | solution.py:149
  329.2 2.4 scatter_custom_fusion.1
  331.7 2.6 scatter_fusion
  334.3 2.5 scatter_fusion.1
  336.8 2.5 scatter_fusion.2
  339.3 2.5 scatter_fusion.3
  341.8 2.5 scatter_fusion.4
  344.2 2.5 scatter_fusion.5
  346.7 2.5 scatter_fusion.6
  349.2 2.5 scatter_fusion.7
  351.6 2.5 scatter_fusion.8
  354.9 10.6 %all-to-all-start.1 = ((bf16[64,16,192]{2,1,0:T(8,128)(2,1)}), bf16[64,16,192]{2,1,0:T(8,128)(2,1)}, u32[]{:S(2)}, u32[]{:S(2)}) async-start(bf16[64,16,192]{2,1,0:T(8,128)(2,1)} %bitcast.21), calls=%async_computation.5 | async-start | bytes 1048576 | tf_op jit(solution)/shard_map/all_to_all | solution.py:158
  370.6 12.0 %all-to-all-done.1 = bf16[64,16,192]{2,1,0:T(8,128)(2,1)} async-done(((bf16[64,16,192]{2,1,0:T(8,128)(2,1)}), bf16[64,16,192]{2,1,0:T(8,128)(2,1)}, u32[]{:S(2)}, u32[]{:S(2)}) %all-to-all-start.1) | async-done | bytes 393248 | tf_op jit(solution)/shard_map/all_to_all | solution.py:158
  382.6 6.6 %scatter_custom_fusion.11 = f32[256,192]{1,0:T(8,128)S(1)} fusion(f32[256,192]{1,0:T(8,128)S(1)} %copy.94, s32[1024]{0:T(1024)S(1)} %bitcast.99, bf16[1024,192]{1,0:T(8,128)(2,1)} %bitcast.27), kind=kCustom, calls=%fused_computation.60 | custom fusion | flops 393216 | bytes 589824 | tf_op jit(solution)/shard_map/scatter-add | solution.py:165
  393.7 179.0 %all-reduce.5.cloned.1.call-done = (f32[256,192]{0,1:T(8,128)}, f32[768,384]{0,1:T(8,128)}) async-done(((f32[256,192]{0,1:T(8,128)}, f32[768,384]{0,1:T(8,128)}), (f32[256,192]{0,1:T(8,128)}, f32[768,384]{0,1:T(8,128)})) %all-reduce.5.cloned.1.call-update) | async-done | bytes 1376272
  (162 shorter events, 66.7 us)
Async XLA Ops:
  7.2 51.0 %copy-start = (bf16[768,768]{1,0:T(8,128)(2,1)S(1)}, bf16[768,768]{1,0:T(8,128)(2,1)}, u32[]{:S(2)}) copy-start(bf16[768,768]{1,0:T(8,128)(2,1)} %param.18) | copy-start | bytes 3538948
  7.2 33.8 %reduce-scatter.7.cloned.1.call-start = ((), (), s32[]{:S(2)}) async-start(), calls=%async_computation.6 | async-start | bytes 983040 | tf_op jit(solution)/shard_map/reduce_scatter | solution.py:60
  11.3 29.7 %copy-start.7 = (bf16[512,768]{1,0:T(8,128)(2,1)S(1)}, bf16[512,768]{1,0:T(8,128)(2,1)}, u32[]{:S(2)}) copy-start(bf16[512,768]{1,0:T(8,128)(2,1)} %param.13) | copy-start | bytes 2359300
  13.2 76.6 %reduce-scatter.9.cloned.1.call-start = ((), (), s32[]{:S(2)}) async-start(), calls=%async_computation.7 | async-start | bytes 983040 | tf_op jit(solution)/shard_map/reduce_scatter | solution.py:75
  58.2 8.0 %copy-start.13 = (s32[1,64,16]{1,2,0:T(8,128)S(1)}, s32[1,64,16]{1,2,0:T(8,128)}, u32[]{:S(2)}) copy-start(s32[1,64,16]{1,2,0:T(8,128)} %param.21) | copy-start | bytes 12292
  58.2 9.0 %copy-start.29 = (s32[256]{0:T(256)S(1)}, s32[256]{0:T(256)}, u32[]{:S(2)}) copy-start(s32[256]{0:T(256)} %param.22) | copy-start | bytes 3076
  64.9 156.0 %copy-start.1 = (bf16[256,768]{1,0:T(8,128)(2,1)S(1)}, bf16[256,768]{1,0:T(8,128)(2,1)}, u32[]{:S(2)}) copy-start(bf16[256,768]{1,0:T(8,128)(2,1)} %param.19) | copy-start | bytes 1179652
  228.1 13.2 %copy-start.26 = (s32[256,10]{0,1:T(8,128)S(1)}, s32[256,10]{0,1:T(8,128)}, u32[]{:S(2)}) copy-start(s32[256,10]{0,1:T(8,128)} %param.20) | copy-start | bytes 30724
  228.1 19.2 %copy-start.5 = (bf16[768,192]{0,1:T(8,128)(2,1)S(1)}, bf16[768,192]{0,1:T(8,128)(2,1)}, u32[]{:S(2)}) copy-start(bf16[768,192]{0,1:T(8,128)(2,1)} %param.23) | copy-start | bytes 884740
  228.1 51.6 %all-to-all-start = ((bf16[64,16,768]{2,1,0:T(8,128)(2,1)}), bf16[64,16,768]{2,1,0:T(8,128)(2,1)S(1)}, u32[]{:S(2)}, u32[]{:S(2)}) async-start(bf16[64,16,768]{2,1,0:T(8,128)(2,1)} %broadcast_select_fusion), calls=%async_computation.2 | async-start | bytes 3145728 | tf_op jit(solution)/shard_map/all_to_all | solution.py:117
  240.6 87.6 %reduce-scatter.13.cloned.1.call-start = ((), (), s32[]{:S(2)}) async-start(), calls=%async_computation.9 | async-start | bytes 491520 | tf_op jit(solution)/shard_map/reduce_scatter | solution.py:149
  241.3 38.4 %copy-start.14 = (s32[256,1]{0,1:T(1,128)}, s32[256,1]{0,1:T(1,128)S(1)}, u32[]{:S(2)}) copy-start(s32[256,1]{0,1:T(1,128)S(1)} %get-tuple-element.31) | copy-start | bytes 3076
  241.3 38.4 %copy-start.16 = (s32[256,1]{0,1:T(1,128)}, s32[256,1]{0,1:T(1,128)S(1)}, u32[]{:S(2)}) copy-start(s32[256,1]{0,1:T(1,128)S(1)} %get-tuple-element.32) | copy-start | bytes 3076
  241.4 38.4 %copy-start.18 = (s32[256,1]{0,1:T(1,128)}, s32[256,1]{0,1:T(1,128)S(1)}, u32[]{:S(2)}) copy-start(s32[256,1]{0,1:T(1,128)S(1)} %get-tuple-element.33) | copy-start | bytes 3076
  241.4 38.4 %copy-start.20 = (s32[256,1]{0,1:T(1,128)}, s32[256,1]{0,1:T(1,128)S(1)}, u32[]{:S(2)}) copy-start(s32[256,1]{0,1:T(1,128)S(1)} %get-tuple-element.34) | copy-start | bytes 3076
  241.4 38.4 %copy-start.22 = (s32[256,1]{0,1:T(1,128)}, s32[256,1]{0,1:T(1,128)S(1)}, u32[]{:S(2)}) copy-start(s32[256,1]{0,1:T(1,128)S(1)} %get-tuple-element.35) | copy-start | bytes 3076
  241.4 38.4 %copy-start.24 = (s32[256,1]{0,1:T(1,128)}, s32[256,1]{0,1:T(1,128)S(1)}, u32[]{:S(2)}) copy-start(s32[256,1]{0,1:T(1,128)S(1)} %get-tuple-element.36) | copy-start | bytes 3076
  241.4 38.4 %copy-start.28 = (s32[256,1]{0,1:T(1,128)}, s32[256,1]{0,1:T(1,128)S(1)}, u32[]{:S(2)}) copy-start(s32[256,1]{0,1:T(1,128)S(1)} %get-tuple-element.29) | copy-start | bytes 3076
  307.4 21.7 %copy-start.3 = (bf16[256,192]{0,1:T(8,128)(2,1)}, bf16[256,192]{0,1:T(8,128)(2,1)S(1)}, u32[]{:S(2)}) copy-start(bf16[256,192]{0,1:T(8,128)(2,1)S(1)} %get-tuple-element.22) | copy-start | bytes 294916
  308.5 61.0 %reduce-scatter.11.cloned.1.call-start = ((), (), s32[]{:S(2)}) async-start(), calls=%async_computation.8 | async-start | bytes 491520 | tf_op jit(solution)/shard_map/reduce_scatter | solution.py:146
  308.6 23.0 %copy-start.25 = (s32[256,1]{0,1:T(1,128)S(1)}, s32[256,1]{0,1:T(1,128)}, u32[]{:S(2)}) copy-start(s32[256,1]{0,1:T(1,128)} %copy-done.24) | copy-start | bytes 3076
  354.9 27.6 %all-to-all-start.1 = ((bf16[64,16,192]{2,1,0:T(8,128)(2,1)}), bf16[64,16,192]{2,1,0:T(8,128)(2,1)}, u32[]{:S(2)}, u32[]{:S(2)}) async-start(bf16[64,16,192]{2,1,0:T(8,128)(2,1)} %bitcast.21), calls=%async_computation.5 | async-start | bytes 1048576 | tf_op jit(solution)/shard_map/all_to_all | solution.py:158
  365.6 207.1 %all-reduce.5.cloned.1.call-start = ((), (), s32[]{:S(2)}) async-start(), calls=%async_computation.10 | async-start | bytes 2752512
  390.2 2.8 copy-start.11
  (17 other events, 36.5 us)
Sparse Core Ops, SparseCore 0:
  13.3 27.5 reduce-scatter.6
  65.0 24.7 reduce-scatter.8
  308.6 19.5 reduce-scatter.12
  330.7 23.1 reduce-scatter.10
  391.2 181.3 all-reduce.4
where the time goes:
time: 595 us; the launch traced here: 584 us
  waiting for transfers between devices  291 us (49%)
  blocking collectives  142 us (24%)
  other arithmetic  54.9 us (9%)
  local copies, waits for them, and re-layouts  37.2 us (6%)
  starting transfers between devices  24 us (4%)
  matrix products  18.3 us (3%)
  between operations  16.7 us (3%)
    unnamed x6, waiting for transfers between devices  179 us
    all_gather x1, blocking collectives, local(): fresh_all = lax.all_gather(fresh_local, ('dom', 'mp'), axis=0, tiled=True)  128 us
    all_to_all x1, waiting for transfers between devices, local(): lax.all_to_all(outgoing, 'dom', split_axis=0, concat_axis=0, tiled=True)  31.4 us
    reduce_scatter x1, waiting for transfers between devices, encode_block(): lax.psum_scatter(jnp.dot(context, w_out, preferred_element_type=jnp.float...  27.7 us
    scatter-add x10, other arithmetic, local(): grad_extended = grad_extended.at[nbr[:, neighbour]].add(grad_total)  24.7 us
    reduce_scatter x1, waiting for transfers between devices, encode_block(): lax.psum_scatter(partial_sums.astype(jnp.bfloat16), 'mp', scatter_dimensi...  22.1 us
    gather x10, local copies, waits for them, and re-layouts, local(): total = total + extended[nbr[:, neighbour]].astype(jnp.float32)  20.7 us
    reduce_scatter x1, waiting for transfers between devices, local(): lax.psum_scatter(neigh_terms.astype(jnp.bfloat16), 'mp', scatter_dimensio...  18.5 us
  transfers between devices with their start and end apart: 7, of which 6 were waited for; matrix products, arithmetic and copies ran while one was open for 7% of the time, Pallas kernels for 0%

commit v1 on v0

v1 whole, which is shorter than its diff:
```python
import math

import jax
import jax.numpy as jnp
from jax import lax
from jax.experimental import pallas as pl
from jax.experimental.pallas import tpu as pltpu
from jax.sharding import Mesh, PartitionSpec as P

HEADS = 12
EPSILON = 1e-05
NX, NZ, NC, NY = 4, 8, 2, 4
BF = jnp.bfloat16
F32 = jnp.float32


def layer_norm(values):
    center = values - jnp.mean(values, axis=-1, keepdims=True)
    spread = jnp.mean(center * center, axis=-1, keepdims=True)
    return center * lax.rsqrt(spread + EPSILON)


def exact_gelu(values):
    return 0.5 * values * (1.0 + lax.erf(values * math.sqrt(0.5)))


def dot(a, b):
    return jnp.dot(a, b, preferred_element_type=F32)


def dot_t(a, b):
    return lax.dot_general(a, b, (((0,), (0,)), ((), ())), preferred_element_type=F32)


def dot_nt(a, b):
    return lax.dot_general(a, b, (((1,), (1,)), ((), ())), preferred_element_type=F32)


def pull(value, axis, shift):
    count = {"x": NX, "z": NZ, "c": NC, "y": NY}[axis]
    return lax.ppermute(value, axis, [((i + shift) % count, i) for i in range(count)])


def whole(count):
    return [pl.BlockSpec(memory_space=pltpu.VMEM)] * count


def far_off(count):
    return [pl.BlockSpec(memory_space=pltpu.HBM)] * count


def scalars():
    return [pl.BlockSpec(memory_space=pltpu.SMEM)]


def grant(mib, flops, bytes_accessed):
    return {
        "compiler_params": pltpu.CompilerParams(vmem_limit_bytes=mib * 2**20),
        "cost_estimate": pl.CostEstimate(
            flops=flops, bytes_accessed=bytes_accessed, transcendentals=0
        ),
    }


def room(*arrays):
    return [pltpu.VMEM(a.shape, a.dtype) for a in arrays] + [pltpu.SemaphoreType.DMA((len(arrays),))]


def fetch(sources, targets, semaphores):
    copies = [
        pltpu.make_async_copy(source, target, semaphores.at[k])
        for k, (source, target) in enumerate(zip(sources, targets))
    ]
    for copy in copies:
        copy.start()
    return copies


DOM, CORE, ME, LENGTHS = 0, 1, 2, 3


def attend(rows, lengths, weights_qkv):
    model_width = rows.shape[1]
    text_count = lengths.shape[0]
    length = rows.shape[0] // text_count
    local_width = weights_qkv.shape[2]
    head_dim = model_width // HEADS
    head_count = local_width // head_dim
    packed = dot(rows, weights_qkv.reshape(model_width, 3 * local_width)).astype(BF)
    packed = packed.reshape(text_count, length, 3, head_count, head_dim)
    scores = jnp.einsum(
        "tqhc,tkhc->thqk", packed[:, :, 0], packed[:, :, 1], preferred_element_type=F32
    ) / math.sqrt(head_dim)
    live_keys = jnp.arange(length)[None, :] < lengths[:, None]
    scores = jnp.where(live_keys[:, None, None, :], scores, -1e30)
    row_peak = jnp.max(scores, axis=-1, keepdims=True)
    weights = jnp.exp(scores - row_peak)
    attention_probs = (weights / jnp.sum(weights, axis=-1, keepdims=True)).astype(BF)
    context = jnp.einsum(
        "thqk,tkhc->tqhc", attention_probs, packed[:, :, 2], preferred_element_type=F32
    )
    return context.astype(BF).reshape(text_count * length, local_width)


def norm_kernel(residual_ref, own_ref, near_ref, far_ref, across_ref, out_ref):
    total = residual_ref[...].astype(F32) + own_ref[...].astype(F32)
    for ref in (near_ref, far_ref, across_ref):
        total = total + ref[...].astype(F32)
    out_ref[...] = layer_norm(total).astype(BF)


def first_layer_norm(residual, parts):
    return pl.pallas_call(
        norm_kernel,
        out_shape=jax.ShapeDtypeStruct(residual.shape, BF),
        in_specs=whole(5),
        out_specs=whole(1)[0],
        name="first_norm",
        **grant(16, 4000000000, 1200000),
    )(residual, *parts)


def feed_kernel(block_ref, up_ref, down_ref, out_ref):
    inner = exact_gelu(dot(block_ref[...], up_ref[...])).astype(BF)
    out_ref[...] = dot(inner, down_ref[...]).astype(out_ref.dtype)


def feed_first_kernel(block_ref, up_hbm, down_hbm, out_ref, up_ref, down_ref, semaphores):
    copies = fetch((up_hbm, down_hbm), (up_ref, down_ref), semaphores)
    copies[0].wait()
    inner = exact_gelu(dot(block_ref[...], up_ref[...])).astype(BF)
    copies[1].wait()
    out_ref[...] = dot(inner, down_ref[...])


def feed_first(block, w_up, w_down):
    return pl.pallas_call(
        feed_first_kernel,
        out_shape=(
            jax.ShapeDtypeStruct(block.shape, F32),
            jax.ShapeDtypeStruct(w_up.shape, BF),
            jax.ShapeDtypeStruct(w_down.shape, BF),
        ),
        in_specs=whole(1) + far_off(2),
        out_specs=tuple(whole(3)),
        scratch_shapes=[pltpu.SemaphoreType.DMA((2,))],
        name="feed_first",
        **grant(16, 8000000000, 9000000),
    )(block, w_up, w_down)


def feed(block, w_up, w_down):
    return pl.pallas_call(
        feed_kernel,
        out_shape=jax.ShapeDtypeStruct(block.shape, BF),
        in_specs=whole(3),
        out_specs=whole(1)[0],
        name="feed",
        **grant(16, 8000000000, 9000000),
    )(block, w_up, w_down)


def pool_kernel(place_ref, first_ref, own_ref, near_ref, far_ref, across_ref, out_ref):
    total = first_ref[...].astype(F32) + own_ref[...]
    for ref in (near_ref, far_ref, across_ref):
        total = total + ref[...].astype(F32)
    normed = layer_norm(total)
    length = place_ref[LENGTHS + place_ref[ME]]
    live = lax.broadcasted_iota(jnp.int32, normed.shape, 0) < length
    pooled = jnp.sum(jnp.where(live, normed, 0.0), axis=0, keepdims=True)
    out_ref[...] = (pooled / length.astype(F32)).astype(BF)


def pooled_row(place, first_norm, parts):
    return pl.pallas_call(
        pool_kernel,
        out_shape=jax.ShapeDtypeStruct((1, first_norm.shape[1]), BF),
        in_specs=scalars() + whole(5),
        out_specs=whole(1)[0],
        name="pooled_row",
        **grant(16, 4000000000, 1200000),
    )(place, first_norm, *parts)


def spread_kernel(own_ref, near_ref, far_ref, across_ref, out_ref):
    refs = (own_ref, near_ref, far_ref, across_ref)
    index = lax.broadcasted_iota(jnp.int32, out_ref.shape[1:], 0)
    rows = jnp.zeros(out_ref.shape[1:], F32)
    for s, ref in enumerate(refs):
        rows = jnp.where(index == s, ref[...].astype(F32), rows)
    out_ref[...] = jnp.broadcast_to(rows.astype(BF)[None], out_ref.shape)


def spread_rows(rows, chips):
    return pl.pallas_call(
        spread_kernel,
        out_shape=jax.ShapeDtypeStruct((chips, len(rows), rows[0].shape[1]), BF),
        in_specs=whole(len(rows)),
        out_specs=whole(1)[0],
        name="spread_rows",
        **grant(16, 1000000, 200000),
    )(*rows)


def sliced(values, index, width):
    total = values[:, :width]
    for k in range(1, values.shape[1] // width):
        total = jnp.where(index == k, values[:, k * width : (k + 1) * width], total)
    return total


def text_rows(target, count, dom):
    shape = (count, target.shape[1])
    row_ids = lax.broadcasted_iota(jnp.int32, shape, 0) + dom * count
    text_ids = lax.broadcasted_iota(jnp.int32, shape, 1)
    holds = row_ids == target
    row_text = jnp.sum(jnp.where(holds, text_ids + 1, 0), axis=1, keepdims=True) - 1
    return holds.astype(F32).astype(BF), row_text


def slot_texts(texts, chips, core, me):
    slot = lax.broadcasted_iota(jnp.int32, (1, texts), 1)
    step = slot % NY
    slot_y = ((step ^ (step >> 1)) + me) % NY
    slot_core = (slot // (chips * NY) + core) % NC
    return ((slot // NY % chips) * NC + slot_core) * NY + slot_y


def outgoing_kernel(place_ref, target_ref, wanted_ref, hist_hbm, out_ref, hist_ref, semaphores):
    copies = fetch((hist_hbm,), (hist_ref,), semaphores)
    count, width = hist_ref.shape
    _, row_text = text_rows(target_ref[...], count, place_ref[DOM])
    column = lax.broadcasted_iota(jnp.int32, (count, width), 1)
    code = jnp.where(
        column == 0, 32 + row_text // 16, jnp.where(column == 1, 32 + row_text % 16, 0)
    ).astype(F32)
    ids = lax.broadcasted_iota(jnp.int32, (wanted_ref.shape[0], count), 1)
    pick = (wanted_ref[...] == ids).astype(F32).astype(BF)
    copies[0].wait()
    coded = jnp.where(row_text >= 0, code, hist_ref[...].astype(F32)).astype(BF)
    out_ref[...] = dot(pick, coded).astype(BF).reshape(out_ref.shape)


def outgoing_rows(place, target, wanted, hist, chips):
    rows, width = wanted.shape[0], hist.shape[1]
    return pl.pallas_call(
        outgoing_kernel,
        out_shape=jax.ShapeDtypeStruct((chips, NC, rows // chips // NC, width), BF),
        in_specs=scalars() + whole(2) + far_off(1),
        out_specs=pl.BlockSpec(),
        scratch_shapes=room(hist),
        name="outgoing_rows",
        **grant(52, 2000000000, 6000000),
    )(place, target, wanted, hist)


def halo_kernel(
    place_ref,
    target_hbm,
    links_hbm,
    hist_hbm,
    received_hbm,
    across_hbm,
    sum_ref,
    counts_slot_ref,
    counts_text_ref,
    target_ref,
    links_ref,
    hist_ref,
    received_ref,
    across_ref,
    semaphores,
):
    copies = fetch(
        (target_hbm, links_hbm, hist_hbm, received_hbm, across_hbm),
        (target_ref, links_ref, hist_ref, received_ref, across_ref),
        semaphores,
    )
    chips, slot_count, width = across_ref.shape
    size = chips * slot_count
    fanout, count = links_ref.shape
    texts = target_ref.shape[1]
    core, me = place_ref[CORE], place_ref[ME]
    slots = slot_texts(texts, chips, core, me)
    text_ids = lax.broadcasted_iota(jnp.int32, slots.shape, 1)
    copies[0].wait()
    copies[1].wait()
    place, row_text = text_rows(target_ref[...], count, place_ref[DOM])

    def counted(ids):
        total = jnp.zeros(ids.shape, F32)
        for neighbour in range(fanout):
            total = total + (links_ref[neighbour : neighbour + 1, :] == ids).astype(F32)
        return total.astype(BF)

    near = counted(lax.broadcasted_iota(jnp.int32, (count, count), 0))
    copies[2].wait()
    base = jnp.where(row_text >= 0, 0.0, hist_ref[...].astype(F32))
    total = dot_t(near, base.astype(BF))
    counts_slot = dot_t(near, (row_text == slots).astype(F32).astype(BF))
    counts_text = dot_t(near, place)
    copies[3].wait()
    copies[4].wait()
    for received, source in ((received_ref[:, core], core), (across_ref[...], 1 - core)):
        received = received.reshape(size, width)
        first = received[:, 0:128].astype(F32)
        is_text = first[:, 0:1] > 24
        text = ((first[:, 0:1] - 32) * 16 + first[:, 1:2] - 32).astype(jnp.int32)
        text = jnp.where(is_text, text, -1)
        halo = received * jnp.where(is_text, 0.0, 1.0).astype(BF)
        row = lax.broadcasted_iota(jnp.int32, (size, count), 0)
        row = (row // slot_count * NC + source) * slot_count + row % slot_count
        far = counted(row + count)
        total = total + dot_t(far, halo)
        counts_slot = counts_slot + dot_t(far, (text == slots).astype(F32).astype(BF))
        counts_text = counts_text + dot_t(far, (text == text_ids).astype(F32).astype(BF))
    sum_ref[...] = total
    counts_slot_ref[...] = counts_slot.astype(BF)
    counts_text_ref[...] = counts_text.astype(BF)


def halo_sums(place, received, across, target, links, hist):
    count = hist.shape[0]
    square = jax.ShapeDtypeStruct((count, target.shape[1]), BF)
    return pl.pallas_call(
        halo_kernel,
        out_shape=(jax.ShapeDtypeStruct(hist.shape, F32), square, square),
        in_specs=scalars() + far_off(5),
        out_specs=(pl.BlockSpec(),) * 3,
        scratch_shapes=room(target, links, hist, received, across),
        name="halo_sums",
        **grant(52, 1000000000, 5000000),
    )(place, target, links, hist, received, across)


def sage_kernel(
    fanout,
    share,
    own_texts,
    place_ref,
    fresh_ref,
    other_ref,
    *refs,
):
    sources, (sage_ref, keep_ref, send_ref), targets = refs[:8], refs[8:11], refs[11:-1]
    copies = fetch(sources, targets, refs[-1])
    target_ref, counts_slot_ref, counts_text_ref, sums_ref, hist_ref = targets[:5]
    w_self_ref, w_neigh_ref, upstream_ref = targets[5:]
    half = fresh_ref.shape[0]
    quarter, width = w_self_ref.shape
    count = hist_ref.shape[0]
    texts = target_ref.shape[1]
    core, me = place_ref[CORE], place_ref[ME]
    fresh, other = fresh_ref[...], other_ref[...]

    block = share + own_texts
    wide = keep_ref.shape[0]
    ids = lax.broadcasted_iota(jnp.int32, (width + texts, wide), 0)
    column = lax.broadcasted_iota(jnp.int32, (1, wide), 1)
    stand = []
    for side in (1 - core, core):
        owner, inside = column // block * NC + side, column % block
        row = jnp.where(
            inside < share, owner * share + inside, width + owner * own_texts + inside - share
        )
        stand.append((ids == row).astype(F32).astype(BF))

    for copy in copies[:4]:
        copy.wait()
    added = dot(counts_slot_ref[:, :half], fresh) + dot(counts_slot_ref[:, half:], other)
    agg_rows = ((sums_ref[...] + added) / fanout).astype(BF)
    copies[4].wait()
    place, row_text = text_rows(target_ref[...], count, place_ref[DOM])
    place_slot = (row_text == slot_texts(texts, half // NY, core, me)).astype(F32).astype(BF)
    placed = dot(place_slot[:, :half], fresh) + dot(place_slot[:, half:], other)
    table = jnp.where(row_text >= 0, placed, hist_ref[...].astype(F32)).astype(BF)
    for copy in copies[5:]:
        copy.wait()
    pre_act = dot_nt(table, w_self_ref[...]) + dot_nt(agg_rows, w_neigh_ref[...])
    cdf = 0.5 * (1.0 + lax.erf(pre_act * math.sqrt(0.5)))
    density = jnp.exp(-0.5 * pre_act * pre_act) * (1.0 / math.sqrt(2.0 * math.pi))
    sage_ref[...] = (pre_act * cdf).T.astype(BF)
    upstream = upstream_ref[...].astype(F32).T
    grad_pre = (upstream * (cdf + pre_act * density)).astype(BF)
    self_rows = jnp.concatenate([table, place], axis=1)
    neigh_rows = jnp.concatenate([agg_rows, counts_text_ref[...]], axis=1)
    for out_ref, side in zip((send_ref, keep_ref), stand):
        out_ref[:, :quarter] = dot_t(dot(self_rows, side).astype(BF), grad_pre).astype(BF)
        out_ref[:, quarter:] = dot_t(dot(neigh_rows, side).astype(BF), grad_pre).astype(BF)


def sage(
    place, fresh, other, sums, counts, target, hist, w_self, w_neigh, upstream, fanout, share
):
    quarter, width = w_self.shape
    count, texts = hist.shape[0], target.shape[1]
    own_texts = texts * share // width
    block = jax.ShapeDtypeStruct(((width + texts) // NC, 2 * quarter), BF)
    return pl.pallas_call(
        lambda *refs: sage_kernel(fanout, share, own_texts, *refs),
        out_shape=(jax.ShapeDtypeStruct((quarter, count), BF), block, block),
        in_specs=scalars() + whole(2) + far_off(8),
        out_specs=tuple(whole(3)),
        scratch_shapes=room(target, *counts, sums, hist, w_self, w_neigh, upstream),
        name="sage",
        **grant(52, 2000000000, 8000000),
    )(place, fresh, other, target, *counts, sums, hist, w_self, w_neigh, upstream)


def combine_kernel(keep_ref, got_ref, out_ref):
    sums = keep_ref[...].astype(F32) + got_ref[...].astype(F32)
    out_ref[...] = sums.astype(BF).reshape(out_ref.shape)


def combine(keep, got, chips):
    rows, width = keep.shape
    return pl.pallas_call(
        combine_kernel,
        out_shape=jax.ShapeDtypeStruct((chips, rows // chips, width), BF),
        in_specs=whole(2),
        out_specs=whole(1)[0],
        name="combine",
        **grant(16, 200000, 1200000),
    )(keep, got)


def final_kernel(fanout, place_ref, parts_ref, w_self_hbm, w_neigh_hbm, *refs):
    self_ref, neigh_ref, term_refs = refs[0], refs[1], refs[2 : 2 + NY]
    w_self_ref, w_neigh_ref, semaphores = refs[2 + NY :]
    copies = fetch((w_self_hbm, w_neigh_hbm), (w_self_ref, w_neigh_ref), semaphores)
    share, quarter = self_ref.shape
    total = jnp.sum(parts_ref[...].astype(F32), axis=0)
    self_ref[...] = total[:share, :quarter]
    neigh_ref[...] = total[:share, quarter:]
    rows = total[share:]
    at_rows = rows[:, :quarter].astype(BF)
    at_links = (rows[:, quarter:] / fanout).astype(BF)
    for copy in copies:
        copy.wait()
    terms = dot(at_rows, w_self_ref[...]) + dot(at_links, w_neigh_ref[...])
    for s, ref in enumerate(term_refs):
        ref[...] = sliced(terms, lax.rem(place_ref[ME] + s, NY), quarter)


def final_sums(place, parts, w_self, w_neigh, share, fanout):
    quarter = w_self.shape[0]
    grads = jax.ShapeDtypeStruct((share, quarter), F32)
    texts = jax.ShapeDtypeStruct((parts.shape[1] - share, quarter), F32)
    return pl.pallas_call(
        lambda *refs: final_kernel(fanout, *refs),
        out_shape=(grads, grads) + (texts,) * NY,
        in_specs=scalars() + whole(1) + far_off(2),
        out_specs=tuple(whole(2 + NY)),
        scratch_shapes=room(w_self, w_neigh),
        name="final_sums",
        **grant(16, 10000000, 1000000),
    )(place, parts, w_self, w_neigh)


def local(
    hidden_states,
    text_len,
    w_qkv,
    w_out,
    w_up,
    w_down,
    hist,
    nbr,
    send_rows,
    fresh_target,
    w_self,
    w_neigh,
    upstream,
):
    my_x, my_z, my_c, my_y = (lax.axis_index(axis) for axis in "xzcy")
    model_width = hist.shape[1]
    peer_count, slot_count = send_rows.shape[1:]
    fanout = nbr.shape[1]
    share = model_width // peer_count
    chips = peer_count // NC
    dom = (my_x * NZ + my_z) * NC + my_c
    place = jnp.concatenate([jnp.stack([dom, my_c, my_y]).astype(jnp.int32), text_len])

    texts = (NY, hidden_states.shape[0] // NY, model_width)
    context = attend(hidden_states, text_len, w_qkv)
    attended = dot(context, w_out).astype(BF).reshape(texts)

    def part(s):
        return lax.dynamic_index_in_dim(attended, (my_y + s) % NY, 0, keepdims=False)

    residual = lax.dynamic_index_in_dim(hidden_states.reshape(texts), my_y, 0, keepdims=False)
    parts = [part(0)] + [pull(part(NY - s), "y", s) for s in (2, 1, 3)]
    first_norm = first_layer_norm(residual, parts)

    target = fresh_target[None, :]
    attended, wanted = lax.optimization_barrier((attended, send_rows))
    wanted = wanted.reshape(peer_count * slot_count, 1)
    outgoing = outgoing_rows(place, target, wanted, hist, chips)
    received = lax.all_to_all(outgoing, ("x", "z"), split_axis=0, concat_axis=0, tiled=True)

    others = {s: pull(first_norm, "y", s) for s in (1, 3, 2)}
    own, up, down = feed_first(first_norm, w_up, w_down)
    parts = [own] + [pull(feed(others[s], up, down), "y", NY - s) for s in (1, 3, 2)]
    fresh_row = pooled_row(place, first_norm, parts)

    rows = spread_rows([fresh_row] + [pull(fresh_row, "y", s) for s in (1, 3, 2)], chips)
    _, received = lax.optimization_barrier((rows, received))
    fresh = lax.all_to_all(rows, ("x", "z"), split_axis=0, concat_axis=0, tiled=True)
    across = pull(lax.dynamic_index_in_dim(received, 1 - my_c, 1, keepdims=False), "c", 1)
    sums, *counts = halo_sums(place, received, across, target, nbr.T, hist)
    fresh, sums = lax.optimization_barrier((fresh, sums))
    fresh = fresh.reshape(-1, model_width)
    other = pull(fresh, "c", 1)

    sage_out, keep, send = sage(
        place,
        fresh,
        other,
        sums,
        counts,
        target,
        hist,
        w_self.T,
        w_neigh.T,
        upstream.T,
        fanout,
        share,
    )
    parts = combine(keep, pull(send, "c", 1), chips)
    parts = lax.all_to_all(parts, ("x", "z"), split_axis=0, concat_axis=0, tiled=True)
    grad_self_w, grad_neigh_w, grad_fresh, *terms = final_sums(
        place, parts, w_self.T, w_neigh.T, share, fanout
    )
    for s in (2, 1, 3):
        grad_fresh = grad_fresh + pull(terms[NY - s - 1], "y", s)
    return (sage_out.T, grad_fresh, grad_self_w, grad_neigh_w)


def solution(mesh):
    dom = ("x", "z", "c")
    split = Mesh(mesh.devices.reshape(NX, NZ, NC, NY), dom + ("y",))
    in_specs = (
        P(dom, None),
        P(dom),
        P(None, None, "y"),
        P("y", None),
        P(None, "y"),
        P("y", None),
        P(dom, None),
        P(dom, None),
        P(dom, None, None),
        P(),
        P(None, "y"),
        P(None, "y"),
        P(dom, "y"),
    )
    out_specs = (P(dom, "y"),) * 4
    return jax.shard_map(local, mesh=split, in_specs=in_specs, out_specs=out_specs, check_vma=False)
```

time: 595 us -> 124 us (0.21); the launches traced: 584 us -> 124 us
  waiting for transfers between devices: 291 us -> 35.2 us
  blocking collectives: 142 us -> 19.9 us
  other arithmetic: 54.9 us -> 1.48 us
  local copies, waits for them, and re-layouts: 37.2 us -> 5.8 us
  Pallas kernels: 0 us -> 20.4 us
  between operations: 16.7 us -> 1.08 us
  matrix products: 18.3 us -> 3.34 us
  starting transfers between devices: 24 us -> 36.5 us
    unnamed x6 -> x0, waiting for transfers between devices: 179 us -> none
    all_gather x2 -> x0, blocking collectives: 142 us -> none  [the longest x1 128 us: local(): fresh_all = lax.all_gather(fresh_local, ('dom', 'mp'), axis=0, tiled=True)]
    reduce_scatter x4 -> x0, waiting for transfers between devices: 68.3 us -> none  [the longest x1 27.7 us: encode_block(): lax.psum_scatter(jnp.dot(context, w_out, preferred_element_type=jnp.float...]
    all_to_all x2, waiting for transfers between devices: 43.4 us -> 9.85 us  [the longest x1 4.99 us: local(): lax.all_to_all(rows, ('x', 'z'), split_axis=0, concat_axis=0, tiled=True)]
    scatter-add x11 -> x0, other arithmetic: 31.3 us -> none  [the longest x10 24.7 us: local(): grad_extended = grad_extended.at[nbr[:, neighbour]].add(grad_total)]
    gather x13 -> x0, local copies, waits for them, and re-layouts: 25.8 us -> none  [the longest x10 20.7 us: local(): total = total + extended[nbr[:, neighbour]].astype(jnp.float32)]
    ppermute x0 -> x18, waiting for transfers between devices: none -> 25.4 us  [pull(): lax.ppermute(value, axis, [((i + shift) % count, i) for i in range(count)])]
    pallas_call x0 -> x12, Pallas kernels: none -> 20.4 us  [the longest x1 6.23 us: sage(): pl.pallas_call(lambda *refs: sage_kernel(fanout, share, own_texts, *refs)...]
  transfers between devices with their start and end apart: 7 -> 20, of which waited for: 6 -> 13; matrix products, arithmetic and copies ran while one was open for 7% -> 1% of each run, Pallas kernels for 0% -> 10%
where the time goes in v1:
time: 124 us
  starting transfers between devices  36.5 us (29%)
  waiting for transfers between devices  35.2 us (28%)
  Pallas kernels  20.4 us (16%)
  blocking collectives  19.9 us (16%)
  local copies, waits for them, and re-layouts  5.8 us (5%)
  matrix products  3.34 us (3%)
  other arithmetic  1.48 us (1%)
    ppermute x18, waiting for transfers between devices, pull(): lax.ppermute(value, axis, [((i + shift) % count, i) for i in range(count)])  25.4 us
    all_to_all x1, blocking collectives, local(): lax.all_to_all(parts, ('x', 'z'), split_axis=0, concat_axis=0, tiled=True)  19.9 us
    ppermute x18, starting transfers between devices, pull(): lax.ppermute(value, axis, [((i + shift) % count, i) for i in range(count)])  19.5 us
    all_to_all x1, starting transfers between devices, local(): lax.all_to_all(outgoing, ('x', 'z'), split_axis=0, concat_axis=0, tiled=T...  11.3 us
    pallas_call x1, Pallas kernels, sage(): pl.pallas_call(lambda *refs: sage_kernel(fanout, share, own_texts, *refs)...  6.23 us
    all_to_all x1, starting transfers between devices, local(): lax.all_to_all(rows, ('x', 'z'), split_axis=0, concat_axis=0, tiled=True)  5.72 us
    all_to_all x1, waiting for transfers between devices, local(): lax.all_to_all(rows, ('x', 'z'), split_axis=0, concat_axis=0, tiled=True)  4.99 us
    all_to_all x1, waiting for transfers between devices, local(): lax.all_to_all(outgoing, ('x', 'z'), split_axis=0, concat_axis=0, tiled=T...  4.86 us
  transfers between devices with their start and end apart: 20, of which 13 were waited for; matrix products, arithmetic and copies ran while one was open for 1% of the time, Pallas kernels for 10%

profile of v1, /device:TPU:32, one launch (start us, length us, event | category | flops | bytes accessed | tf_op | source)
XLA Modules:
  0.0 123.7 jit_solution(11892814956121349745)
XLA Ops:
  1.8 1.8 %convolution_convert_fusion.1 = bf16[512,576]{0,1:T(8,128)(2,1)S(1)} fusion(bf16[512,768]{1,0:T(8,128)(2,1)} %param.13, bf16[768,576]{0,1:T(8,128)(2,1)S(1)} %bitcast.56), kind=kOutput, calls=%fused_computation.3 | convolution fusion | flops 453279744 | bytes 2260992 | tf_op jit(solution)/shard_map/dot_general | solution.py:28
  6.4 3.3 %collective-permute-start = (bf16[128,768]{1,0:T(8,128)(2,1)S(1)}, bf16[128,768]{1,0:T(8,128)(2,1)S(1)}, u32[]{:S(2)}, u32[]{:S(2)}) collective-permute-start(bf16[128,768]{1,0:T(8,128)(2,1)S(1)} %get-tuple-element.44), channel_id=1, source_target_pairs={{2,0},{3,1},{0,2},{1,3},{6,4},{7,5},{4,6},{5,7},{10,8},{11,9},{8,1... | collective-permute-start | bytes 589832 | tf_op jit(solution)/shard_map/ppermute | solution.py:41
  12.2 2.8 %outgoing_rows.1 = bf16[32,2,16,768]{3,2,1,0:T(8,128)(2,1)} custom-call(s32[7]{0:T(128)S(1)} %pad_add_fusion.place_ref.refs_0_, s32[1,256]{1,0:T(1,128)S(1)} %bitcast.63, s32[1024,1]{1,0:T(8,128)S(1)} %reshape.55.wanted_ref, bf16[256,768]{1,0:T(8,128)(2,1)S(1)} %copy-done.5), custom_call_target="tpu_custom_call" | custom-call | flops 2000000000 | bytes 6000000 | tf_op jit(solution)/shard_map/outgoing_rows/pallas_call | solution.py:246
  15.0 11.3 %all-to-all-start.1 = ((bf16[32,2,16,768]{3,2,1,0:T(8,128)(2,1)}), bf16[32,2,16,768]{3,2,1,0:T(8,128)(2,1)}, u32[]{:S(2)}, u32[]{:S(2)}) async-start(bf16[32,2,16,768]{3,2,1,0:T(8,128)(2,1)} %outgoing_rows.1), calls=%async_computation.1 | async-start | bytes 3145728 | tf_op jit(solution)/shard_map/all_to_all | solution.py:499
  27.5 2.3 %collective-permute-start.3 = (bf16[128,768]{1,0:T(8,128)(2,1)S(1)}, bf16[128,768]{1,0:T(8,128)(2,1)S(1)}, u32[]{:S(2)}, u32[]{:S(2)}) collective-permute-start(bf16[128,768]{1,0:T(8,128)(2,1)S(1)} %first_norm.1.block_ref.first_ref), channel_id=1, source_target_pairs={{1,0},{2,1},{3,2},{0,3},{5,4},{6,5},{7,6},{4,7},{9,8},{10,9},{11,1... | collective-permute-start | bytes 589832 | tf_op jit(solution)/shard_map/ppermute | solution.py:41
  29.9 1.6 %collective-permute-start.7 = (bf16[128,768]{1,0:T(8,128)(2,1)S(1)}, bf16[128,768]{1,0:T(8,128)(2,1)S(1)}, u32[]{:S(2)}, u32[]{:S(2)}) collective-permute-start(bf16[128,768]{1,0:T(8,128)(2,1)S(1)} %first_norm.1.block_ref.first_ref), channel_id=1, source_target_pairs={{2,0},{3,1},{0,2},{1,3},{6,4},{7,5},{4,6},{5,7},{10,8},{11,9},{8,1... | collective-permute-start | bytes 589832 | tf_op jit(solution)/shard_map/ppermute | solution.py:41
  32.7 4.6 %collective-permute-done.3.block_ref = bf16[128,768]{1,0:T(8,128)(2,1)S(1)} collective-permute-done((bf16[128,768]{1,0:T(8,128)(2,1)S(1)}, bf16[128,768]{1,0:T(8,128)(2,1)S(1)}, u32[]{:S(2)}, u32[]{:S(2)}) %collective-permute-start.3) | collective-permute-done | bytes 196640 | tf_op jit(solution)/shard_map/ppermute | solution.py:41
  38.0 3.8 %collective-permute-done.5.block_ref = bf16[128,768]{1,0:T(8,128)(2,1)S(1)} collective-permute-done((bf16[128,768]{1,0:T(8,128)(2,1)S(1)}, bf16[128,768]{1,0:T(8,128)(2,1)S(1)}, u32[]{:S(2)}, u32[]{:S(2)}) %collective-permute-start.5) | collective-permute-done | bytes 196640 | tf_op jit(solution)/shard_map/ppermute | solution.py:41
  43.2 1.6 %collective-permute-start.8 = (bf16[128,768]{1,0:T(8,128)(2,1)S(1)}, bf16[128,768]{1,0:T(8,128)(2,1)S(1)}, u32[]{:S(2)}, u32[]{:S(2)}) collective-permute-start(bf16[128,768]{1,0:T(8,128)(2,1)S(1)} %feed.5), channel_id=1, source_target_pairs={{2,0},{3,1},{0,2},{1,3},{6,4},{7,5},{4,6},{5,7},{10,8},{11,9},{8,1... | collective-permute-start | bytes 589832 | tf_op jit(solution)/shard_map/ppermute | solution.py:41
  44.8 2.0 %collective-permute-done.4.near_ref = bf16[128,768]{1,0:T(8,128)(2,1)S(1)} collective-permute-done((bf16[128,768]{1,0:T(8,128)(2,1)S(1)}, bf16[128,768]{1,0:T(8,128)(2,1)S(1)}, u32[]{:S(2)}, u32[]{:S(2)}) %collective-permute-start.4) | collective-permute-done | bytes 196640 | tf_op jit(solution)/shard_map/ppermute | solution.py:41
  46.8 1.5 %collective-permute-done.6.far_ref = bf16[128,768]{1,0:T(8,128)(2,1)S(1)} collective-permute-done((bf16[128,768]{1,0:T(8,128)(2,1)S(1)}, bf16[128,768]{1,0:T(8,128)(2,1)S(1)}, u32[]{:S(2)}, u32[]{:S(2)}) %collective-permute-start.6) | collective-permute-done | bytes 196640 | tf_op jit(solution)/shard_map/ppermute | solution.py:41
  48.2 2.4 %collective-permute-done.8.across_ref = bf16[128,768]{1,0:T(8,128)(2,1)S(1)} collective-permute-done((bf16[128,768]{1,0:T(8,128)(2,1)S(1)}, bf16[128,768]{1,0:T(8,128)(2,1)S(1)}, u32[]{:S(2)}, u32[]{:S(2)}) %collective-permute-start.8) | collective-permute-done | bytes 196640 | tf_op jit(solution)/shard_map/ppermute | solution.py:41
  51.5 2.5 %collective-permute-start.9 = (bf16[1,768]{1,0:T(2,128)(2,1)S(1)}, bf16[1,768]{1,0:T(2,128)(2,1)S(1)}, u32[]{:S(2)}, u32[]{:S(2)}) collective-permute-start(bf16[1,768]{1,0:T(2,128)(2,1)S(1)} %pooled_row.1.own_ref), channel_id=1, source_target_pairs={{1,0},{2,1},{3,2},{0,3},{5,4},{6,5},{7,6},{4,7},{9,8},{10,9},{11,1... | collective-permute-start | bytes 4616 | tf_op jit(solution)/shard_map/ppermute | solution.py:41
  54.0 1.7 %collective-permute-start.11 = (bf16[1,768]{1,0:T(2,128)(2,1)S(1)}, bf16[1,768]{1,0:T(2,128)(2,1)S(1)}, u32[]{:S(2)}, u32[]{:S(2)}) collective-permute-start(bf16[1,768]{1,0:T(2,128)(2,1)S(1)} %pooled_row.1.own_ref), channel_id=1, source_target_pairs={{2,0},{3,1},{0,2},{1,3},{6,4},{7,5},{4,6},{5,7},{10,8},{11,9},{8,1... | collective-permute-start | bytes 4616 | tf_op jit(solution)/shard_map/ppermute | solution.py:41
  55.7 3.1 %collective-permute-done.10.far_ref = bf16[1,768]{1,0:T(2,128)(2,1)S(1)} collective-permute-done((bf16[1,768]{1,0:T(2,128)(2,1)S(1)}, bf16[1,768]{1,0:T(2,128)(2,1)S(1)}, u32[]{:S(2)}, u32[]{:S(2)}) %collective-permute-start.10) | collective-permute-done | bytes 1568 | tf_op jit(solution)/shard_map/ppermute | solution.py:41
  59.8 4.9 %all-to-all-done.1.received_hbm = bf16[32,2,16,768]{3,2,1,0:T(8,128)(2,1)} async-done(((bf16[32,2,16,768]{3,2,1,0:T(8,128)(2,1)}), bf16[32,2,16,768]{3,2,1,0:T(8,128)(2,1)}, u32[]{:S(2)}, u32[]{:S(2)}) %all-to-all-start.1) | async-done | bytes 1572896 | tf_op jit(solution)/shard_map/all_to_all | solution.py:499
  66.0 5.7 %all-to-all-start = ((bf16[32,4,768]{2,1,0:T(4,128)(2,1)}), bf16[32,4,768]{2,1,0:T(4,128)(2,1)S(1)}, u32[]{:S(2)}, u32[]{:S(2)}) async-start(bf16[32,4,768]{2,1,0:T(4,128)(2,1)} %spread_rows.1), calls=%async_computation | async-start | bytes 393216 | tf_op jit(solution)/shard_map/all_to_all | solution.py:508
  72.6 4.8 %halo_sums.1 = (f32[256,768]{1,0:T(8,128)S(1)}, bf16[256,256]{1,0:T(8,128)(2,1)S(1)}, bf16[256,256]{1,0:T(8,128)(2,1)S(1)}) custom-call(s32[7]{0:T(128)S(1)} %pad_add_fusion.place_ref.refs_0_, s32[1,256]{1,0:T(1,128)S(1)} %bitcast.64, s32[10,256]{1,0:T(8,128)S(1)} %bitcast.62, bf16[256,768]{1,0:T(8,128)(2,1)S(1)} %copy-done.5, ...), custom_call_target="tpu_custom_call" | custom-call | flops 1000000000 | bytes 5000000 | tf_op jit(solution)/shard_map/halo_sums/pallas_call | solution.py:325
  78.4 5.0 %all-to-all-done = bf16[32,4,768]{2,1,0:T(4,128)(2,1)S(1)} async-done(((bf16[32,4,768]{2,1,0:T(4,128)(2,1)}), bf16[32,4,768]{2,1,0:T(4,128)(2,1)S(1)}, u32[]{:S(2)}, u32[]{:S(2)}) %all-to-all-start) | async-done | bytes 196640 | tf_op jit(solution)/shard_map/all_to_all | solution.py:508
  84.9 6.2 %sage.1 = (bf16[192,256]{1,0:T(8,128)(2,1)}, bf16[512,384]{1,0:T(8,128)(2,1)S(1)}, bf16[512,384]{1,0:T(8,128)(2,1)}) custom-call(s32[7]{0:T(128)S(1)} %pad_add_fusion.place_ref.refs_0_, bf16[128,768]{1,0:T(8,128)(2,1)S(1)} %reshape.54.refs_1_, bf16[128,768]{1,0:T(8,128)(2,1)S(1)} %collective-permute-done.13.refs_2_, s32[1,256]{1,0:T(1,128)S(1)} %bitcast.65, ...), custom_call_target="tpu_custom_call" | custom-call | flops 2000000000 | bytes 8000000 | tf_op jit(solution)/shard_map/sage/pallas_call | solution.py:399
  91.4 1.8 %collective-permute-done.14.got_ref = bf16[512,384]{1,0:T(8,128)(2,1)S(1)} collective-permute-done((bf16[512,384]{1,0:T(8,128)(2,1)}, bf16[512,384]{1,0:T(8,128)(2,1)S(1)}, u32[]{:S(2)}, u32[]{:S(2)}) %collective-permute-start.14) | collective-permute-done | bytes 393248 | tf_op jit(solution)/shard_map/ppermute | solution.py:41
  93.3 19.9 %all_to_all.15.refs_1_ = bf16[32,16,384]{2,1,0:T(8,128)(2,1)S(1)} all-to-all(bf16[32,16,384]{2,1,0:T(8,128)(2,1)S(1)} %combine.1), channel_id=1, replica_groups=mesh['x'=4,'z'=8,'c'=2,'y'=4] {'x','z'}, dimensions={0} | all-to-all | bytes 786432 | tf_op jit(solution)/shard_map/all_to_all | solution.py:530
  115.6 2.4 %collective-permute-start.16 = (f32[4,192]{1,0:T(4,128)S(1)}, f32[4,192]{1,0:T(4,128)S(1)}, u32[]{:S(2)}, u32[]{:S(2)}) collective-permute-start(f32[4,192]{1,0:T(4,128)S(1)} %get-tuple-element.38), channel_id=1, source_target_pairs={{1,0},{2,1},{3,2},{0,3},{5,4},{6,5},{7,6},{4,7},{9,8},{10,9},{11,1... | collective-permute-start | bytes 9224 | tf_op jit(solution)/shard_map/ppermute | solution.py:41
  119.6 3.5 %collective-permute-done.15 = f32[4,192]{1,0:T(4,128)S(1)} collective-permute-done((f32[4,192]{1,0:T(4,128)S(1)}, f32[4,192]{1,0:T(4,128)S(1)}, u32[]{:S(2)}, u32[]{:S(2)}) %collective-permute-start.15) | collective-permute-done | bytes 3104 | tf_op jit(solution)/shard_map/ppermute | solution.py:41
  (74 shorter events, 22.2 us)
Async XLA Ops:
  6.4 20.8 %collective-permute-start = (bf16[128,768]{1,0:T(8,128)(2,1)S(1)}, bf16[128,768]{1,0:T(8,128)(2,1)S(1)}, u32[]{:S(2)}, u32[]{:S(2)}) collective-permute-start(bf16[128,768]{1,0:T(8,128)(2,1)S(1)} %get-tuple-element.44), channel_id=1, source_target_pairs={{2,0},{3,1},{0,2},{1,3},{6,4},{7,5},{4,6},{5,7},{10,8},{11,9},{8,1... | collective-permute-start | bytes 589832 | tf_op jit(solution)/shard_map/ppermute | solution.py:41
  9.6 17.6 %collective-permute-start.1 = (bf16[128,768]{1,0:T(8,128)(2,1)S(1)}, bf16[128,768]{1,0:T(8,128)(2,1)S(1)}, u32[]{:S(2)}, u32[]{:S(2)}) collective-permute-start(bf16[128,768]{1,0:T(8,128)(2,1)S(1)} %get-tuple-element.43), channel_id=1, source_target_pairs={{1,0},{2,1},{3,2},{0,3},{5,4},{6,5},{7,6},{4,7},{9,8},{10,9},{11,1... | collective-permute-start | bytes 589832 | tf_op jit(solution)/shard_map/ppermute | solution.py:41
  10.7 16.5 %collective-permute-start.2 = (bf16[128,768]{1,0:T(8,128)(2,1)S(1)}, bf16[128,768]{1,0:T(8,128)(2,1)S(1)}, u32[]{:S(2)}, u32[]{:S(2)}) collective-permute-start(bf16[128,768]{1,0:T(8,128)(2,1)S(1)} %get-tuple-element.42), channel_id=1, source_target_pairs={{3,0},{0,1},{1,2},{2,3},{7,4},{4,5},{5,6},{6,7},{11,8},{8,9},{9,10... | collective-permute-start | bytes 589832 | tf_op jit(solution)/shard_map/ppermute | solution.py:41
  15.0 49.7 %all-to-all-start.1 = ((bf16[32,2,16,768]{3,2,1,0:T(8,128)(2,1)}), bf16[32,2,16,768]{3,2,1,0:T(8,128)(2,1)}, u32[]{:S(2)}, u32[]{:S(2)}) async-start(bf16[32,2,16,768]{3,2,1,0:T(8,128)(2,1)} %outgoing_rows.1), calls=%async_computation.1 | async-start | bytes 3145728 | tf_op jit(solution)/shard_map/all_to_all | solution.py:499
  27.5 9.8 %collective-permute-start.3 = (bf16[128,768]{1,0:T(8,128)(2,1)S(1)}, bf16[128,768]{1,0:T(8,128)(2,1)S(1)}, u32[]{:S(2)}, u32[]{:S(2)}) collective-permute-start(bf16[128,768]{1,0:T(8,128)(2,1)S(1)} %first_norm.1.block_ref.first_ref), channel_id=1, source_target_pairs={{1,0},{2,1},{3,2},{0,3},{5,4},{6,5},{7,6},{4,7},{9,8},{10,9},{11,1... | collective-permute-start | bytes 589832 | tf_op jit(solution)/shard_map/ppermute | solution.py:41
  29.9 12.0 %collective-permute-start.5 = (bf16[128,768]{1,0:T(8,128)(2,1)S(1)}, bf16[128,768]{1,0:T(8,128)(2,1)S(1)}, u32[]{:S(2)}, u32[]{:S(2)}) collective-permute-start(bf16[128,768]{1,0:T(8,128)(2,1)S(1)} %first_norm.1.block_ref.first_ref), channel_id=1, source_target_pairs={{3,0},{0,1},{1,2},{2,3},{7,4},{4,5},{5,6},{6,7},{11,8},{8,9},{9,10... | collective-permute-start | bytes 589832 | tf_op jit(solution)/shard_map/ppermute | solution.py:41
  29.9 12.7 %collective-permute-start.7 = (bf16[128,768]{1,0:T(8,128)(2,1)S(1)}, bf16[128,768]{1,0:T(8,128)(2,1)S(1)}, u32[]{:S(2)}, u32[]{:S(2)}) collective-permute-start(bf16[128,768]{1,0:T(8,128)(2,1)S(1)} %first_norm.1.block_ref.first_ref), channel_id=1, source_target_pairs={{2,0},{3,1},{0,2},{1,3},{6,4},{7,5},{4,6},{5,7},{10,8},{11,9},{8,1... | collective-permute-start | bytes 589832 | tf_op jit(solution)/shard_map/ppermute | solution.py:41
  38.0 8.8 %collective-permute-start.4 = (bf16[128,768]{1,0:T(8,128)(2,1)S(1)}, bf16[128,768]{1,0:T(8,128)(2,1)S(1)}, u32[]{:S(2)}, u32[]{:S(2)}) collective-permute-start(bf16[128,768]{1,0:T(8,128)(2,1)S(1)} %feed.3), channel_id=1, source_target_pairs={{3,0},{0,1},{1,2},{2,3},{7,4},{4,5},{5,6},{6,7},{11,8},{8,9},{9,10... | collective-permute-start | bytes 589832 | tf_op jit(solution)/shard_map/ppermute | solution.py:41
  42.5 5.7 %collective-permute-start.6 = (bf16[128,768]{1,0:T(8,128)(2,1)S(1)}, bf16[128,768]{1,0:T(8,128)(2,1)S(1)}, u32[]{:S(2)}, u32[]{:S(2)}) collective-permute-start(bf16[128,768]{1,0:T(8,128)(2,1)S(1)} %feed.4), channel_id=1, source_target_pairs={{1,0},{2,1},{3,2},{0,3},{5,4},{6,5},{7,6},{4,7},{9,8},{10,9},{11,1... | collective-permute-start | bytes 589832 | tf_op jit(solution)/shard_map/ppermute | solution.py:41
  43.2 7.4 %collective-permute-start.8 = (bf16[128,768]{1,0:T(8,128)(2,1)S(1)}, bf16[128,768]{1,0:T(8,128)(2,1)S(1)}, u32[]{:S(2)}, u32[]{:S(2)}) collective-permute-start(bf16[128,768]{1,0:T(8,128)(2,1)S(1)} %feed.5), channel_id=1, source_target_pairs={{2,0},{3,1},{0,2},{1,3},{6,4},{7,5},{4,6},{5,7},{10,8},{11,9},{8,1... | collective-permute-start | bytes 589832 | tf_op jit(solution)/shard_map/ppermute | solution.py:41
  51.5 21.1 %copy-start.7 = (s32[256,10]{0,1:T(8,128)S(1)}, s32[256,10]{0,1:T(8,128)}, u32[]{:S(2)}) copy-start(s32[256,10]{0,1:T(8,128)} %param.20) | copy-start | bytes 30724
  51.5 4.2 %collective-permute-start.9 = (bf16[1,768]{1,0:T(2,128)(2,1)S(1)}, bf16[1,768]{1,0:T(2,128)(2,1)S(1)}, u32[]{:S(2)}, u32[]{:S(2)}) collective-permute-start(bf16[1,768]{1,0:T(2,128)(2,1)S(1)} %pooled_row.1.own_ref), channel_id=1, source_target_pairs={{1,0},{2,1},{3,2},{0,3},{5,4},{6,5},{7,6},{4,7},{9,8},{10,9},{11,1... | collective-permute-start | bytes 4616 | tf_op jit(solution)/shard_map/ppermute | solution.py:41
  54.0 4.8 %collective-permute-start.10 = (bf16[1,768]{1,0:T(2,128)(2,1)S(1)}, bf16[1,768]{1,0:T(2,128)(2,1)S(1)}, u32[]{:S(2)}, u32[]{:S(2)}) collective-permute-start(bf16[1,768]{1,0:T(2,128)(2,1)S(1)} %pooled_row.1.own_ref), channel_id=1, source_target_pairs={{3,0},{0,1},{1,2},{2,3},{7,4},{4,5},{5,6},{6,7},{11,8},{8,9},{9,10... | collective-permute-start | bytes 4616 | tf_op jit(solution)/shard_map/ppermute | solution.py:41
  54.0 5.1 %collective-permute-start.11 = (bf16[1,768]{1,0:T(2,128)(2,1)S(1)}, bf16[1,768]{1,0:T(2,128)(2,1)S(1)}, u32[]{:S(2)}, u32[]{:S(2)}) collective-permute-start(bf16[1,768]{1,0:T(2,128)(2,1)S(1)} %pooled_row.1.own_ref), channel_id=1, source_target_pairs={{2,0},{3,1},{0,2},{1,3},{6,4},{7,5},{4,6},{5,7},{10,8},{11,9},{8,1... | collective-permute-start | bytes 4616 | tf_op jit(solution)/shard_map/ppermute | solution.py:41
  65.9 5.8 %collective-permute-start.12 = (bf16[32,16,768]{2,1,0:T(8,128)(2,1)S(1)}, bf16[32,16,768]{2,1,0:T(8,128)(2,1)S(1)}, u32[]{:S(2)}, u32[]{:S(2)}) collective-permute-start(bf16[32,16,768]{2,1,0:T(8,128)(2,1)S(1)} %dynamic-slice_bitcast_fusion), channel_id=1, source_target_pairs={{4,0},{0,4},{5,1},{1,5},{6,2},{2,6},{7,3},{3,7},{12,8},{8,12},{13,... | collective-permute-start | bytes 2359304 | tf_op jit(solution)/shard_map/ppermute | solution.py:41
  66.0 17.4 %all-to-all-start = ((bf16[32,4,768]{2,1,0:T(4,128)(2,1)}), bf16[32,4,768]{2,1,0:T(4,128)(2,1)S(1)}, u32[]{:S(2)}, u32[]{:S(2)}) async-start(bf16[32,4,768]{2,1,0:T(4,128)(2,1)} %spread_rows.1), calls=%async_computation | async-start | bytes 393216 | tf_op jit(solution)/shard_map/all_to_all | solution.py:508
  72.6 12.3 %copy-start.1 = (bf16[768,192]{0,1:T(8,128)(2,1)S(1)}, bf16[768,192]{0,1:T(8,128)(2,1)}, u32[]{:S(2)}) copy-start(bf16[768,192]{0,1:T(8,128)(2,1)} %param.23) | copy-start | bytes 884740
  72.6 12.3 %copy-start.2 = (bf16[768,192]{0,1:T(8,128)(2,1)S(1)}, bf16[768,192]{0,1:T(8,128)(2,1)}, u32[]{:S(2)}) copy-start(bf16[768,192]{0,1:T(8,128)(2,1)} %param.24) | copy-start | bytes 884740
  72.6 12.3 %copy-start.6 = (bf16[256,192]{0,1:T(8,128)(2,1)S(1)}, bf16[256,192]{0,1:T(8,128)(2,1)}, u32[]{:S(2)}) copy-start(bf16[256,192]{0,1:T(8,128)(2,1)} %param.25) | copy-start | bytes 294916
  83.4 1.5 %collective-permute-start.13 = (bf16[128,768]{1,0:T(8,128)(2,1)S(1)}, bf16[128,768]{1,0:T(8,128)(2,1)S(1)}, u32[]{:S(2)}, u32[]{:S(2)}) collective-permute-start(bf16[128,768]{1,0:T(8,128)(2,1)S(1)} %reshape.54.refs_1_), channel_id=1, source_target_pairs={{4,0},{0,4},{5,1},{1,5},{6,2},{2,6},{7,3},{3,7},{12,8},{8,12},{13,... | collective-permute-start | bytes 589832 | tf_op jit(solution)/shard_map/ppermute | solution.py:41
  91.2 2.0 %collective-permute-start.14 = (bf16[512,384]{1,0:T(8,128)(2,1)}, bf16[512,384]{1,0:T(8,128)(2,1)S(1)}, u32[]{:S(2)}, u32[]{:S(2)}) collective-permute-start(bf16[512,384]{1,0:T(8,128)(2,1)} %get-tuple-element.35), channel_id=1, source_target_pairs={{4,0},{0,4},{5,1},{1,5},{6,2},{2,6},{7,3},{3,7},{12,8},{8,12},{13,... | collective-permute-start | bytes 1179656 | tf_op jit(solution)/shard_map/ppermute | solution.py:41
  114.7 4.9 %collective-permute-start.17 = (f32[4,192]{1,0:T(4,128)S(1)}, f32[4,192]{1,0:T(4,128)S(1)}, u32[]{:S(2)}, u32[]{:S(2)}) collective-permute-start(f32[4,192]{1,0:T(4,128)S(1)} %get-tuple-element.39), channel_id=1, source_target_pairs={{3,0},{0,1},{1,2},{2,3},{7,4},{4,5},{5,6},{6,7},{11,8},{8,9},{9,10... | collective-permute-start | bytes 9224 | tf_op jit(solution)/shard_map/ppermute | solution.py:41
  115.6 4.0 %collective-permute-start.16 = (f32[4,192]{1,0:T(4,128)S(1)}, f32[4,192]{1,0:T(4,128)S(1)}, u32[]{:S(2)}, u32[]{:S(2)}) collective-permute-start(f32[4,192]{1,0:T(4,128)S(1)} %get-tuple-element.38), channel_id=1, source_target_pairs={{1,0},{2,1},{3,2},{0,3},{5,4},{6,5},{7,6},{4,7},{9,8},{10,9},{11,1... | collective-permute-start | bytes 9224 | tf_op jit(solution)/shard_map/ppermute | solution.py:41
  118.0 5.1 %collective-permute-start.15 = (f32[4,192]{1,0:T(4,128)S(1)}, f32[4,192]{1,0:T(4,128)S(1)}, u32[]{:S(2)}, u32[]{:S(2)}) collective-permute-start(f32[4,192]{1,0:T(4,128)S(1)} %get-tuple-element.37), channel_id=1, source_target_pairs={{2,0},{3,1},{0,2},{1,3},{6,4},{7,5},{4,6},{5,7},{10,8},{11,9},{8,1... | collective-permute-start | bytes 9224 | tf_op jit(solution)/shard_map/ppermute | solution.py:41
  (10 other events, 35.9 us)

commit v2 on v1

--- a/solution.py
+++ b/solution.py
@@ -333,90 +333,175 @@
     )(place, target, links, hist, received, across)
 
 
+def head_kernel(fanout, place_ref, fresh_ref, *refs):
+    sources, semaphores, (counts_ref, sums_ref, hist_ref, target_ref, up_ref) = (
+        refs[:8],
+        refs[-6],
+        refs[-5:],
+    )
+    table_ref, agg_ref, other_ref, texts_ref, w_self_ref, w_neigh_ref, upstream_ref = refs[8:-6]
+    target_hbm, counts_hbm, texts_hbm, sums_hbm, hist_hbm, w_self_hbm, w_neigh_hbm, up_hbm = sources
+    copies = fetch(
+        (counts_hbm, sums_hbm, target_hbm, hist_hbm, up_hbm, texts_hbm, w_self_hbm, w_neigh_hbm),
+        (
+            counts_ref,
+            sums_ref,
+            target_ref,
+            hist_ref,
+            up_ref,
+            texts_ref.at[1],
+            w_self_ref,
+            w_neigh_ref,
+        ),
+        semaphores,
+    )
+    half = fresh_ref.shape[0]
+    count = hist_ref.shape[0]
+    fresh = fresh_ref[...]
+    copies[0].wait()
+    copies[1].wait()
+    agg_ref[...] = sums_ref[...] + dot(counts_ref[:, :half], fresh)
+    other_ref[1] = counts_ref[:, half:]
+    copies[2].wait()
+    place, row_text = text_rows(target_ref[...], count, place_ref[DOM])
+    texts_ref[0] = place
+    slots = slot_texts(place.shape[1], half // NY, place_ref[CORE], place_ref[ME])
+    place_slot = (row_text == slots).astype(F32).astype(BF)
+    other_ref[0] = place_slot[:, half:]
+    placed = dot(place_slot[:, :half], fresh)
+    copies[3].wait()
+    table_ref[...] = jnp.where(row_text >= 0, placed, hist_ref[...].astype(F32)).astype(BF)
+    copies[4].wait()
+    upstream_ref[...] = up_ref[...].astype(F32).T
+    for copy in copies[5:]:
+        copy.wait()
+
+
+def sage_head(place, fresh, counts, sums, target, hist, w_self, w_neigh, upstream, fanout):
+    counts_slot, counts_text = counts
+    count, texts = counts_text.shape
+    return pl.pallas_call(
+        lambda *refs: head_kernel(fanout, *refs),
+        out_shape=(
+            jax.ShapeDtypeStruct(hist.shape, BF),
+            jax.ShapeDtypeStruct(hist.shape, F32),
+            jax.ShapeDtypeStruct((2, count, texts - fresh.shape[0]), BF),
+            jax.ShapeDtypeStruct((2, count, texts), BF),
+            jax.ShapeDtypeStruct(w_self.shape, BF),
+            jax.ShapeDtypeStruct(w_neigh.shape, BF),
+            jax.ShapeDtypeStruct(upstream.shape[::-1], F32),
+        ),
+        in_specs=scalars() + whole(1) + far_off(8),
+        out_specs=tuple(whole(7)),
+        scratch_shapes=[
+            pltpu.SemaphoreType.DMA((8,)),
+            pltpu.VMEM(counts_slot.shape, BF),
+            pltpu.VMEM(sums.shape, F32),
+            pltpu.VMEM(hist.shape, BF),
+            pltpu.VMEM(target.shape, jnp.int32),
+            pltpu.VMEM(upstream.shape, BF),
+        ],
+        name="sage_head",
+        **grant(48, 3000000000, 4000000),
+    )(place, fresh, target, counts_slot, counts_text, sums, hist, w_self, w_neigh, upstream)
+
+
 def sage_kernel(
     fanout,
-    share,
-    own_texts,
     place_ref,
     fresh_ref,
+    table_ref,
+    agg_ref,
     other_ref,
-    *refs,
+    texts_ref,
+    w_self_ref,
+    w_neigh_ref,
+    upstream_ref,
+    act_ref,
+    weights_ref,
+    terms_ref,
+    send_ref,
+    blocks_ref,
 ):
-    sources, (sage_ref, keep_ref, send_ref), targets = refs[:8], refs[8:11], refs[11:-1]
-    copies = fetch(sources, targets, refs[-1])
-    target_ref, counts_slot_ref, counts_text_ref, sums_ref, hist_ref = targets[:5]
-    w_self_ref, w_neigh_ref, upstream_ref = targets[5:]
-    half = fresh_ref.shape[0]
-    quarter, width = w_self_ref.shape
-    count = hist_ref.shape[0]
-    texts = target_ref.shape[1]
-    core, me = place_ref[CORE], place_ref[ME]
-    fresh, other = fresh_ref[...], other_ref[...]
-
-    block = share + own_texts
-    wide = keep_ref.shape[0]
-    ids = lax.broadcasted_iota(jnp.int32, (width + texts, wide), 0)
-    column = lax.broadcasted_iota(jnp.int32, (1, wide), 1)
-    stand = []
-    for side in (1 - core, core):
-        owner, inside = column // block * NC + side, column % block
-        row = jnp.where(
-            inside < share, owner * share + inside, width + owner * own_texts + inside - share
-        )
-        stand.append((ids == row).astype(F32).astype(BF))
-
-    for copy in copies[:4]:
-        copy.wait()
-    added = dot(counts_slot_ref[:, :half], fresh) + dot(counts_slot_ref[:, half:], other)
-    agg_rows = ((sums_ref[...] + added) / fanout).astype(BF)
-    copies[4].wait()
-    place, row_text = text_rows(target_ref[...], count, place_ref[DOM])
-    place_slot = (row_text == slot_texts(texts, half // NY, core, me)).astype(F32).astype(BF)
-    placed = dot(place_slot[:, :half], fresh) + dot(place_slot[:, half:], other)
-    table = jnp.where(row_text >= 0, placed, hist_ref[...].astype(F32)).astype(BF)
-    for copy in copies[5:]:
-        copy.wait()
+    fresh = fresh_ref[...]
+    quarter = w_self_ref.shape[0]
+    table = table_ref[...] + dot(other_ref[0], fresh).astype(BF)
+    agg_rows = ((agg_ref[...] + dot(other_ref[1], fresh)) / fanout).astype(BF)
     pre_act = dot_nt(table, w_self_ref[...]) + dot_nt(agg_rows, w_neigh_ref[...])
     cdf = 0.5 * (1.0 + lax.erf(pre_act * math.sqrt(0.5)))
     density = jnp.exp(-0.5 * pre_act * pre_act) * (1.0 / math.sqrt(2.0 * math.pi))
-    sage_ref[...] = (pre_act * cdf).T.astype(BF)
-    upstream = upstream_ref[...].astype(F32).T
-    grad_pre = (upstream * (cdf + pre_act * density)).astype(BF)
-    self_rows = jnp.concatenate([table, place], axis=1)
-    neigh_rows = jnp.concatenate([agg_rows, counts_text_ref[...]], axis=1)
-    for out_ref, side in zip((send_ref, keep_ref), stand):
-        out_ref[:, :quarter] = dot_t(dot(self_rows, side).astype(BF), grad_pre).astype(BF)
-        out_ref[:, quarter:] = dot_t(dot(neigh_rows, side).astype(BF), grad_pre).astype(BF)
-
-
-def sage(
-    place, fresh, other, sums, counts, target, hist, w_self, w_neigh, upstream, fanout, share
-):
+    act_ref[...] = pre_act * cdf
+    grad_pre = (upstream_ref[...] * (cdf + pre_act * density)).astype(BF)
+    chips = weights_ref.shape[0]
+    for k, rows in enumerate((table, agg_rows)):
+        part = slice(k * quarter, (k + 1) * quarter)
+        weights_ref[:, :, part] = dot_t(rows, grad_pre).reshape(chips, -1, quarter)
+        terms_ref[:, :, part] = dot_t(texts_ref[k], grad_pre).reshape(chips, -1, quarter)
+    put_blocks(1 - place_ref[CORE], weights_ref, terms_ref, blocks_ref)
+    send_ref[...] = blocks_ref[...].astype(BF)
+
+
+def put_blocks(side, weights_ref, terms_ref, blocks_ref):
+    share, own_texts = weights_ref.shape[1] // NC, terms_ref.shape[1] // NC
+    for core in range(NC):
+
+        @pl.when(side == core)
+        def _():
+            rows = slice(core * share, (core + 1) * share)
+            blocks_ref[:, :share, :] = weights_ref[:, rows, :]
+            rows = slice(core * own_texts, (core + 1) * own_texts)
+            blocks_ref[:, share:, :] = terms_ref[:, rows, :]
+
+
+def sage(place, fresh, table, agg, other, texts, w_self, w_neigh, upstream, fanout, chips):
     quarter, width = w_self.shape
-    count, texts = hist.shape[0], target.shape[1]
-    own_texts = texts * share // width
-    block = jax.ShapeDtypeStruct(((width + texts) // NC, 2 * quarter), BF)
-    return pl.pallas_call(
-        lambda *refs: sage_kernel(fanout, share, own_texts, *refs),
-        out_shape=(jax.ShapeDtypeStruct((quarter, count), BF), block, block),
-        in_specs=scalars() + whole(2) + far_off(8),
-        out_specs=tuple(whole(3)),
-        scratch_shapes=room(target, *counts, sums, hist, w_self, w_neigh, upstream),
+    count = table.shape[0]
+    share, own_texts = width // chips, texts.shape[2] // chips
+    block = (chips, (share + own_texts) // NC, 2 * quarter)
+    return pl.pallas_call(
+        lambda *refs: sage_kernel(fanout, *refs),
+        out_shape=(
+            jax.ShapeDtypeStruct((count, quarter), F32),
+            jax.ShapeDtypeStruct((chips, share, 2 * quarter), F32),
+            jax.ShapeDtypeStruct((chips, own_texts, 2 * quarter), F32),
+            jax.ShapeDtypeStruct(block, BF),
+        ),
+        in_specs=scalars() + whole(8),
+        out_specs=tuple(whole(4)),
+        scratch_shapes=[pltpu.VMEM(block, F32)],
         name="sage",
-        **grant(52, 2000000000, 8000000),
-    )(place, fresh, other, target, *counts, sums, hist, w_self, w_neigh, upstream)
+        **grant(16, 2000000000, 8000000),
+    )(place, fresh, table, agg, other, texts, w_self, w_neigh, upstream)
+
+
+def tail_kernel(place_ref, act_ref, weights_ref, terms_ref, sage_ref, keep_ref):
+    sage_ref[...] = act_ref[...].T.astype(BF)
+    put_blocks(place_ref[CORE], weights_ref, terms_ref, keep_ref)
+
+
+def sage_tail(place, act, weights, terms, send):
+    return pl.pallas_call(
+        tail_kernel,
+        out_shape=(
+            jax.ShapeDtypeStruct(act.shape[::-1], BF),
+            jax.ShapeDtypeStruct(send.shape, F32),
+        ),
+        in_specs=scalars() + whole(3),
+        out_specs=tuple(whole(2)),
+        name="sage_tail",
+        **grant(16, 3000000000, 4000000),
+    )(place, act, weights, terms)
 
 
 def combine_kernel(keep_ref, got_ref, out_ref):
-    sums = keep_ref[...].astype(F32) + got_ref[...].astype(F32)
-    out_ref[...] = sums.astype(BF).reshape(out_ref.shape)
-
-
-def combine(keep, got, chips):
-    rows, width = keep.shape
+    sums = keep_ref[...] + got_ref[...].astype(F32)
+    out_ref[...] = sums.astype(BF)
+
+
+def combine(keep, got):
     return pl.pallas_call(
         combine_kernel,
-        out_shape=jax.ShapeDtypeStruct((chips, rows // chips, width), BF),
+        out_shape=jax.ShapeDtypeStruct(got.shape, BF),
         in_specs=whole(2),
         out_specs=whole(1)[0],
         name="combine",
@@ -424,10 +509,9 @@
     )(keep, got)
 
 
-def final_kernel(fanout, place_ref, parts_ref, w_self_hbm, w_neigh_hbm, *refs):
-    self_ref, neigh_ref, term_refs = refs[0], refs[1], refs[2 : 2 + NY]
-    w_self_ref, w_neigh_ref, semaphores = refs[2 + NY :]
-    copies = fetch((w_self_hbm, w_neigh_hbm), (w_self_ref, w_neigh_ref), semaphores)
+def final_kernel(
+    fanout, place_ref, parts_ref, w_self_ref, w_neigh_ref, self_ref, neigh_ref, *term_refs
+):
     share, quarter = self_ref.shape
     total = jnp.sum(parts_ref[...].astype(F32), axis=0)
     self_ref[...] = total[:share, :quarter]
@@ -435,8 +519,6 @@
     rows = total[share:]
     at_rows = rows[:, :quarter].astype(BF)
     at_links = (rows[:, quarter:] / fanout).astype(BF)
-    for copy in copies:
-        copy.wait()
     terms = dot(at_rows, w_self_ref[...]) + dot(at_links, w_neigh_ref[...])
     for s, ref in enumerate(term_refs):
         ref[...] = sliced(terms, lax.rem(place_ref[ME] + s, NY), quarter)
@@ -449,9 +531,8 @@
     return pl.pallas_call(
         lambda *refs: final_kernel(fanout, *refs),
         out_shape=(grads, grads) + (texts,) * NY,
-        in_specs=scalars() + whole(1) + far_off(2),
+        in_specs=scalars() + whole(3),
         out_specs=tuple(whole(2 + NY)),
-        scratch_shapes=room(w_self, w_neigh),
         name="final_sums",
         **grant(16, 10000000, 1000000),
     )(place, parts, w_self, w_neigh)
@@ -479,7 +560,6 @@
     share = model_width // peer_count
     chips = peer_count // NC
     dom = (my_x * NZ + my_z) * NC + my_c
-    place = jnp.concatenate([jnp.stack([dom, my_c, my_y]).astype(jnp.int32), text_len])
 
     texts = (NY, hidden_states.shape[0] // NY, model_width)
     context = attend(hidden_states, text_len, w_qkv)
@@ -493,7 +573,8 @@
     first_norm = first_layer_norm(residual, parts)
 
     target = fresh_target[None, :]
-    attended, wanted = lax.optimization_barrier((attended, send_rows))
+    attended, wanted, lengths = lax.optimization_barrier((attended, send_rows, text_len))
+    place = jnp.concatenate([jnp.stack([dom, my_c, my_y]).astype(jnp.int32), lengths])
     wanted = wanted.reshape(peer_count * slot_count, 1)
     outgoing = outgoing_rows(place, target, wanted, hist, chips)
     received = lax.all_to_all(outgoing, ("x", "z"), split_axis=0, concat_axis=0, tiled=True)
@@ -512,21 +593,12 @@
     fresh = fresh.reshape(-1, model_width)
     other = pull(fresh, "c", 1)
 
-    sage_out, keep, send = sage(
-        place,
-        fresh,
-        other,
-        sums,
-        counts,
-        target,
-        hist,
-        w_self.T,
-        w_neigh.T,
-        upstream.T,
-        fanout,
-        share,
+    begun = sage_head(
+        place, fresh, counts, sums, target, hist, w_self.T, w_neigh.T, upstream.T, fanout
     )
-    parts = combine(keep, pull(send, "c", 1), chips)
+    act, weights, terms, send = sage(place, other, *begun, fanout, chips)
+    sage_out, keep = sage_tail(place, act, weights, terms, send)
+    parts = combine(keep, pull(send, "c", 1))
     parts = lax.all_to_all(parts, ("x", "z"), split_axis=0, concat_axis=0, tiled=True)
     grad_self_w, grad_neigh_w, grad_fresh, *terms = final_sums(
         place, parts, w_self.T, w_neigh.T, share, fanout

time: 124 us -> 121 us (0.976)
  waiting for transfers between devices: 35.2 us -> 33.2 us
    ppermute x18, waiting for transfers between devices: 25.4 us -> 18.4 us  [pull(): lax.ppermute(value, axis, [((i + shift) % count, i) for i in range(count)])]
    all_to_all x1, waiting for transfers between devices: 4.86 us -> 8.02 us  [local(): lax.all_to_all(outgoing, ('x', 'z'), split_axis=0, concat_axis=0, tiled=T...]
    all_to_all x1, waiting for transfers between devices: 4.99 us -> 6.77 us  [local(): lax.all_to_all(rows, ('x', 'z'), split_axis=0, concat_axis=0, tiled=True)]
    unnamed x28 -> x24, local copies, waits for them, and re-layouts: 2.66 us -> 1.87 us
    pallas_call x2 -> x4, Pallas kernels: 6.32 us -> 5.87 us  [the longest x1 2.28 us: sage_head(): pl.pallas_call(lambda *refs: head_kernel(fanout, *refs), out_shape=(jax.S...]
  transfers between devices with their start and end apart: 20 -> 20, of which waited for: 13 -> 12; matrix products, arithmetic and copies ran while one was open for 1% -> 1% of each run, Pallas kernels for 10% -> 14%
where the time goes in v2:
time: 121 us; the launch traced here: 120 us
  starting transfers between devices  37.1 us (31%)
  waiting for transfers between devices  33.2 us (27%)
  Pallas kernels  20.2 us (17%)
  blocking collectives  19.7 us (16%)
  local copies, waits for them, and re-layouts  5.01 us (4%)
  matrix products  3.34 us (3%)
    ppermute x18, starting transfers between devices, pull(): lax.ppermute(value, axis, [((i + shift) % count, i) for i in range(count)])  20.1 us
    all_to_all x1, blocking collectives, local(): lax.all_to_all(parts, ('x', 'z'), split_axis=0, concat_axis=0, tiled=True)  19.7 us
    ppermute x18, waiting for transfers between devices, pull(): lax.ppermute(value, axis, [((i + shift) % count, i) for i in range(count)])  18.4 us
    all_to_all x1, starting transfers between devices, local(): lax.all_to_all(outgoing, ('x', 'z'), split_axis=0, concat_axis=0, tiled=T...  11.3 us
    all_to_all x1, waiting for transfers between devices, local(): lax.all_to_all(outgoing, ('x', 'z'), split_axis=0, concat_axis=0, tiled=T...  8.02 us
    all_to_all x1, waiting for transfers between devices, local(): lax.all_to_all(rows, ('x', 'z'), split_axis=0, concat_axis=0, tiled=True)  6.77 us
    all_to_all x1, starting transfers between devices, local(): lax.all_to_all(rows, ('x', 'z'), split_axis=0, concat_axis=0, tiled=True)  5.71 us
    pallas_call x1, Pallas kernels, halo_sums(): pl.pallas_call(halo_kernel, out_shape=(jax.ShapeDtypeStruct(hist.shape, F...  4.81 us
  transfers between devices with their start and end apart: 20, of which 12 were waited for; matrix products, arithmetic and copies ran while one was open for 1% of the time, Pallas kernels for 14%

profile of v2, /device:TPU:32, one launch (start us, length us, event | category | flops | bytes accessed | tf_op | source)
XLA Modules:
  0.0 120.4 jit_solution(4440838920943856625)
XLA Ops:
  1.8 1.8 %convolution_convert_fusion.1 = bf16[512,576]{0,1:T(8,128)(2,1)S(1)} fusion(bf16[512,768]{1,0:T(8,128)(2,1)} %param.13, bf16[768,576]{0,1:T(8,128)(2,1)S(1)} %bitcast.56), kind=kOutput, calls=%fused_computation.3 | convolution fusion | flops 453279744 | bytes 2260992 | tf_op jit(solution)/shard_map/dot_general | solution.py:28
  6.6 3.3 %collective-permute-start = (bf16[128,768]{1,0:T(8,128)(2,1)S(1)}, bf16[128,768]{1,0:T(8,128)(2,1)S(1)}, u32[]{:S(2)}, u32[]{:S(2)}) collective-permute-start(bf16[128,768]{1,0:T(8,128)(2,1)S(1)} %get-tuple-element.66), channel_id=1, source_target_pairs={{2,0},{3,1},{0,2},{1,3},{6,4},{7,5},{4,6},{5,7},{10,8},{11,9},{8,1... | collective-permute-start | bytes 589832 | tf_op jit(solution)/shard_map/ppermute | solution.py:41
  12.4 2.8 %outgoing_rows.1 = bf16[32,2,16,768]{3,2,1,0:T(8,128)(2,1)} custom-call(s32[7]{0:T(128)S(1)} %pad_add_fusion.place_ref.refs_0_, s32[1,256]{1,0:T(1,128)S(1)} %bitcast.63, s32[1024,1]{1,0:T(8,128)S(1)} %reshape.55.wanted_ref, bf16[256,768]{1,0:T(8,128)(2,1)S(1)} %copy-done.5), custom_call_target="tpu_custom_call" | custom-call | flops 2000000000 | bytes 6000000 | tf_op jit(solution)/shard_map/outgoing_rows/pallas_call | solution.py:246
  15.2 11.3 %all-to-all-start.1 = ((bf16[32,2,16,768]{3,2,1,0:T(8,128)(2,1)}), bf16[32,2,16,768]{3,2,1,0:T(8,128)(2,1)}, u32[]{:S(2)}, u32[]{:S(2)}) async-start(bf16[32,2,16,768]{3,2,1,0:T(8,128)(2,1)} %outgoing_rows.1), calls=%async_computation.1 | async-start | bytes 3145728 | tf_op jit(solution)/shard_map/all_to_all | solution.py:580
  28.6 2.4 %collective-permute-start.5 = (bf16[128,768]{1,0:T(8,128)(2,1)S(1)}, bf16[128,768]{1,0:T(8,128)(2,1)S(1)}, u32[]{:S(2)}, u32[]{:S(2)}) collective-permute-start(bf16[128,768]{1,0:T(8,128)(2,1)S(1)} %first_norm.1.block_ref.first_ref), channel_id=1, source_target_pairs={{3,0},{0,1},{1,2},{2,3},{7,4},{4,5},{5,6},{6,7},{11,8},{8,9},{9,10... | collective-permute-start | bytes 589832 | tf_op jit(solution)/shard_map/ppermute | solution.py:41
  33.1 3.7 %collective-permute-done.7.block_ref = bf16[128,768]{1,0:T(8,128)(2,1)S(1)} collective-permute-done((bf16[128,768]{1,0:T(8,128)(2,1)S(1)}, bf16[128,768]{1,0:T(8,128)(2,1)S(1)}, u32[]{:S(2)}, u32[]{:S(2)}) %collective-permute-start.7) | collective-permute-done | bytes 196640 | tf_op jit(solution)/shard_map/ppermute | solution.py:41
  38.5 1.9 %collective-permute-done.5.block_ref = bf16[128,768]{1,0:T(8,128)(2,1)S(1)} collective-permute-done((bf16[128,768]{1,0:T(8,128)(2,1)S(1)}, bf16[128,768]{1,0:T(8,128)(2,1)S(1)}, u32[]{:S(2)}, u32[]{:S(2)}) %collective-permute-start.5) | collective-permute-done | bytes 196640 | tf_op jit(solution)/shard_map/ppermute | solution.py:41
  42.3 1.7 %collective-permute-start.4 = (bf16[128,768]{1,0:T(8,128)(2,1)S(1)}, bf16[128,768]{1,0:T(8,128)(2,1)S(1)}, u32[]{:S(2)}, u32[]{:S(2)}) collective-permute-start(bf16[128,768]{1,0:T(8,128)(2,1)S(1)} %feed.3), channel_id=1, source_target_pairs={{3,0},{0,1},{1,2},{2,3},{7,4},{4,5},{5,6},{6,7},{11,8},{8,9},{9,10... | collective-permute-start | bytes 589832 | tf_op jit(solution)/shard_map/ppermute | solution.py:41
  44.0 2.1 %collective-permute-done.8.across_ref = bf16[128,768]{1,0:T(8,128)(2,1)S(1)} collective-permute-done((bf16[128,768]{1,0:T(8,128)(2,1)S(1)}, bf16[128,768]{1,0:T(8,128)(2,1)S(1)}, u32[]{:S(2)}, u32[]{:S(2)}) %collective-permute-start.8) | collective-permute-done | bytes 196640 | tf_op jit(solution)/shard_map/ppermute | solution.py:41
  46.1 2.4 %collective-permute-done.6.far_ref = bf16[128,768]{1,0:T(8,128)(2,1)S(1)} collective-permute-done((bf16[128,768]{1,0:T(8,128)(2,1)S(1)}, bf16[128,768]{1,0:T(8,128)(2,1)S(1)}, u32[]{:S(2)}, u32[]{:S(2)}) %collective-permute-start.6) | collective-permute-done | bytes 196640 | tf_op jit(solution)/shard_map/ppermute | solution.py:41
  50.6 2.0 %collective-permute-start.11 = (bf16[1,768]{1,0:T(2,128)(2,1)S(1)}, bf16[1,768]{1,0:T(2,128)(2,1)S(1)}, u32[]{:S(2)}, u32[]{:S(2)}) collective-permute-start(bf16[1,768]{1,0:T(2,128)(2,1)S(1)} %pooled_row.1.own_ref), channel_id=1, source_target_pairs={{2,0},{3,1},{0,2},{1,3},{6,4},{7,5},{4,6},{5,7},{10,8},{11,9},{8,1... | collective-permute-start | bytes 4616 | tf_op jit(solution)/shard_map/ppermute | solution.py:41
  53.7 1.6 %collective-permute-done.10.far_ref = bf16[1,768]{1,0:T(2,128)(2,1)S(1)} collective-permute-done((bf16[1,768]{1,0:T(2,128)(2,1)S(1)}, bf16[1,768]{1,0:T(2,128)(2,1)S(1)}, u32[]{:S(2)}, u32[]{:S(2)}) %collective-permute-start.10) | collective-permute-done | bytes 1568 | tf_op jit(solution)/shard_map/ppermute | solution.py:41
  56.9 8.0 %all-to-all-done.1.received_hbm = bf16[32,2,16,768]{3,2,1,0:T(8,128)(2,1)} async-done(((bf16[32,2,16,768]{3,2,1,0:T(8,128)(2,1)}), bf16[32,2,16,768]{3,2,1,0:T(8,128)(2,1)}, u32[]{:S(2)}, u32[]{:S(2)}) %all-to-all-start.1) | async-done | bytes 1572896 | tf_op jit(solution)/shard_map/all_to_all | solution.py:580
  66.3 5.7 %all-to-all-start = ((bf16[32,4,768]{2,1,0:T(4,128)(2,1)}), bf16[32,4,768]{2,1,0:T(4,128)(2,1)S(1)}, u32[]{:S(2)}, u32[]{:S(2)}) async-start(bf16[32,4,768]{2,1,0:T(4,128)(2,1)} %spread_rows.1), calls=%async_computation | async-start | bytes 393216 | tf_op jit(solution)/shard_map/all_to_all | solution.py:589
  72.0 4.8 %halo_sums.1 = (f32[256,768]{1,0:T(8,128)S(1)}, bf16[256,256]{1,0:T(8,128)(2,1)S(1)}, bf16[256,256]{1,0:T(8,128)(2,1)S(1)}) custom-call(s32[7]{0:T(128)S(1)} %pad_add_fusion.place_ref.refs_0_, s32[1,256]{1,0:T(1,128)S(1)} %bitcast.64, s32[10,256]{1,0:T(8,128)S(1)} %bitcast.62, bf16[256,768]{1,0:T(8,128)(2,1)S(1)} %copy-done.5, ...), custom_call_target="tpu_custom_call" | custom-call | flops 1000000000 | bytes 5000000 | tf_op jit(solution)/shard_map/halo_sums/pallas_call | solution.py:325
  76.8 6.8 %all-to-all-done = bf16[32,4,768]{2,1,0:T(4,128)(2,1)S(1)} async-done(((bf16[32,4,768]{2,1,0:T(4,128)(2,1)}), bf16[32,4,768]{2,1,0:T(4,128)(2,1)S(1)}, u32[]{:S(2)}, u32[]{:S(2)}) %all-to-all-start) | async-done | bytes 196640 | tf_op jit(solution)/shard_map/all_to_all | solution.py:589
  83.8 2.3 %sage_head.1 = (bf16[256,768]{1,0:T(8,128)(2,1)S(1)}, f32[256,768]{1,0:T(8,128)S(1)}, bf16[2,256,128]{2,1,0:T(8,128)(2,1)S(1)}, bf16[2,256,256]{2,1,0:T(8,128)(2...) custom-call(s32[7]{0:T(128)S(1)} %pad_add_fusion.place_ref.refs_0_, ...), custom_call_target="tpu_custom_call" | custom-call | flops 3000000000 | bytes 4000000 | tf_op jit(solution)/shard_map/sage_head/pallas_call | solution.py:383
  86.1 2.2 %sage.1 = (f32[256,192]{1,0:T(8,128)S(1)}, f32[32,24,384]{2,1,0:T(8,128)S(1)}, f32[32,8,384]{2,1,0:T(8,128)S(1)}, bf16[32,16,384]{2,1,0:T(8,128)(2,1)S(1)}) custom-call(s32[7]{0:T(128)S(1)} %pad_add_fusion.place_ref.refs_0_, bf16[128,768]{1,0:T(8,128)(2,1)S(1)} %collective-permute-done.13.refs_1_, bf16[256,768]{1,0:T(8,128)(2,1)S(1)} %get-tuple-element.45.refs_2_, ...), custom_call_target="tpu_custom_call" | custom-call | flops 2000000000 | bytes 8000000 | tf_op jit(solution)/shard_map/sage/pallas_call | solution.py:461
  88.8 1.4 %sage_tail.1 = (bf16[192,256]{1,0:T(8,128)(2,1)}, f32[32,16,384]{2,1,0:T(8,128)S(1)}) custom-call(s32[7]{0:T(128)S(1)} %pad_add_fusion.place_ref.refs_0_, f32[256,192]{1,0:T(8,128)S(1)} %get-tuple-element.52.act_ref, f32[32,24,384]{2,1,0:T(8,128)S(1)} %get-tuple-element.53.weights_ref, f32[32,8,384]{2,1,0:T(8,128)S(1)} %get-tuple-element.54.terms_ref), custom_call_target="tpu_custom_call" | custom-call | flops 3000000000 | bytes 4000000 | tf_op jit(solution)/shard_map/sage_tail/pallas_call | solution.py:483
  90.2 19.7 %all_to_all.15.refs_1_ = bf16[32,16,384]{2,1,0:T(8,128)(2,1)S(1)} all-to-all(bf16[32,16,384]{2,1,0:T(8,128)(2,1)S(1)} %combine.1), channel_id=1, replica_groups=mesh['x'=4,'z'=8,'c'=2,'y'=4] {'x','z'}, dimensions={0} | all-to-all | bytes 786432 | tf_op jit(solution)/shard_map/all_to_all | solution.py:602
  109.9 1.7 %final_sums.1 = (f32[12,192]{1,0:T(8,128)}, f32[12,192]{1,0:T(8,128)}, f32[4,192]{1,0:T(4,128)S(1)}, f32[4,192]{1,0:T(4,128)S(1)}, f32[4,192]{1,0:T(4,128)S(1)}, /*index=5*/f32[4,192]{1,0:T(4,128)S(1)}) custom-call(s32[7]{0:T(128)S(1)} %pad_add_fusion.place_ref.refs_0_, bf16[32,16,384]{2,1,0:T(8,128)(2,1)S(1)} %all_to_all.15.refs_1_, ...), custom_call_target="tpu_custom_call" | custom-call | flops 10000000 | bytes 1000000 | tf_op jit(solution)/shard_map/final_sums/pallas_call | solution.py:531
  112.6 2.4 %collective-permute-start.16 = (f32[4,192]{1,0:T(4,128)S(1)}, f32[4,192]{1,0:T(4,128)S(1)}, u32[]{:S(2)}, u32[]{:S(2)}) collective-permute-start(f32[4,192]{1,0:T(4,128)S(1)} %get-tuple-element.60), channel_id=1, source_target_pairs={{1,0},{2,1},{3,2},{0,3},{5,4},{6,5},{7,6},{4,7},{9,8},{10,9},{11,1... | collective-permute-start | bytes 9224 | tf_op jit(solution)/shard_map/ppermute | solution.py:41
  115.0 1.8 %collective-permute-done.15 = f32[4,192]{1,0:T(4,128)S(1)} collective-permute-done((f32[4,192]{1,0:T(4,128)S(1)}, f32[4,192]{1,0:T(4,128)S(1)}, u32[]{:S(2)}, u32[]{:S(2)}) %collective-permute-start.15) | collective-permute-done | bytes 3104 | tf_op jit(solution)/shard_map/ppermute | solution.py:41
  116.8 3.0 %collective-permute-done.17 = f32[4,192]{1,0:T(4,128)S(1)} collective-permute-done((f32[4,192]{1,0:T(4,128)S(1)}, f32[4,192]{1,0:T(4,128)S(1)}, u32[]{:S(2)}, u32[]{:S(2)}) %collective-permute-start.17) | collective-permute-done | bytes 3104 | tf_op jit(solution)/shard_map/ppermute | solution.py:41
  (72 shorter events, 22.8 us)
Async XLA Ops:
  6.6 20.8 %collective-permute-start = (bf16[128,768]{1,0:T(8,128)(2,1)S(1)}, bf16[128,768]{1,0:T(8,128)(2,1)S(1)}, u32[]{:S(2)}, u32[]{:S(2)}) collective-permute-start(bf16[128,768]{1,0:T(8,128)(2,1)S(1)} %get-tuple-element.66), channel_id=1, source_target_pairs={{2,0},{3,1},{0,2},{1,3},{6,4},{7,5},{4,6},{5,7},{10,8},{11,9},{8,1... | collective-permute-start | bytes 589832 | tf_op jit(solution)/shard_map/ppermute | solution.py:41
  9.9 17.6 %collective-permute-start.1 = (bf16[128,768]{1,0:T(8,128)(2,1)S(1)}, bf16[128,768]{1,0:T(8,128)(2,1)S(1)}, u32[]{:S(2)}, u32[]{:S(2)}) collective-permute-start(bf16[128,768]{1,0:T(8,128)(2,1)S(1)} %get-tuple-element.65), channel_id=1, source_target_pairs={{1,0},{2,1},{3,2},{0,3},{5,4},{6,5},{7,6},{4,7},{9,8},{10,9},{11,1... | collective-permute-start | bytes 589832 | tf_op jit(solution)/shard_map/ppermute | solution.py:41
  11.0 16.5 %collective-permute-start.2 = (bf16[128,768]{1,0:T(8,128)(2,1)S(1)}, bf16[128,768]{1,0:T(8,128)(2,1)S(1)}, u32[]{:S(2)}, u32[]{:S(2)}) collective-permute-start(bf16[128,768]{1,0:T(8,128)(2,1)S(1)} %get-tuple-element.64), channel_id=1, source_target_pairs={{3,0},{0,1},{1,2},{2,3},{7,4},{4,5},{5,6},{6,7},{11,8},{8,9},{9,10... | collective-permute-start | bytes 589832 | tf_op jit(solution)/shard_map/ppermute | solution.py:41
  15.2 49.7 %all-to-all-start.1 = ((bf16[32,2,16,768]{3,2,1,0:T(8,128)(2,1)}), bf16[32,2,16,768]{3,2,1,0:T(8,128)(2,1)}, u32[]{:S(2)}, u32[]{:S(2)}) async-start(bf16[32,2,16,768]{3,2,1,0:T(8,128)(2,1)} %outgoing_rows.1), calls=%async_computation.1 | async-start | bytes 3145728 | tf_op jit(solution)/shard_map/all_to_all | solution.py:580
  27.8 9.0 %collective-permute-start.7 = (bf16[128,768]{1,0:T(8,128)(2,1)S(1)}, bf16[128,768]{1,0:T(8,128)(2,1)S(1)}, u32[]{:S(2)}, u32[]{:S(2)}) collective-permute-start(bf16[128,768]{1,0:T(8,128)(2,1)S(1)} %first_norm.1.block_ref.first_ref), channel_id=1, source_target_pairs={{2,0},{3,1},{0,2},{1,3},{6,4},{7,5},{4,6},{5,7},{10,8},{11,9},{8,1... | collective-permute-start | bytes 589832 | tf_op jit(solution)/shard_map/ppermute | solution.py:41
  28.6 11.7 %collective-permute-start.5 = (bf16[128,768]{1,0:T(8,128)(2,1)S(1)}, bf16[128,768]{1,0:T(8,128)(2,1)S(1)}, u32[]{:S(2)}, u32[]{:S(2)}) collective-permute-start(bf16[128,768]{1,0:T(8,128)(2,1)S(1)} %first_norm.1.block_ref.first_ref), channel_id=1, source_target_pairs={{3,0},{0,1},{1,2},{2,3},{7,4},{4,5},{5,6},{6,7},{11,8},{8,9},{9,10... | collective-permute-start | bytes 589832 | tf_op jit(solution)/shard_map/ppermute | solution.py:41
  31.0 10.7 %collective-permute-start.3 = (bf16[128,768]{1,0:T(8,128)(2,1)S(1)}, bf16[128,768]{1,0:T(8,128)(2,1)S(1)}, u32[]{:S(2)}, u32[]{:S(2)}) collective-permute-start(bf16[128,768]{1,0:T(8,128)(2,1)S(1)} %first_norm.1.block_ref.first_ref), channel_id=1, source_target_pairs={{1,0},{2,1},{3,2},{0,3},{5,4},{6,5},{7,6},{4,7},{9,8},{10,9},{11,1... | collective-permute-start | bytes 589832 | tf_op jit(solution)/shard_map/ppermute | solution.py:41
  37.5 8.6 %collective-permute-start.8 = (bf16[128,768]{1,0:T(8,128)(2,1)S(1)}, bf16[128,768]{1,0:T(8,128)(2,1)S(1)}, u32[]{:S(2)}, u32[]{:S(2)}) collective-permute-start(bf16[128,768]{1,0:T(8,128)(2,1)S(1)} %feed.5), channel_id=1, source_target_pairs={{2,0},{3,1},{0,2},{1,3},{6,4},{7,5},{4,6},{5,7},{10,8},{11,9},{8,1... | collective-permute-start | bytes 589832 | tf_op jit(solution)/shard_map/ppermute | solution.py:41
  41.0 7.5 %collective-permute-start.6 = (bf16[128,768]{1,0:T(8,128)(2,1)S(1)}, bf16[128,768]{1,0:T(8,128)(2,1)S(1)}, u32[]{:S(2)}, u32[]{:S(2)}) collective-permute-start(bf16[128,768]{1,0:T(8,128)(2,1)S(1)} %feed.4), channel_id=1, source_target_pairs={{1,0},{2,1},{3,2},{0,3},{5,4},{6,5},{7,6},{4,7},{9,8},{10,9},{11,1... | collective-permute-start | bytes 589832 | tf_op jit(solution)/shard_map/ppermute | solution.py:41
  42.3 7.2 %collective-permute-start.4 = (bf16[128,768]{1,0:T(8,128)(2,1)S(1)}, bf16[128,768]{1,0:T(8,128)(2,1)S(1)}, u32[]{:S(2)}, u32[]{:S(2)}) collective-permute-start(bf16[128,768]{1,0:T(8,128)(2,1)S(1)} %feed.3), channel_id=1, source_target_pairs={{3,0},{0,1},{1,2},{2,3},{7,4},{4,5},{5,6},{6,7},{11,8},{8,9},{9,10... | collective-permute-start | bytes 589832 | tf_op jit(solution)/shard_map/ppermute | solution.py:41
  50.4 21.6 %copy-start.7 = (s32[256,10]{0,1:T(8,128)S(1)}, s32[256,10]{0,1:T(8,128)}, u32[]{:S(2)}) copy-start(s32[256,10]{0,1:T(8,128)} %param.20) | copy-start | bytes 30724
  50.4 4.9 %collective-permute-start.10 = (bf16[1,768]{1,0:T(2,128)(2,1)S(1)}, bf16[1,768]{1,0:T(2,128)(2,1)S(1)}, u32[]{:S(2)}, u32[]{:S(2)}) collective-permute-start(bf16[1,768]{1,0:T(2,128)(2,1)S(1)} %pooled_row.1.own_ref), channel_id=1, source_target_pairs={{3,0},{0,1},{1,2},{2,3},{7,4},{4,5},{5,6},{6,7},{11,8},{8,9},{9,10... | collective-permute-start | bytes 4616 | tf_op jit(solution)/shard_map/ppermute | solution.py:41
  50.6 5.1 %collective-permute-start.11 = (bf16[1,768]{1,0:T(2,128)(2,1)S(1)}, bf16[1,768]{1,0:T(2,128)(2,1)S(1)}, u32[]{:S(2)}, u32[]{:S(2)}) collective-permute-start(bf16[1,768]{1,0:T(2,128)(2,1)S(1)} %pooled_row.1.own_ref), channel_id=1, source_target_pairs={{2,0},{3,1},{0,2},{1,3},{6,4},{7,5},{4,6},{5,7},{10,8},{11,9},{8,1... | collective-permute-start | bytes 4616 | tf_op jit(solution)/shard_map/ppermute | solution.py:41
  52.6 3.6 %collective-permute-start.9 = (bf16[1,768]{1,0:T(2,128)(2,1)S(1)}, bf16[1,768]{1,0:T(2,128)(2,1)S(1)}, u32[]{:S(2)}, u32[]{:S(2)}) collective-permute-start(bf16[1,768]{1,0:T(2,128)(2,1)S(1)} %pooled_row.1.own_ref), channel_id=1, source_target_pairs={{1,0},{2,1},{3,2},{0,3},{5,4},{6,5},{7,6},{4,7},{9,8},{10,9},{11,1... | collective-permute-start | bytes 4616 | tf_op jit(solution)/shard_map/ppermute | solution.py:41
  66.2 5.8 %collective-permute-start.12 = (bf16[32,16,768]{2,1,0:T(8,128)(2,1)S(1)}, bf16[32,16,768]{2,1,0:T(8,128)(2,1)}, u32[]{:S(2)}, u32[]{:S(2)}) collective-permute-start(bf16[32,16,768]{2,1,0:T(8,128)(2,1)S(1)} %dynamic-slice_bitcast_fusion), channel_id=1, source_target_pairs={{4,0},{0,4},{5,1},{1,5},{6,2},{2,6},{7,3},{3,7},{12,8},{8,12},{13,... | collective-permute-start | bytes 2359304 | tf_op jit(solution)/shard_map/ppermute | solution.py:41
  66.3 17.4 %all-to-all-start = ((bf16[32,4,768]{2,1,0:T(4,128)(2,1)}), bf16[32,4,768]{2,1,0:T(4,128)(2,1)S(1)}, u32[]{:S(2)}, u32[]{:S(2)}) async-start(bf16[32,4,768]{2,1,0:T(4,128)(2,1)} %spread_rows.1), calls=%async_computation | async-start | bytes 393216 | tf_op jit(solution)/shard_map/all_to_all | solution.py:589
  72.0 11.8 %copy-start.1 = (bf16[768,192]{0,1:T(8,128)(2,1)S(1)}, bf16[768,192]{0,1:T(8,128)(2,1)}, u32[]{:S(2)}) copy-start(bf16[768,192]{0,1:T(8,128)(2,1)} %param.23) | copy-start | bytes 884740
  72.0 11.8 %copy-start.2 = (bf16[768,192]{0,1:T(8,128)(2,1)S(1)}, bf16[768,192]{0,1:T(8,128)(2,1)}, u32[]{:S(2)}) copy-start(bf16[768,192]{0,1:T(8,128)(2,1)} %param.24) | copy-start | bytes 884740
  72.0 11.8 %copy-start.6 = (bf16[256,192]{0,1:T(8,128)(2,1)S(1)}, bf16[256,192]{0,1:T(8,128)(2,1)}, u32[]{:S(2)}) copy-start(bf16[256,192]{0,1:T(8,128)(2,1)} %param.25) | copy-start | bytes 294916
  83.7 2.4 %collective-permute-start.13 = (bf16[128,768]{1,0:T(8,128)(2,1)S(1)}, bf16[128,768]{1,0:T(8,128)(2,1)S(1)}, u32[]{:S(2)}, u32[]{:S(2)}) collective-permute-start(bf16[128,768]{1,0:T(8,128)(2,1)S(1)} %reshape.54.refs_1_), channel_id=1, source_target_pairs={{4,0},{0,4},{5,1},{1,5},{6,2},{2,6},{7,3},{3,7},{12,8},{8,12},{13,... | collective-permute-start | bytes 589832 | tf_op jit(solution)/shard_map/ppermute | solution.py:41
  88.3 1.9 %collective-permute-start.14 = (bf16[32,16,384]{2,1,0:T(8,128)(2,1)S(1)}, bf16[32,16,384]{2,1,0:T(8,128)(2,1)S(1)}, u32[]{:S(2)}, u32[]{:S(2)}) collective-permute-start(bf16[32,16,384]{2,1,0:T(8,128)(2,1)S(1)} %get-tuple-element.57), channel_id=1, source_target_pairs={{4,0},{0,4},{5,1},{1,5},{6,2},{2,6},{7,3},{3,7},{12,8},{8,12},{13,... | collective-permute-start | bytes 1179656 | tf_op jit(solution)/shard_map/ppermute | solution.py:41
  111.6 5.1 %collective-permute-start.15 = (f32[4,192]{1,0:T(4,128)S(1)}, f32[4,192]{1,0:T(4,128)S(1)}, u32[]{:S(2)}, u32[]{:S(2)}) collective-permute-start(f32[4,192]{1,0:T(4,128)S(1)} %get-tuple-element.59), channel_id=1, source_target_pairs={{2,0},{3,1},{0,2},{1,3},{6,4},{7,5},{4,6},{5,7},{10,8},{11,9},{8,1... | collective-permute-start | bytes 9224 | tf_op jit(solution)/shard_map/ppermute | solution.py:41
  112.6 4.1 %collective-permute-start.16 = (f32[4,192]{1,0:T(4,128)S(1)}, f32[4,192]{1,0:T(4,128)S(1)}, u32[]{:S(2)}, u32[]{:S(2)}) collective-permute-start(f32[4,192]{1,0:T(4,128)S(1)} %get-tuple-element.60), channel_id=1, source_target_pairs={{1,0},{2,1},{3,2},{0,3},{5,4},{6,5},{7,6},{4,7},{9,8},{10,9},{11,1... | collective-permute-start | bytes 9224 | tf_op jit(solution)/shard_map/ppermute | solution.py:41
  115.0 4.8 %collective-permute-start.17 = (f32[4,192]{1,0:T(4,128)S(1)}, f32[4,192]{1,0:T(4,128)S(1)}, u32[]{:S(2)}, u32[]{:S(2)}) collective-permute-start(f32[4,192]{1,0:T(4,128)S(1)} %get-tuple-element.61), channel_id=1, source_target_pairs={{3,0},{0,1},{1,2},{2,3},{7,4},{4,5},{5,6},{6,7},{11,8},{8,9},{9,10... | collective-permute-start | bytes 9224 | tf_op jit(solution)/shard_map/ppermute | solution.py:41
  (8 other events, 29.1 us)

commit v3 on v2

--- a/solution.py
+++ b/solution.py
@@ -34,6 +34,10 @@
 
 def dot_nt(a, b):
     return lax.dot_general(a, b, (((1,), (1,)), ((), ())), preferred_element_type=F32)
+
+
+def swap(value):
+    return lax.ppermute(value, "y", [(i, i ^ 1) for i in range(NY)])
 
 
 def pull(value, axis, shift):
@@ -226,126 +230,177 @@
     return ((slot // NY % chips) * NC + slot_core) * NY + slot_y
 
 
-def outgoing_kernel(place_ref, target_ref, wanted_ref, hist_hbm, out_ref, hist_ref, semaphores):
+def outgoing_kernel(
+    place_ref, target_ref, wanted_ref, hist_hbm, out_hbm, hist_ref, semaphores, rows_ref, out_sems
+):
     copies = fetch((hist_hbm,), (hist_ref,), semaphores)
-    count, width = hist_ref.shape
+    count, width = hist_ref.shape[0], rows_ref.shape[3]
     _, row_text = text_rows(target_ref[...], count, place_ref[DOM])
     column = lax.broadcasted_iota(jnp.int32, (count, width), 1)
     code = jnp.where(
         column == 0, 32 + row_text // 16, jnp.where(column == 1, 32 + row_text % 16, 0)
     ).astype(F32)
-    ids = lax.broadcasted_iota(jnp.int32, (wanted_ref.shape[0], count), 1)
-    pick = (wanted_ref[...] == ids).astype(F32).astype(BF)
+    parts = out_sems.shape[0]
+    chips = rows_ref.shape[0] // parts
+    size = wanted_ref.shape[0] // parts
+    ids = lax.broadcasted_iota(jnp.int32, (size, count), 1)
     copies[0].wait()
-    coded = jnp.where(row_text >= 0, code, hist_ref[...].astype(F32)).astype(BF)
-    out_ref[...] = dot(pick, coded).astype(BF).reshape(out_ref.shape)
+    hist = sliced(hist_ref[...].astype(F32), place_ref[ME] % 2, width)
+    coded = jnp.where(row_text >= 0, code, hist).astype(BF)
+    sent = []
+    for part in range(parts):
+        wanted = wanted_ref[part * size : (part + 1) * size, :]
+        pick = (wanted == ids).astype(F32).astype(BF)
+        chunk = rows_ref.at[part * chips : (part + 1) * chips]
+        chunk[...] = dot(pick, coded).astype(BF).reshape(chunk.shape)
+        copy = pltpu.make_async_copy(
+            chunk, out_hbm.at[part * chips : (part + 1) * chips], out_sems.at[part]
+        )
+        copy.start()
+        sent.append(copy)
+    for copy in sent:
+        copy.wait()
 
 
 def outgoing_rows(place, target, wanted, hist, chips):
-    rows, width = wanted.shape[0], hist.shape[1]
+    rows, width = wanted.shape[0], hist.shape[1] // 2
+    shape = (chips, NC, rows // chips // NC, width)
+    parts = 4
     return pl.pallas_call(
         outgoing_kernel,
-        out_shape=jax.ShapeDtypeStruct((chips, NC, rows // chips // NC, width), BF),
+        out_shape=jax.ShapeDtypeStruct(shape, BF),
         in_specs=scalars() + whole(2) + far_off(1),
-        out_specs=pl.BlockSpec(),
-        scratch_shapes=room(hist),
+        out_specs=far_off(1)[0],
+        scratch_shapes=room(hist)
+        + [pltpu.VMEM(shape, BF), pltpu.SemaphoreType.DMA((parts,))],
         name="outgoing_rows",
         **grant(52, 2000000000, 6000000),
     )(place, target, wanted, hist)
 
 
+def counts_kernel(slot_count, place_ref, links_ref, counts_ref):
+    fanout, count = links_ref.shape
+    size = (counts_ref.shape[0] - count) // NC
+    local = lax.broadcasted_iota(jnp.int32, (count, count), 0)
+    row = lax.broadcasted_iota(jnp.int32, (size, count), 0)
+    core = place_ref[CORE]
+    start = 0
+    for ids in (
+        local,
+        (row // slot_count * NC + core) * slot_count + row % slot_count + count,
+        (row // slot_count * NC + 1 - core) * slot_count + row % slot_count + count,
+    ):
+        total = jnp.zeros(ids.shape, F32)
+        for neighbour in range(fanout):
+            total = total + (links_ref[neighbour : neighbour + 1, :] == ids).astype(F32)
+        counts_ref[start : start + ids.shape[0], :] = total.astype(BF)
+        start += ids.shape[0]
+
+
+def link_counts(place, links, peers, slot_count):
+    count = links.shape[1]
+    return pl.pallas_call(
+        lambda *refs: counts_kernel(slot_count, *refs),
+        out_shape=jax.ShapeDtypeStruct((count + peers * slot_count, count), BF),
+        in_specs=scalars() + whole(1),
+        out_specs=pl.BlockSpec(),
+        name="link_counts",
+        **grant(48, 4000000000, 2000000),
+    )(place, links)
+
+
 def halo_kernel(
     place_ref,
     target_hbm,
-    links_hbm,
+    counts_hbm,
     hist_hbm,
     received_hbm,
     across_hbm,
     sum_ref,
-    counts_slot_ref,
-    counts_text_ref,
+    texts_ref,
     target_ref,
-    links_ref,
+    counts_ref,
     hist_ref,
     received_ref,
     across_ref,
     semaphores,
 ):
+    core, me = place_ref[CORE], place_ref[ME]
+    chips, slot_count, width = received_ref.shape
+    size = chips * slot_count
+    count = hist_ref.shape[0]
     copies = fetch(
-        (target_hbm, links_hbm, hist_hbm, received_hbm, across_hbm),
-        (target_ref, links_ref, hist_ref, received_ref, across_ref),
+        (target_hbm, counts_hbm, hist_hbm, received_hbm.at[:, core], across_hbm.at[:, core]),
+        (target_ref, counts_ref, hist_ref, received_ref, across_ref),
         semaphores,
     )
-    chips, slot_count, width = across_ref.shape
-    size = chips * slot_count
-    fanout, count = links_ref.shape
-    texts = target_ref.shape[1]
-    core, me = place_ref[CORE], place_ref[ME]
-    slots = slot_texts(texts, chips, core, me)
+    slots = slot_texts(target_ref.shape[1], chips, core, me)
     text_ids = lax.broadcasted_iota(jnp.int32, slots.shape, 1)
     copies[0].wait()
-    copies[1].wait()
     place, row_text = text_rows(target_ref[...], count, place_ref[DOM])
-
-    def counted(ids):
-        total = jnp.zeros(ids.shape, F32)
-        for neighbour in range(fanout):
-            total = total + (links_ref[neighbour : neighbour + 1, :] == ids).astype(F32)
-        return total.astype(BF)
-
-    near = counted(lax.broadcasted_iota(jnp.int32, (count, count), 0))
-    copies[2].wait()
-    base = jnp.where(row_text >= 0, 0.0, hist_ref[...].astype(F32))
+    for copy in copies[1:]:
+        copy.wait()
+    near = counts_ref[:count, :]
+    base = jnp.where(row_text >= 0, 0.0, sliced(hist_ref[...].astype(F32), me % 2, width))
     total = dot_t(near, base.astype(BF))
     counts_slot = dot_t(near, (row_text == slots).astype(F32).astype(BF))
     counts_text = dot_t(near, place)
-    copies[3].wait()
-    copies[4].wait()
-    for received, source in ((received_ref[:, core], core), (across_ref[...], 1 - core)):
-        received = received.reshape(size, width)
+    for k, ref in enumerate((received_ref, across_ref)):
+        received = ref[...].reshape(size, width)
         first = received[:, 0:128].astype(F32)
         is_text = first[:, 0:1] > 24
         text = ((first[:, 0:1] - 32) * 16 + first[:, 1:2] - 32).astype(jnp.int32)
         text = jnp.where(is_text, text, -1)
         halo = received * jnp.where(is_text, 0.0, 1.0).astype(BF)
-        row = lax.broadcasted_iota(jnp.int32, (size, count), 0)
-        row = (row // slot_count * NC + source) * slot_count + row % slot_count
-        far = counted(row + count)
+        far = counts_ref[count + k * size : count + (k + 1) * size, :]
         total = total + dot_t(far, halo)
         counts_slot = counts_slot + dot_t(far, (text == slots).astype(F32).astype(BF))
         counts_text = counts_text + dot_t(far, (text == text_ids).astype(F32).astype(BF))
-    sum_ref[...] = total
-    counts_slot_ref[...] = counts_slot.astype(BF)
-    counts_text_ref[...] = counts_text.astype(BF)
-
-
-def halo_sums(place, received, across, target, links, hist):
+    sum_ref[...] = total.astype(BF)
+    texts_ref[0] = counts_slot.astype(BF)
+    texts_ref[1] = counts_text.astype(BF)
+
+
+def halo_sums(place, received, across, target, counts, hist):
     count = hist.shape[0]
-    square = jax.ShapeDtypeStruct((count, target.shape[1]), BF)
+    square = jax.ShapeDtypeStruct((2, count, target.shape[1]), BF)
+    rows = pltpu.VMEM((received.shape[0],) + received.shape[2:], BF)
     return pl.pallas_call(
         halo_kernel,
-        out_shape=(jax.ShapeDtypeStruct(hist.shape, F32), square, square),
+        out_shape=(jax.ShapeDtypeStruct((count, received.shape[3]), BF), square),
         in_specs=scalars() + far_off(5),
-        out_specs=(pl.BlockSpec(),) * 3,
-        scratch_shapes=room(target, links, hist, received, across),
+        out_specs=(pl.BlockSpec(),) * 2,
+        scratch_shapes=room(target, counts, hist)[:-1]
+        + [rows, rows, pltpu.SemaphoreType.DMA((5,))],
         name="halo_sums",
-        **grant(52, 1000000000, 5000000),
-    )(place, target, links, hist, received, across)
+        **grant(32, 1000000000, 5000000),
+    )(place, target, counts, hist, received, across)
 
 
 def head_kernel(fanout, place_ref, fresh_ref, *refs):
-    sources, semaphores, (counts_ref, sums_ref, hist_ref, target_ref, up_ref) = (
+    sources, semaphores, (counts_ref, sums_ref, got_ref, hist_ref, target_ref, up_ref) = (
         refs[:8],
-        refs[-6],
-        refs[-5:],
+        refs[-7],
+        refs[-6:],
     )
-    table_ref, agg_ref, other_ref, texts_ref, w_self_ref, w_neigh_ref, upstream_ref = refs[8:-6]
-    target_hbm, counts_hbm, texts_hbm, sums_hbm, hist_hbm, w_self_hbm, w_neigh_hbm, up_hbm = sources
+    table_ref, agg_ref, other_ref, texts_ref, w_self_ref, w_neigh_ref, upstream_ref = refs[8:-7]
+    target_hbm, counts_hbm, sums_hbm, got_hbm, hist_hbm, w_self_hbm, w_neigh_hbm, up_hbm = sources
     copies = fetch(
-        (counts_hbm, sums_hbm, target_hbm, hist_hbm, up_hbm, texts_hbm, w_self_hbm, w_neigh_hbm),
+        (
+            counts_hbm.at[0],
+            sums_hbm,
+            got_hbm,
+            target_hbm,
+            hist_hbm,
+            up_hbm,
+            counts_hbm.at[1],
+            w_self_hbm,
+            w_neigh_hbm,
+        ),
         (
             counts_ref,
             sums_ref,
+            got_ref,
             target_ref,
             hist_ref,
             up_ref,
@@ -358,28 +413,30 @@
     half = fresh_ref.shape[0]
     count = hist_ref.shape[0]
     fresh = fresh_ref[...]
-    copies[0].wait()
-    copies[1].wait()
-    agg_ref[...] = sums_ref[...] + dot(counts_ref[:, :half], fresh)
+    for copy in copies[:3]:
+        copy.wait()
+    first, second = sums_ref[...].astype(F32), got_ref[...].astype(F32)
+    low = place_ref[ME] % 2 == 0
+    sums = [jnp.where(low, first, second), jnp.where(low, second, first)]
+    agg_ref[...] = jnp.concatenate(sums, axis=1) + dot(counts_ref[:, :half], fresh)
     other_ref[1] = counts_ref[:, half:]
-    copies[2].wait()
+    copies[3].wait()
     place, row_text = text_rows(target_ref[...], count, place_ref[DOM])
     texts_ref[0] = place
     slots = slot_texts(place.shape[1], half // NY, place_ref[CORE], place_ref[ME])
     place_slot = (row_text == slots).astype(F32).astype(BF)
     other_ref[0] = place_slot[:, half:]
     placed = dot(place_slot[:, :half], fresh)
-    copies[3].wait()
+    copies[4].wait()
     table_ref[...] = jnp.where(row_text >= 0, placed, hist_ref[...].astype(F32)).astype(BF)
-    copies[4].wait()
+    copies[5].wait()
     upstream_ref[...] = up_ref[...].astype(F32).T
-    for copy in copies[5:]:
+    for copy in copies[6:]:
         copy.wait()
 
 
 def sage_head(place, fresh, counts, sums, target, hist, w_self, w_neigh, upstream, fanout):
-    counts_slot, counts_text = counts
-    count, texts = counts_text.shape
+    _, count, texts = counts.shape
     return pl.pallas_call(
         lambda *refs: head_kernel(fanout, *refs),
         out_shape=(
@@ -394,16 +451,17 @@
         in_specs=scalars() + whole(1) + far_off(8),
         out_specs=tuple(whole(7)),
         scratch_shapes=[
-            pltpu.SemaphoreType.DMA((8,)),
-            pltpu.VMEM(counts_slot.shape, BF),
-            pltpu.VMEM(sums.shape, F32),
+            pltpu.SemaphoreType.DMA((9,)),
+            pltpu.VMEM((count, texts), BF),
+            pltpu.VMEM(sums[0].shape, BF),
+            pltpu.VMEM(sums[1].shape, BF),
             pltpu.VMEM(hist.shape, BF),
             pltpu.VMEM(target.shape, jnp.int32),
             pltpu.VMEM(upstream.shape, BF),
         ],
         name="sage_head",
         **grant(48, 3000000000, 4000000),
-    )(place, fresh, target, counts_slot, counts_text, sums, hist, w_self, w_neigh, upstream)
+    )(place, fresh, target, counts, *sums, hist, w_self, w_neigh, upstream)
 
 
 def sage_kernel(
@@ -509,14 +567,9 @@
     )(keep, got)
 
 
-def final_kernel(
-    fanout, place_ref, parts_ref, w_self_ref, w_neigh_ref, self_ref, neigh_ref, *term_refs
-):
-    share, quarter = self_ref.shape
-    total = jnp.sum(parts_ref[...].astype(F32), axis=0)
-    self_ref[...] = total[:share, :quarter]
-    neigh_ref[...] = total[:share, quarter:]
-    rows = total[share:]
+def final_kernel(fanout, share, place_ref, parts_ref, w_self_ref, w_neigh_ref, *term_refs):
+    quarter = w_self_ref.shape[0]
+    rows = jnp.sum(parts_ref[...].astype(F32), axis=0)[share:]
     at_rows = rows[:, :quarter].astype(BF)
     at_links = (rows[:, quarter:] / fanout).astype(BF)
     terms = dot(at_rows, w_self_ref[...]) + dot(at_links, w_neigh_ref[...])
@@ -524,18 +577,36 @@
         ref[...] = sliced(terms, lax.rem(place_ref[ME] + s, NY), quarter)
 
 
-def final_sums(place, parts, w_self, w_neigh, share, fanout):
+def final_terms(place, parts, w_self, w_neigh, share, fanout):
     quarter = w_self.shape[0]
-    grads = jax.ShapeDtypeStruct((share, quarter), F32)
     texts = jax.ShapeDtypeStruct((parts.shape[1] - share, quarter), F32)
     return pl.pallas_call(
-        lambda *refs: final_kernel(fanout, *refs),
-        out_shape=(grads, grads) + (texts,) * NY,
+        lambda *refs: final_kernel(fanout, share, *refs),
+        out_shape=(texts,) * NY,
         in_specs=scalars() + whole(3),
-        out_specs=tuple(whole(2 + NY)),
-        name="final_sums",
+        out_specs=tuple(whole(NY)),
+        name="final_terms",
         **grant(16, 10000000, 1000000),
     )(place, parts, w_self, w_neigh)
+
+
+def weight_kernel(parts_ref, self_ref, neigh_ref):
+    share, quarter = self_ref.shape
+    total = jnp.sum(parts_ref[...].astype(F32), axis=0)
+    self_ref[...] = total[:share, :quarter]
+    neigh_ref[...] = total[:share, quarter:]
+
+
+def final_weights(parts, share):
+    grads = jax.ShapeDtypeStruct((share, parts.shape[2] // 2), F32)
+    return pl.pallas_call(
+        weight_kernel,
+        out_shape=(grads, grads),
+        in_specs=whole(1),
+        out_specs=(pl.BlockSpec(),) * 2,
+        name="final_weights",
+        **grant(16, 3000000000, 4000000),
+    )(parts)
 
 
 def local(
@@ -581,14 +652,20 @@
 
     others = {s: pull(first_norm, "y", s) for s in (1, 3, 2)}
     own, up, down = feed_first(first_norm, w_up, w_down)
+    up, late_nbr = lax.optimization_barrier((up, nbr))
+    linked = link_counts(place, late_nbr.T, peer_count, slot_count)
+    others[2], linked = lax.optimization_barrier((others[2], linked))
     parts = [own] + [pull(feed(others[s], up, down), "y", NY - s) for s in (1, 3, 2)]
     fresh_row = pooled_row(place, first_norm, parts)
 
-    rows = spread_rows([fresh_row] + [pull(fresh_row, "y", s) for s in (1, 3, 2)], chips)
-    _, received = lax.optimization_barrier((rows, received))
+    rows = [fresh_row] + [pull(fresh_row, "y", s) for s in (1, 3, 2)]
+    _, received = lax.optimization_barrier((fresh_row, received))
+    across = pull(received, "c", 1)
+    sums, counts = halo_sums(place, received, across, target, linked, hist)
+    rows, sums, counts = lax.optimization_barrier((rows, sums, counts))
+    rows = spread_rows(rows, chips)
     fresh = lax.all_to_all(rows, ("x", "z"), split_axis=0, concat_axis=0, tiled=True)
-    across = pull(lax.dynamic_index_in_dim(received, 1 - my_c, 1, keepdims=False), "c", 1)
-    sums, *counts = halo_sums(place, received, across, target, nbr.T, hist)
+    sums = (sums, swap(sums))
     fresh, sums = lax.optimization_barrier((fresh, sums))
     fresh = fresh.reshape(-1, model_width)
     other = pull(fresh, "c", 1)
@@ -600,9 +677,8 @@
     sage_out, keep = sage_tail(place, act, weights, terms, send)
     parts = combine(keep, pull(send, "c", 1))
     parts = lax.all_to_all(parts, ("x", "z"), split_axis=0, concat_axis=0, tiled=True)
-    grad_self_w, grad_neigh_w, grad_fresh, *terms = final_sums(
-        place, parts, w_self.T, w_neigh.T, share, fanout
-    )
+    grad_fresh, *terms = final_terms(place, parts, w_self.T, w_neigh.T, share, fanout)
+    grad_self_w, grad_neigh_w = final_weights(parts, share)
     for s in (2, 1, 3):
         grad_fresh = grad_fresh + pull(terms[NY - s - 1], "y", s)
     return (sage_out.T, grad_fresh, grad_self_w, grad_neigh_w)

time: 121 us -> 116 us (0.959)
  waiting for transfers between devices: 33.2 us -> 21.9 us
  starting transfers between devices: 37.1 us -> 43.6 us
    all_to_all x1, waiting for transfers between devices: 8.02 us -> 0.01 us  [local(): lax.all_to_all(outgoing, ('x', 'z'), split_axis=0, concat_axis=0, tiled=T...]
    ppermute x18, waiting for transfers between devices: 18.4 us -> 11.9 us  [pull(): lax.ppermute(value, axis, [((i + shift) % count, i) for i in range(count)])]
    ppermute x0 -> x1, waiting for transfers between devices: none -> 5.11 us  [swap(): return lax.ppermute(value, 'y', [(i, i ^ 1) for i in range(NY)])]
    all_to_all x1, starting transfers between devices: 5.71 us -> 9.79 us  [local(): lax.all_to_all(rows, ('x', 'z'), split_axis=0, concat_axis=0, tiled=True)]
    all_to_all x1, waiting for transfers between devices: 6.77 us -> 4.82 us  [local(): lax.all_to_all(rows, ('x', 'z'), split_axis=0, concat_axis=0, tiled=True)]
    ppermute x18, starting transfers between devices: 20.1 us -> 21.5 us  [pull(): lax.ppermute(value, axis, [((i + shift) % count, i) for i in range(count)])]
    pallas_call x3 -> x5, Pallas kernels: 9.32 us -> 8.19 us  [the longest x1 2.3 us: halo_sums(): pl.pallas_call(halo_kernel, out_shape=(jax.ShapeDtypeStruct((count, recei...]
    unnamed x24 -> x28, local copies, waits for them, and re-layouts: 1.87 us -> 2.96 us
  transfers between devices with their start and end apart: 20 -> 21, of which waited for: 12 -> 9; matrix products, arithmetic and copies ran while one was open for 1% -> 1% of each run, Pallas kernels for 14% -> 13%
where the time goes in v3:
time: 116 us; the launch traced here: 115 us
  starting transfers between devices  43.6 us (38%)
  waiting for transfers between devices  21.9 us (19%)
  blocking collectives  20.2 us (17%)
  Pallas kernels  19.5 us (17%)
  local copies, waits for them, and re-layouts  4.91 us (4%)
  matrix products  3.34 us (3%)
    ppermute x18, starting transfers between devices, pull(): lax.ppermute(value, axis, [((i + shift) % count, i) for i in range(count)])  21.5 us
    all_to_all x1, blocking collectives, local(): lax.all_to_all(parts, ('x', 'z'), split_axis=0, concat_axis=0, tiled=True)  20.2 us
    ppermute x18, waiting for transfers between devices, pull(): lax.ppermute(value, axis, [((i + shift) % count, i) for i in range(count)])  11.9 us
    all_to_all x1, starting transfers between devices, local(): lax.all_to_all(outgoing, ('x', 'z'), split_axis=0, concat_axis=0, tiled=T...  11.2 us
    all_to_all x1, starting transfers between devices, local(): lax.all_to_all(rows, ('x', 'z'), split_axis=0, concat_axis=0, tiled=True)  9.79 us
    ppermute x1, waiting for transfers between devices, swap(): return lax.ppermute(value, 'y', [(i, i ^ 1) for i in range(NY)])  5.11 us
    all_to_all x1, waiting for transfers between devices, local(): lax.all_to_all(rows, ('x', 'z'), split_axis=0, concat_axis=0, tiled=True)  4.82 us
    unnamed x28, local copies, waits for them, and re-layouts  2.96 us
  transfers between devices with their start and end apart: 21, of which 9 were waited for; matrix products, arithmetic and copies ran while one was open for 1% of the time, Pallas kernels for 13%

profile of v3, /device:TPU:32, one launch (start us, length us, event | category | flops | bytes accessed | tf_op | source)
XLA Modules:
  0.0 115.3 jit_solution(11247711339342195457)
XLA Ops:
  1.8 1.8 %convolution_convert_fusion.1 = bf16[512,576]{0,1:T(8,128)(2,1)S(1)} fusion(bf16[512,768]{1,0:T(8,128)(2,1)} %param.13, bf16[768,576]{0,1:T(8,128)(2,1)S(1)} %bitcast.54), kind=kOutput, calls=%fused_computation.3 | convolution fusion | flops 453279744 | bytes 2260992 | tf_op jit(solution)/shard_map/dot_general | solution.py:28
  6.6 3.3 %collective-permute-start = (bf16[128,768]{1,0:T(8,128)(2,1)S(1)}, bf16[128,768]{1,0:T(8,128)(2,1)S(1)}, u32[]{:S(2)}, u32[]{:S(2)}) collective-permute-start(bf16[128,768]{1,0:T(8,128)(2,1)S(1)} %get-tuple-element.86), channel_id=1, source_target_pairs={{2,0},{3,1},{0,2},{1,3},{6,4},{7,5},{4,6},{5,7},{10,8},{11,9},{8,1... | collective-permute-start | bytes 589832 | tf_op jit(solution)/shard_map/ppermute | solution.py:45
  12.4 2.2 %outgoing_rows.1 = bf16[32,2,16,384]{3,2,1,0:T(8,128)(2,1)} custom-call(s32[7]{0:T(128)S(1)} %pad_add_fusion.refs_0_.place_ref, s32[1,256]{1,0:T(1,128)S(1)} %bitcast.61, s32[1024,1]{1,0:T(8,128)S(1)} %reshape.55.wanted_ref, bf16[256,768]{1,0:T(8,128)(2,1)S(1)} %copy-done.5), custom_call_target="tpu_custom_call" | custom-call | flops 2000000000 | bytes 6000000 | tf_op jit(solution)/shard_map/outgoing_rows/pallas_call | solution.py:269
  14.6 11.2 %all-to-all-start = ((bf16[32,2,16,384]{3,2,1,0:T(8,128)(2,1)}), bf16[32,2,16,384]{3,2,1,0:T(8,128)(2,1)S(1)}, u32[]{:S(2)}, u32[]{:S(2)}) async-start(bf16[32,2,16,384]{3,2,1,0:T(8,128)(2,1)} %outgoing_rows.1), calls=%async_computation | async-start | bytes 1572864 | tf_op jit(solution)/shard_map/all_to_all | solution.py:651
  27.9 2.4 %collective-permute-start.5 = (bf16[128,768]{1,0:T(8,128)(2,1)S(1)}, bf16[128,768]{1,0:T(8,128)(2,1)S(1)}, u32[]{:S(2)}, u32[]{:S(2)}) collective-permute-start(bf16[128,768]{1,0:T(8,128)(2,1)S(1)} %first_norm.1.block_ref.first_ref), channel_id=1, source_target_pairs={{3,0},{0,1},{1,2},{2,3},{7,4},{4,5},{5,6},{6,7},{11,8},{8,9},{9,10... | collective-permute-start | bytes 589832 | tf_op jit(solution)/shard_map/ppermute | solution.py:45
  31.2 1.3 %feed_first.1 = (f32[128,768]{1,0:T(8,128)S(1)}, bf16[768,768]{1,0:T(8,128)(2,1)S(1)}, bf16[768,768]{1,0:T(8,128)(2,1)S(1)}) custom-call(bf16[128,768]{1,0:T(8,128)(2,1)S(1)} %first_norm.1.block_ref.first_ref, bf16[768,768]{1,0:T(8,128)(2,1)S(1)} %copy-done.3, bf16[768,768]{1,0:T(8,128)(2,1)S(1)} %copy-done.4), custom_call_target="tpu_custom_call" | custom-call | flops 8000000000 | bytes 9000000 | tf_op jit(solution)/shard_map/feed_first/pallas_call | solution.py:141
  32.4 1.9 %link_counts.1.counts_hbm = bf16[1280,256]{1,0:T(8,128)(2,1)S(1)} custom-call(s32[7]{0:T(128)S(1)} %pad_add_fusion.refs_0_.place_ref, s32[10,256]{1,0:T(8,128)S(1)} %bitcast.60), custom_call_target="tpu_custom_call" | custom-call | flops 4000000000 | bytes 2000000 | tf_op jit(solution)/shard_map/link_counts/pallas_call | solution.py:302
  34.4 1.7 %collective-permute-done.7.block_ref = bf16[128,768]{1,0:T(8,128)(2,1)S(1)} collective-permute-done((bf16[128,768]{1,0:T(8,128)(2,1)S(1)}, bf16[128,768]{1,0:T(8,128)(2,1)S(1)}, u32[]{:S(2)}, u32[]{:S(2)}) %collective-permute-start.7) | collective-permute-done | bytes 196640 | tf_op jit(solution)/shard_map/ppermute | solution.py:45
  37.8 1.2 %collective-permute-done.5.block_ref = bf16[128,768]{1,0:T(8,128)(2,1)S(1)} collective-permute-done((bf16[128,768]{1,0:T(8,128)(2,1)S(1)}, bf16[128,768]{1,0:T(8,128)(2,1)S(1)}, u32[]{:S(2)}, u32[]{:S(2)}) %collective-permute-start.5) | collective-permute-done | bytes 196640 | tf_op jit(solution)/shard_map/ppermute | solution.py:45
  39.7 1.4 %collective-permute-start.6 = (bf16[128,768]{1,0:T(8,128)(2,1)S(1)}, bf16[128,768]{1,0:T(8,128)(2,1)S(1)}, u32[]{:S(2)}, u32[]{:S(2)}) collective-permute-start(bf16[128,768]{1,0:T(8,128)(2,1)S(1)} %feed.4), channel_id=1, source_target_pairs={{1,0},{2,1},{3,2},{0,3},{5,4},{6,5},{7,6},{4,7},{9,8},{10,9},{11,1... | collective-permute-start | bytes 589832 | tf_op jit(solution)/shard_map/ppermute | solution.py:45
  42.7 3.2 %collective-permute-done.8.across_ref = bf16[128,768]{1,0:T(8,128)(2,1)S(1)} collective-permute-done((bf16[128,768]{1,0:T(8,128)(2,1)S(1)}, bf16[128,768]{1,0:T(8,128)(2,1)S(1)}, u32[]{:S(2)}, u32[]{:S(2)}) %collective-permute-start.8) | collective-permute-done | bytes 196640 | tf_op jit(solution)/shard_map/ppermute | solution.py:45
  45.9 1.6 %collective-permute-done.6.far_ref = bf16[128,768]{1,0:T(8,128)(2,1)S(1)} collective-permute-done((bf16[128,768]{1,0:T(8,128)(2,1)S(1)}, bf16[128,768]{1,0:T(8,128)(2,1)S(1)}, u32[]{:S(2)}, u32[]{:S(2)}) %collective-permute-start.6) | collective-permute-done | bytes 196640 | tf_op jit(solution)/shard_map/ppermute | solution.py:45
  47.5 1.2 %collective-permute-done.4.near_ref = bf16[128,768]{1,0:T(8,128)(2,1)S(1)} collective-permute-done((bf16[128,768]{1,0:T(8,128)(2,1)S(1)}, bf16[128,768]{1,0:T(8,128)(2,1)S(1)}, u32[]{:S(2)}, u32[]{:S(2)}) %collective-permute-start.4) | collective-permute-done | bytes 196640 | tf_op jit(solution)/shard_map/ppermute | solution.py:45
  49.8 2.1 %collective-permute-start.11 = (bf16[1,768]{1,0:T(2,128)(2,1)S(1)}, bf16[1,768]{1,0:T(2,128)(2,1)S(1)}, u32[]{:S(2)}, u32[]{:S(2)}) collective-permute-start(bf16[1,768]{1,0:T(2,128)(2,1)S(1)} %pooled_row.1.own_ref), channel_id=1, source_target_pairs={{2,0},{3,1},{0,2},{1,3},{6,4},{7,5},{4,6},{5,7},{10,8},{11,9},{8,1... | collective-permute-start | bytes 4616 | tf_op jit(solution)/shard_map/ppermute | solution.py:45
  54.1 2.3 %halo_sums.1 = (bf16[256,384]{1,0:T(8,128)(2,1)S(1)}, bf16[2,256,256]{2,1,0:T(8,128)(2,1)S(1)}) custom-call(s32[7]{0:T(128)S(1)} %pad_add_fusion.refs_0_.place_ref, s32[1,256]{1,0:T(1,128)S(1)} %bitcast.62, bf16[1280,256]{1,0:T(8,128)(2,1)S(1)} %copy-done.10, bf16[256,768]{1,0:T(8,128)(2,1)S(1)} %copy-done.5, ...), custom_call_target="tpu_custom_call" | custom-call | flops 1000000000 | bytes 5000000 | tf_op jit(solution)/shard_map/halo_sums/pallas_call | solution.py:368
  57.2 9.8 %all-to-all-start.1 = ((bf16[32,4,768]{2,1,0:T(4,128)(2,1)}), bf16[32,4,768]{2,1,0:T(4,128)(2,1)S(1)}, u32[]{:S(2)}, u32[]{:S(2)}) async-start(bf16[32,4,768]{2,1,0:T(4,128)(2,1)} %spread_rows.1), calls=%async_computation.1 | async-start | bytes 393216 | tf_op jit(solution)/shard_map/all_to_all | solution.py:667
  68.0 5.1 %collective-permute-done.13.refs_5_ = bf16[256,384]{1,0:T(8,128)(2,1)S(1)} collective-permute-done((bf16[256,384]{1,0:T(8,128)(2,1)S(1)}, bf16[256,384]{1,0:T(8,128)(2,1)S(1)}, u32[]{:S(2)}, u32[]{:S(2)}) %collective-permute-start.13) | collective-permute-done | bytes 196640 | tf_op jit(solution)/shard_map/ppermute | solution.py:40
  73.2 4.8 %all-to-all-done.1 = bf16[32,4,768]{2,1,0:T(4,128)(2,1)S(1)} async-done(((bf16[32,4,768]{2,1,0:T(4,128)(2,1)}), bf16[32,4,768]{2,1,0:T(4,128)(2,1)S(1)}, u32[]{:S(2)}, u32[]{:S(2)}) %all-to-all-start.1) | async-done | bytes 196640 | tf_op jit(solution)/shard_map/all_to_all | solution.py:667
  78.2 2.8 %sage_head.1 = (bf16[256,768]{1,0:T(8,128)(2,1)S(1)}, f32[256,768]{1,0:T(8,128)S(1)}, bf16[2,256,128]{2,1,0:T(8,128)(2,1)S(1)}, bf16[2,256,256]{2,1,0:T(8,128)(2...) custom-call(s32[7]{0:T(128)S(1)} %pad_add_fusion.refs_0_.place_ref, ...), custom_call_target="tpu_custom_call" | custom-call | flops 3000000000 | bytes 4000000 | tf_op jit(solution)/shard_map/sage_head/pallas_call | solution.py:440
  80.9 2.2 %sage.1 = (f32[256,192]{1,0:T(8,128)S(1)}, f32[32,24,384]{2,1,0:T(8,128)S(1)}, f32[32,8,384]{2,1,0:T(8,128)S(1)}, bf16[32,16,384]{2,1,0:T(8,128)(2,1)S(1)}) custom-call(s32[7]{0:T(128)S(1)} %pad_add_fusion.refs_0_.place_ref, bf16[128,768]{1,0:T(8,128)(2,1)S(1)} %collective-permute-done.14.refs_1_, bf16[256,768]{1,0:T(8,128)(2,1)S(1)} %get-tuple-element.65.refs_2_, ...), custom_call_target="tpu_custom_call" | custom-call | flops 2000000000 | bytes 8000000 | tf_op jit(solution)/shard_map/sage/pallas_call | solution.py:519
  83.6 1.4 %sage_tail.1 = (bf16[192,256]{1,0:T(8,128)(2,1)}, f32[32,16,384]{2,1,0:T(8,128)S(1)}) custom-call(s32[7]{0:T(128)S(1)} %pad_add_fusion.refs_0_.place_ref, f32[256,192]{1,0:T(8,128)S(1)} %get-tuple-element.72.act_ref, f32[32,24,384]{2,1,0:T(8,128)S(1)} %get-tuple-element.73.weights_ref, f32[32,8,384]{2,1,0:T(8,128)S(1)} %get-tuple-element.74.terms_ref), custom_call_target="tpu_custom_call" | custom-call | flops 3000000000 | bytes 4000000 | tf_op jit(solution)/shard_map/sage_tail/pallas_call | solution.py:541
  85.1 20.2 %all_to_all.15.refs_1_.parts_ref = bf16[32,16,384]{2,1,0:T(8,128)(2,1)S(1)} all-to-all(bf16[32,16,384]{2,1,0:T(8,128)(2,1)S(1)} %combine.1), channel_id=1, replica_groups=mesh['x'=4,'z'=8,'c'=2,'y'=4] {'x','z'}, dimensions={0} | all-to-all | bytes 786432 | tf_op jit(solution)/shard_map/all_to_all | solution.py:679
  106.3 2.7 %collective-permute-start.16 = (f32[4,192]{1,0:T(4,128)S(1)}, f32[4,192]{1,0:T(4,128)S(1)}, u32[]{:S(2)}, u32[]{:S(2)}) collective-permute-start(f32[4,192]{1,0:T(4,128)S(1)} %get-tuple-element.79), channel_id=1, source_target_pairs={{2,0},{3,1},{0,2},{1,3},{6,4},{7,5},{4,6},{5,7},{10,8},{11,9},{8,1... | collective-permute-start | bytes 9224 | tf_op jit(solution)/shard_map/ppermute | solution.py:45
  112.6 2.1 %collective-permute-done.18 = f32[4,192]{1,0:T(4,128)S(1)} collective-permute-done((f32[4,192]{1,0:T(4,128)S(1)}, f32[4,192]{1,0:T(4,128)S(1)}, u32[]{:S(2)}, u32[]{:S(2)}) %collective-permute-start.18) | collective-permute-done | bytes 3104 | tf_op jit(solution)/shard_map/ppermute | solution.py:45
  (79 shorter events, 24.3 us)
Async XLA Ops:
  6.6 20.1 %collective-permute-start = (bf16[128,768]{1,0:T(8,128)(2,1)S(1)}, bf16[128,768]{1,0:T(8,128)(2,1)S(1)}, u32[]{:S(2)}, u32[]{:S(2)}) collective-permute-start(bf16[128,768]{1,0:T(8,128)(2,1)S(1)} %get-tuple-element.86), channel_id=1, source_target_pairs={{2,0},{3,1},{0,2},{1,3},{6,4},{7,5},{4,6},{5,7},{10,8},{11,9},{8,1... | collective-permute-start | bytes 589832 | tf_op jit(solution)/shard_map/ppermute | solution.py:45
  9.9 16.9 %collective-permute-start.1 = (bf16[128,768]{1,0:T(8,128)(2,1)S(1)}, bf16[128,768]{1,0:T(8,128)(2,1)S(1)}, u32[]{:S(2)}, u32[]{:S(2)}) collective-permute-start(bf16[128,768]{1,0:T(8,128)(2,1)S(1)} %get-tuple-element.85), channel_id=1, source_target_pairs={{1,0},{2,1},{3,2},{0,3},{5,4},{6,5},{7,6},{4,7},{9,8},{10,9},{11,1... | collective-permute-start | bytes 589832 | tf_op jit(solution)/shard_map/ppermute | solution.py:45
  11.0 15.8 %collective-permute-start.2 = (bf16[128,768]{1,0:T(8,128)(2,1)S(1)}, bf16[128,768]{1,0:T(8,128)(2,1)S(1)}, u32[]{:S(2)}, u32[]{:S(2)}) collective-permute-start(bf16[128,768]{1,0:T(8,128)(2,1)S(1)} %get-tuple-element.84), channel_id=1, source_target_pairs={{3,0},{0,1},{1,2},{2,3},{7,4},{4,5},{5,6},{6,7},{11,8},{8,9},{9,10... | collective-permute-start | bytes 589832 | tf_op jit(solution)/shard_map/ppermute | solution.py:45
  14.6 35.0 %all-to-all-start = ((bf16[32,2,16,384]{3,2,1,0:T(8,128)(2,1)}), bf16[32,2,16,384]{3,2,1,0:T(8,128)(2,1)S(1)}, u32[]{:S(2)}, u32[]{:S(2)}) async-start(bf16[32,2,16,384]{3,2,1,0:T(8,128)(2,1)} %outgoing_rows.1), calls=%async_computation | async-start | bytes 1572864 | tf_op jit(solution)/shard_map/all_to_all | solution.py:651
  27.1 9.0 %collective-permute-start.7 = (bf16[128,768]{1,0:T(8,128)(2,1)S(1)}, bf16[128,768]{1,0:T(8,128)(2,1)S(1)}, u32[]{:S(2)}, u32[]{:S(2)}) collective-permute-start(bf16[128,768]{1,0:T(8,128)(2,1)S(1)} %first_norm.1.block_ref.first_ref), channel_id=1, source_target_pairs={{2,0},{3,1},{0,2},{1,3},{6,4},{7,5},{4,6},{5,7},{10,8},{11,9},{8,1... | collective-permute-start | bytes 589832 | tf_op jit(solution)/shard_map/ppermute | solution.py:45
  27.9 11.1 %collective-permute-start.5 = (bf16[128,768]{1,0:T(8,128)(2,1)S(1)}, bf16[128,768]{1,0:T(8,128)(2,1)S(1)}, u32[]{:S(2)}, u32[]{:S(2)}) collective-permute-start(bf16[128,768]{1,0:T(8,128)(2,1)S(1)} %first_norm.1.block_ref.first_ref), channel_id=1, source_target_pairs={{3,0},{0,1},{1,2},{2,3},{7,4},{4,5},{5,6},{6,7},{11,8},{8,9},{9,10... | collective-permute-start | bytes 589832 | tf_op jit(solution)/shard_map/ppermute | solution.py:45
  30.3 10.8 %collective-permute-start.3 = (bf16[128,768]{1,0:T(8,128)(2,1)S(1)}, bf16[128,768]{1,0:T(8,128)(2,1)S(1)}, u32[]{:S(2)}, u32[]{:S(2)}) collective-permute-start(bf16[128,768]{1,0:T(8,128)(2,1)S(1)} %first_norm.1.block_ref.first_ref), channel_id=1, source_target_pairs={{1,0},{2,1},{3,2},{0,3},{5,4},{6,5},{7,6},{4,7},{9,8},{10,9},{11,1... | collective-permute-start | bytes 589832 | tf_op jit(solution)/shard_map/ppermute | solution.py:45
  36.8 9.1 %collective-permute-start.8 = (bf16[128,768]{1,0:T(8,128)(2,1)S(1)}, bf16[128,768]{1,0:T(8,128)(2,1)S(1)}, u32[]{:S(2)}, u32[]{:S(2)}) collective-permute-start(bf16[128,768]{1,0:T(8,128)(2,1)S(1)} %feed.5), channel_id=1, source_target_pairs={{2,0},{3,1},{0,2},{1,3},{6,4},{7,5},{4,6},{5,7},{10,8},{11,9},{8,1... | collective-permute-start | bytes 589832 | tf_op jit(solution)/shard_map/ppermute | solution.py:45
  39.7 7.8 %collective-permute-start.6 = (bf16[128,768]{1,0:T(8,128)(2,1)S(1)}, bf16[128,768]{1,0:T(8,128)(2,1)S(1)}, u32[]{:S(2)}, u32[]{:S(2)}) collective-permute-start(bf16[128,768]{1,0:T(8,128)(2,1)S(1)} %feed.4), channel_id=1, source_target_pairs={{1,0},{2,1},{3,2},{0,3},{5,4},{6,5},{7,6},{4,7},{9,8},{10,9},{11,1... | collective-permute-start | bytes 589832 | tf_op jit(solution)/shard_map/ppermute | solution.py:45
  41.7 7.0 %collective-permute-start.4 = (bf16[128,768]{1,0:T(8,128)(2,1)S(1)}, bf16[128,768]{1,0:T(8,128)(2,1)S(1)}, u32[]{:S(2)}, u32[]{:S(2)}) collective-permute-start(bf16[128,768]{1,0:T(8,128)(2,1)S(1)} %feed.3), channel_id=1, source_target_pairs={{3,0},{0,1},{1,2},{2,3},{7,4},{4,5},{5,6},{6,7},{11,8},{8,9},{9,10... | collective-permute-start | bytes 589832 | tf_op jit(solution)/shard_map/ppermute | solution.py:45
  49.5 28.6 %copy-start.1 = (bf16[768,192]{0,1:T(8,128)(2,1)S(1)}, bf16[768,192]{0,1:T(8,128)(2,1)}, u32[]{:S(2)}) copy-start(bf16[768,192]{0,1:T(8,128)(2,1)} %param.23) | copy-start | bytes 884740
  49.6 28.6 %copy-start.2 = (bf16[768,192]{0,1:T(8,128)(2,1)S(1)}, bf16[768,192]{0,1:T(8,128)(2,1)}, u32[]{:S(2)}) copy-start(bf16[768,192]{0,1:T(8,128)(2,1)} %param.24) | copy-start | bytes 884740
  49.6 28.6 %copy-start.6 = (bf16[256,192]{0,1:T(8,128)(2,1)S(1)}, bf16[256,192]{0,1:T(8,128)(2,1)}, u32[]{:S(2)}) copy-start(bf16[256,192]{0,1:T(8,128)(2,1)} %param.25) | copy-start | bytes 294916
  49.6 3.4 %collective-permute-start.12 = (bf16[32,2,16,384]{3,2,1,0:T(8,128)(2,1)S(1)}, bf16[32,2,16,384]{3,2,1,0:T(8,128)(2,1)S(1)}, u32[]{:S(2)}, u32[]{:S(2)}) collective-permute-start(bf16[32,2,16,384]{3,2,1,0:T(8,128)(2,1)S(1)} %all-to-all-done.received_hbm), channel_id=1, source_target_pairs={{4,0},{0,4},{5,1},{1,5},{6,2},{2,6},{7,3},{3,7},{12,8},{8,12},{13,... | collective-permute-start | bytes 2359304 | tf_op jit(solution)/shard_map/ppermute | solution.py:45
  49.7 6.7 %collective-permute-start.10 = (bf16[1,768]{1,0:T(2,128)(2,1)S(1)}, bf16[1,768]{1,0:T(2,128)(2,1)S(1)}, u32[]{:S(2)}, u32[]{:S(2)}) collective-permute-start(bf16[1,768]{1,0:T(2,128)(2,1)S(1)} %pooled_row.1.own_ref), channel_id=1, source_target_pairs={{3,0},{0,1},{1,2},{2,3},{7,4},{4,5},{5,6},{6,7},{11,8},{8,9},{9,10... | collective-permute-start | bytes 4616 | tf_op jit(solution)/shard_map/ppermute | solution.py:45
  49.8 6.7 %collective-permute-start.11 = (bf16[1,768]{1,0:T(2,128)(2,1)S(1)}, bf16[1,768]{1,0:T(2,128)(2,1)S(1)}, u32[]{:S(2)}, u32[]{:S(2)}) collective-permute-start(bf16[1,768]{1,0:T(2,128)(2,1)S(1)} %pooled_row.1.own_ref), channel_id=1, source_target_pairs={{2,0},{3,1},{0,2},{1,3},{6,4},{7,5},{4,6},{5,7},{10,8},{11,9},{8,1... | collective-permute-start | bytes 4616 | tf_op jit(solution)/shard_map/ppermute | solution.py:45
  51.9 4.6 %collective-permute-start.9 = (bf16[1,768]{1,0:T(2,128)(2,1)S(1)}, bf16[1,768]{1,0:T(2,128)(2,1)S(1)}, u32[]{:S(2)}, u32[]{:S(2)}) collective-permute-start(bf16[1,768]{1,0:T(2,128)(2,1)S(1)} %pooled_row.1.own_ref), channel_id=1, source_target_pairs={{1,0},{2,1},{3,2},{0,3},{5,4},{6,5},{7,6},{4,7},{9,8},{10,9},{11,1... | collective-permute-start | bytes 4616 | tf_op jit(solution)/shard_map/ppermute | solution.py:45
  57.2 20.8 %all-to-all-start.1 = ((bf16[32,4,768]{2,1,0:T(4,128)(2,1)}), bf16[32,4,768]{2,1,0:T(4,128)(2,1)S(1)}, u32[]{:S(2)}, u32[]{:S(2)}) async-start(bf16[32,4,768]{2,1,0:T(4,128)(2,1)} %spread_rows.1), calls=%async_computation.1 | async-start | bytes 393216 | tf_op jit(solution)/shard_map/all_to_all | solution.py:667
  67.0 6.2 %collective-permute-start.13 = (bf16[256,384]{1,0:T(8,128)(2,1)S(1)}, bf16[256,384]{1,0:T(8,128)(2,1)S(1)}, u32[]{:S(2)}, u32[]{:S(2)}) collective-permute-start(bf16[256,384]{1,0:T(8,128)(2,1)S(1)} %get-tuple-element.63.refs_4_), channel_id=1, source_target_pairs={{0,1},{1,0},{2,3},{3,2},{4,5},{5,4},{6,7},{7,6},{8,9},{9,8},{10,11... | collective-permute-start | bytes 589832 | tf_op jit(solution)/shard_map/ppermute | solution.py:40
  78.0 2.9 %collective-permute-start.14 = (bf16[128,768]{1,0:T(8,128)(2,1)S(1)}, bf16[128,768]{1,0:T(8,128)(2,1)S(1)}, u32[]{:S(2)}, u32[]{:S(2)}) collective-permute-start(bf16[128,768]{1,0:T(8,128)(2,1)S(1)} %reshape.54.refs_1_), channel_id=1, source_target_pairs={{4,0},{0,4},{5,1},{1,5},{6,2},{2,6},{7,3},{3,7},{12,8},{8,12},{13,... | collective-permute-start | bytes 589832 | tf_op jit(solution)/shard_map/ppermute | solution.py:45
  83.1 1.9 %collective-permute-start.15 = (bf16[32,16,384]{2,1,0:T(8,128)(2,1)S(1)}, bf16[32,16,384]{2,1,0:T(8,128)(2,1)S(1)}, u32[]{:S(2)}, u32[]{:S(2)}) collective-permute-start(bf16[32,16,384]{2,1,0:T(8,128)(2,1)S(1)} %get-tuple-element.77), channel_id=1, source_target_pairs={{4,0},{0,4},{5,1},{1,5},{6,2},{2,6},{7,3},{3,7},{12,8},{8,12},{13,... | collective-permute-start | bytes 1179656 | tf_op jit(solution)/shard_map/ppermute | solution.py:45
  106.3 5.5 %collective-permute-start.16 = (f32[4,192]{1,0:T(4,128)S(1)}, f32[4,192]{1,0:T(4,128)S(1)}, u32[]{:S(2)}, u32[]{:S(2)}) collective-permute-start(f32[4,192]{1,0:T(4,128)S(1)} %get-tuple-element.79), channel_id=1, source_target_pairs={{2,0},{3,1},{0,2},{1,3},{6,4},{7,5},{4,6},{5,7},{10,8},{11,9},{8,1... | collective-permute-start | bytes 9224 | tf_op jit(solution)/shard_map/ppermute | solution.py:45
  109.0 3.6 %collective-permute-start.17 = (f32[4,192]{1,0:T(4,128)S(1)}, f32[4,192]{1,0:T(4,128)S(1)}, u32[]{:S(2)}, u32[]{:S(2)}) collective-permute-start(f32[4,192]{1,0:T(4,128)S(1)} %get-tuple-element.80), channel_id=1, source_target_pairs={{1,0},{2,1},{3,2},{0,3},{5,4},{6,5},{7,6},{4,7},{9,8},{10,9},{11,1... | collective-permute-start | bytes 9224 | tf_op jit(solution)/shard_map/ppermute | solution.py:45
  109.9 4.8 %collective-permute-start.18 = (f32[4,192]{1,0:T(4,128)S(1)}, f32[4,192]{1,0:T(4,128)S(1)}, u32[]{:S(2)}, u32[]{:S(2)}) collective-permute-start(f32[4,192]{1,0:T(4,128)S(1)} %get-tuple-element.81), channel_id=1, source_target_pairs={{3,0},{0,1},{1,2},{2,3},{7,4},{4,5},{5,6},{6,7},{11,8},{8,9},{9,10... | collective-permute-start | bytes 9224 | tf_op jit(solution)/shard_map/ppermute | solution.py:45
  (11 other events, 37.9 us)

commit v4 on v3

--- a/solution.py
+++ b/solution.py
@@ -231,9 +231,8 @@
 
 
 def outgoing_kernel(
-    place_ref, target_ref, wanted_ref, hist_hbm, out_hbm, hist_ref, semaphores, rows_ref, out_sems
+    place_ref, target_ref, wanted_ref, hist_ref, out_hbm, rows_ref, out_sems
 ):
-    copies = fetch((hist_hbm,), (hist_ref,), semaphores)
     count, width = hist_ref.shape[0], rows_ref.shape[3]
     _, row_text = text_rows(target_ref[...], count, place_ref[DOM])
     column = lax.broadcasted_iota(jnp.int32, (count, width), 1)
@@ -244,7 +243,6 @@
     chips = rows_ref.shape[0] // parts
     size = wanted_ref.shape[0] // parts
     ids = lax.broadcasted_iota(jnp.int32, (size, count), 1)
-    copies[0].wait()
     hist = sliced(hist_ref[...].astype(F32), place_ref[ME] % 2, width)
     coded = jnp.where(row_text >= 0, code, hist).astype(BF)
     sent = []
@@ -269,10 +267,9 @@
     return pl.pallas_call(
         outgoing_kernel,
         out_shape=jax.ShapeDtypeStruct(shape, BF),
-        in_specs=scalars() + whole(2) + far_off(1),
+        in_specs=scalars() + whole(3),
         out_specs=far_off(1)[0],
-        scratch_shapes=room(hist)
-        + [pltpu.VMEM(shape, BF), pltpu.SemaphoreType.DMA((parts,))],
+        scratch_shapes=[pltpu.VMEM(shape, BF), pltpu.SemaphoreType.DMA((parts,))],
         name="outgoing_rows",
         **grant(52, 2000000000, 6000000),
     )(place, target, wanted, hist)

time: 116 us -> 116 us (level)
  no operation moved by 1% of the time
where the time goes in v4:
time: 116 us; the launch traced here: 115 us
  starting transfers between devices  43.6 us (38%)
  waiting for transfers between devices  21.8 us (19%)
  blocking collectives  20.2 us (17%)
  Pallas kernels  19.3 us (17%)
  local copies, waits for them, and re-layouts  4.91 us (4%)
  matrix products  3.34 us (3%)
    ppermute x18, starting transfers between devices, pull(): lax.ppermute(value, axis, [((i + shift) % count, i) for i in range(count)])  21.5 us
    all_to_all x1, blocking collectives, local(): lax.all_to_all(parts, ('x', 'z'), split_axis=0, concat_axis=0, tiled=True)  20.2 us
    ppermute x18, waiting for transfers between devices, pull(): lax.ppermute(value, axis, [((i + shift) % count, i) for i in range(count)])  11.9 us
    all_to_all x1, starting transfers between devices, local(): lax.all_to_all(outgoing, ('x', 'z'), split_axis=0, concat_axis=0, tiled=T...  11.2 us
    all_to_all x1, starting transfers between devices, local(): lax.all_to_all(rows, ('x', 'z'), split_axis=0, concat_axis=0, tiled=True)  9.79 us
    ppermute x1, waiting for transfers between devices, swap(): return lax.ppermute(value, 'y', [(i, i ^ 1) for i in range(NY)])  5.1 us
    all_to_all x1, waiting for transfers between devices, local(): lax.all_to_all(rows, ('x', 'z'), split_axis=0, concat_axis=0, tiled=True)  4.82 us
    unnamed x28, local copies, waits for them, and re-layouts  2.96 us
  transfers between devices with their start and end apart: 21, of which 9 were waited for; matrix products, arithmetic and copies ran while one was open for 1% of the time, Pallas kernels for 13%

profile of v4, /device:TPU:32, one launch (start us, length us, event | category | flops | bytes accessed | tf_op | source)
XLA Modules:
  0.0 115.1 jit_solution(14281979417048822783)
XLA Ops:
  1.8 1.8 %convolution_convert_fusion.1 = bf16[512,576]{0,1:T(8,128)(2,1)S(1)} fusion(bf16[512,768]{1,0:T(8,128)(2,1)} %param.13, bf16[768,576]{0,1:T(8,128)(2,1)S(1)} %bitcast.54), kind=kOutput, calls=%fused_computation.3 | convolution fusion | flops 453279744 | bytes 2260992 | tf_op jit(solution)/shard_map/dot_general | solution.py:28
  6.6 3.3 %collective-permute-start = (bf16[128,768]{1,0:T(8,128)(2,1)S(1)}, bf16[128,768]{1,0:T(8,128)(2,1)S(1)}, u32[]{:S(2)}, u32[]{:S(2)}) collective-permute-start(bf16[128,768]{1,0:T(8,128)(2,1)S(1)} %get-tuple-element.86), channel_id=1, source_target_pairs={{2,0},{3,1},{0,2},{1,3},{6,4},{7,5},{4,6},{5,7},{10,8},{11,9},{8,1... | collective-permute-start | bytes 589832 | tf_op jit(solution)/shard_map/ppermute | solution.py:45
  12.4 2.0 %outgoing_rows.1 = bf16[32,2,16,384]{3,2,1,0:T(8,128)(2,1)} custom-call(s32[7]{0:T(128)S(1)} %pad_add_fusion.refs_0_.place_ref, s32[1,256]{1,0:T(1,128)S(1)} %bitcast.61, s32[1024,1]{1,0:T(8,128)S(1)} %reshape.55.wanted_ref, bf16[256,768]{1,0:T(8,128)(2,1)S(1)} %copy-done.5), custom_call_target="tpu_custom_call" | custom-call | flops 2000000000 | bytes 6000000 | tf_op jit(solution)/shard_map/outgoing_rows/pallas_call | solution.py:267
  14.4 11.2 %all-to-all-start = ((bf16[32,2,16,384]{3,2,1,0:T(8,128)(2,1)}), bf16[32,2,16,384]{3,2,1,0:T(8,128)(2,1)S(1)}, u32[]{:S(2)}, u32[]{:S(2)}) async-start(bf16[32,2,16,384]{3,2,1,0:T(8,128)(2,1)} %outgoing_rows.1), calls=%async_computation | async-start | bytes 1572864 | tf_op jit(solution)/shard_map/all_to_all | solution.py:648
  27.7 2.4 %collective-permute-start.5 = (bf16[128,768]{1,0:T(8,128)(2,1)S(1)}, bf16[128,768]{1,0:T(8,128)(2,1)S(1)}, u32[]{:S(2)}, u32[]{:S(2)}) collective-permute-start(bf16[128,768]{1,0:T(8,128)(2,1)S(1)} %first_norm.1.block_ref.first_ref), channel_id=1, source_target_pairs={{3,0},{0,1},{1,2},{2,3},{7,4},{4,5},{5,6},{6,7},{11,8},{8,9},{9,10... | collective-permute-start | bytes 589832 | tf_op jit(solution)/shard_map/ppermute | solution.py:45
  31.0 1.3 %feed_first.1 = (f32[128,768]{1,0:T(8,128)S(1)}, bf16[768,768]{1,0:T(8,128)(2,1)S(1)}, bf16[768,768]{1,0:T(8,128)(2,1)S(1)}) custom-call(bf16[128,768]{1,0:T(8,128)(2,1)S(1)} %first_norm.1.block_ref.first_ref, bf16[768,768]{1,0:T(8,128)(2,1)S(1)} %copy-done.3, bf16[768,768]{1,0:T(8,128)(2,1)S(1)} %copy-done.4), custom_call_target="tpu_custom_call" | custom-call | flops 8000000000 | bytes 9000000 | tf_op jit(solution)/shard_map/feed_first/pallas_call | solution.py:141
  32.3 1.9 %link_counts.1.counts_hbm = bf16[1280,256]{1,0:T(8,128)(2,1)S(1)} custom-call(s32[7]{0:T(128)S(1)} %pad_add_fusion.refs_0_.place_ref, s32[10,256]{1,0:T(8,128)S(1)} %bitcast.60), custom_call_target="tpu_custom_call" | custom-call | flops 4000000000 | bytes 2000000 | tf_op jit(solution)/shard_map/link_counts/pallas_call | solution.py:299
  34.2 1.7 %collective-permute-done.7.block_ref = bf16[128,768]{1,0:T(8,128)(2,1)S(1)} collective-permute-done((bf16[128,768]{1,0:T(8,128)(2,1)S(1)}, bf16[128,768]{1,0:T(8,128)(2,1)S(1)}, u32[]{:S(2)}, u32[]{:S(2)}) %collective-permute-start.7) | collective-permute-done | bytes 196640 | tf_op jit(solution)/shard_map/ppermute | solution.py:45
  37.6 1.2 %collective-permute-done.5.block_ref = bf16[128,768]{1,0:T(8,128)(2,1)S(1)} collective-permute-done((bf16[128,768]{1,0:T(8,128)(2,1)S(1)}, bf16[128,768]{1,0:T(8,128)(2,1)S(1)}, u32[]{:S(2)}, u32[]{:S(2)}) %collective-permute-start.5) | collective-permute-done | bytes 196640 | tf_op jit(solution)/shard_map/ppermute | solution.py:45
  39.5 1.4 %collective-permute-start.6 = (bf16[128,768]{1,0:T(8,128)(2,1)S(1)}, bf16[128,768]{1,0:T(8,128)(2,1)S(1)}, u32[]{:S(2)}, u32[]{:S(2)}) collective-permute-start(bf16[128,768]{1,0:T(8,128)(2,1)S(1)} %feed.4), channel_id=1, source_target_pairs={{1,0},{2,1},{3,2},{0,3},{5,4},{6,5},{7,6},{4,7},{9,8},{10,9},{11,1... | collective-permute-start | bytes 589832 | tf_op jit(solution)/shard_map/ppermute | solution.py:45
  42.5 3.2 %collective-permute-done.8.across_ref = bf16[128,768]{1,0:T(8,128)(2,1)S(1)} collective-permute-done((bf16[128,768]{1,0:T(8,128)(2,1)S(1)}, bf16[128,768]{1,0:T(8,128)(2,1)S(1)}, u32[]{:S(2)}, u32[]{:S(2)}) %collective-permute-start.8) | collective-permute-done | bytes 196640 | tf_op jit(solution)/shard_map/ppermute | solution.py:45
  45.7 1.6 %collective-permute-done.6.far_ref = bf16[128,768]{1,0:T(8,128)(2,1)S(1)} collective-permute-done((bf16[128,768]{1,0:T(8,128)(2,1)S(1)}, bf16[128,768]{1,0:T(8,128)(2,1)S(1)}, u32[]{:S(2)}, u32[]{:S(2)}) %collective-permute-start.6) | collective-permute-done | bytes 196640 | tf_op jit(solution)/shard_map/ppermute | solution.py:45
  47.3 1.2 %collective-permute-done.4.near_ref = bf16[128,768]{1,0:T(8,128)(2,1)S(1)} collective-permute-done((bf16[128,768]{1,0:T(8,128)(2,1)S(1)}, bf16[128,768]{1,0:T(8,128)(2,1)S(1)}, u32[]{:S(2)}, u32[]{:S(2)}) %collective-permute-start.4) | collective-permute-done | bytes 196640 | tf_op jit(solution)/shard_map/ppermute | solution.py:45
  49.6 2.1 %collective-permute-start.11 = (bf16[1,768]{1,0:T(2,128)(2,1)S(1)}, bf16[1,768]{1,0:T(2,128)(2,1)S(1)}, u32[]{:S(2)}, u32[]{:S(2)}) collective-permute-start(bf16[1,768]{1,0:T(2,128)(2,1)S(1)} %pooled_row.1.own_ref), channel_id=1, source_target_pairs={{2,0},{3,1},{0,2},{1,3},{6,4},{7,5},{4,6},{5,7},{10,8},{11,9},{8,1... | collective-permute-start | bytes 4616 | tf_op jit(solution)/shard_map/ppermute | solution.py:45
  53.9 2.3 %halo_sums.1 = (bf16[256,384]{1,0:T(8,128)(2,1)S(1)}, bf16[2,256,256]{2,1,0:T(8,128)(2,1)S(1)}) custom-call(s32[7]{0:T(128)S(1)} %pad_add_fusion.refs_0_.place_ref, s32[1,256]{1,0:T(1,128)S(1)} %bitcast.62, bf16[1280,256]{1,0:T(8,128)(2,1)S(1)} %copy-done.10, bf16[256,768]{1,0:T(8,128)(2,1)S(1)} %copy-done.5, ...), custom_call_target="tpu_custom_call" | custom-call | flops 1000000000 | bytes 5000000 | tf_op jit(solution)/shard_map/halo_sums/pallas_call | solution.py:365
  57.0 9.8 %all-to-all-start.1 = ((bf16[32,4,768]{2,1,0:T(4,128)(2,1)}), bf16[32,4,768]{2,1,0:T(4,128)(2,1)S(1)}, u32[]{:S(2)}, u32[]{:S(2)}) async-start(bf16[32,4,768]{2,1,0:T(4,128)(2,1)} %spread_rows.1), calls=%async_computation.1 | async-start | bytes 393216 | tf_op jit(solution)/shard_map/all_to_all | solution.py:664
  67.9 5.1 %collective-permute-done.13.refs_5_ = bf16[256,384]{1,0:T(8,128)(2,1)S(1)} collective-permute-done((bf16[256,384]{1,0:T(8,128)(2,1)S(1)}, bf16[256,384]{1,0:T(8,128)(2,1)S(1)}, u32[]{:S(2)}, u32[]{:S(2)}) %collective-permute-start.13) | collective-permute-done | bytes 196640 | tf_op jit(solution)/shard_map/ppermute | solution.py:40
  73.0 4.8 %all-to-all-done.1 = bf16[32,4,768]{2,1,0:T(4,128)(2,1)S(1)} async-done(((bf16[32,4,768]{2,1,0:T(4,128)(2,1)}), bf16[32,4,768]{2,1,0:T(4,128)(2,1)S(1)}, u32[]{:S(2)}, u32[]{:S(2)}) %all-to-all-start.1) | async-done | bytes 196640 | tf_op jit(solution)/shard_map/all_to_all | solution.py:664
  78.0 2.8 %sage_head.1 = (bf16[256,768]{1,0:T(8,128)(2,1)S(1)}, f32[256,768]{1,0:T(8,128)S(1)}, bf16[2,256,128]{2,1,0:T(8,128)(2,1)S(1)}, bf16[2,256,256]{2,1,0:T(8,128)(2...) custom-call(s32[7]{0:T(128)S(1)} %pad_add_fusion.refs_0_.place_ref, ...), custom_call_target="tpu_custom_call" | custom-call | flops 3000000000 | bytes 4000000 | tf_op jit(solution)/shard_map/sage_head/pallas_call | solution.py:437
  80.7 2.2 %sage.1 = (f32[256,192]{1,0:T(8,128)S(1)}, f32[32,24,384]{2,1,0:T(8,128)S(1)}, f32[32,8,384]{2,1,0:T(8,128)S(1)}, bf16[32,16,384]{2,1,0:T(8,128)(2,1)S(1)}) custom-call(s32[7]{0:T(128)S(1)} %pad_add_fusion.refs_0_.place_ref, bf16[128,768]{1,0:T(8,128)(2,1)S(1)} %collective-permute-done.14.refs_1_, bf16[256,768]{1,0:T(8,128)(2,1)S(1)} %get-tuple-element.65.refs_2_, ...), custom_call_target="tpu_custom_call" | custom-call | flops 2000000000 | bytes 8000000 | tf_op jit(solution)/shard_map/sage/pallas_call | solution.py:516
  83.4 1.4 %sage_tail.1 = (bf16[192,256]{1,0:T(8,128)(2,1)}, f32[32,16,384]{2,1,0:T(8,128)S(1)}) custom-call(s32[7]{0:T(128)S(1)} %pad_add_fusion.refs_0_.place_ref, f32[256,192]{1,0:T(8,128)S(1)} %get-tuple-element.72.act_ref, f32[32,24,384]{2,1,0:T(8,128)S(1)} %get-tuple-element.73.weights_ref, f32[32,8,384]{2,1,0:T(8,128)S(1)} %get-tuple-element.74.terms_ref), custom_call_target="tpu_custom_call" | custom-call | flops 3000000000 | bytes 4000000 | tf_op jit(solution)/shard_map/sage_tail/pallas_call | solution.py:538
  84.9 20.2 %all_to_all.15.refs_1_.parts_ref = bf16[32,16,384]{2,1,0:T(8,128)(2,1)S(1)} all-to-all(bf16[32,16,384]{2,1,0:T(8,128)(2,1)S(1)} %combine.1), channel_id=1, replica_groups=mesh['x'=4,'z'=8,'c'=2,'y'=4] {'x','z'}, dimensions={0} | all-to-all | bytes 786432 | tf_op jit(solution)/shard_map/all_to_all | solution.py:676
  106.1 2.7 %collective-permute-start.16 = (f32[4,192]{1,0:T(4,128)S(1)}, f32[4,192]{1,0:T(4,128)S(1)}, u32[]{:S(2)}, u32[]{:S(2)}) collective-permute-start(f32[4,192]{1,0:T(4,128)S(1)} %get-tuple-element.79), channel_id=1, source_target_pairs={{2,0},{3,1},{0,2},{1,3},{6,4},{7,5},{4,6},{5,7},{10,8},{11,9},{8,1... | collective-permute-start | bytes 9224 | tf_op jit(solution)/shard_map/ppermute | solution.py:45
  112.4 2.1 %collective-permute-done.18 = f32[4,192]{1,0:T(4,128)S(1)} collective-permute-done((f32[4,192]{1,0:T(4,128)S(1)}, f32[4,192]{1,0:T(4,128)S(1)}, u32[]{:S(2)}, u32[]{:S(2)}) %collective-permute-start.18) | collective-permute-done | bytes 3104 | tf_op jit(solution)/shard_map/ppermute | solution.py:45
  (79 shorter events, 24.3 us)
Async XLA Ops:
  6.6 19.9 %collective-permute-start = (bf16[128,768]{1,0:T(8,128)(2,1)S(1)}, bf16[128,768]{1,0:T(8,128)(2,1)S(1)}, u32[]{:S(2)}, u32[]{:S(2)}) collective-permute-start(bf16[128,768]{1,0:T(8,128)(2,1)S(1)} %get-tuple-element.86), channel_id=1, source_target_pairs={{2,0},{3,1},{0,2},{1,3},{6,4},{7,5},{4,6},{5,7},{10,8},{11,9},{8,1... | collective-permute-start | bytes 589832 | tf_op jit(solution)/shard_map/ppermute | solution.py:45
  9.9 16.7 %collective-permute-start.1 = (bf16[128,768]{1,0:T(8,128)(2,1)S(1)}, bf16[128,768]{1,0:T(8,128)(2,1)S(1)}, u32[]{:S(2)}, u32[]{:S(2)}) collective-permute-start(bf16[128,768]{1,0:T(8,128)(2,1)S(1)} %get-tuple-element.85), channel_id=1, source_target_pairs={{1,0},{2,1},{3,2},{0,3},{5,4},{6,5},{7,6},{4,7},{9,8},{10,9},{11,1... | collective-permute-start | bytes 589832 | tf_op jit(solution)/shard_map/ppermute | solution.py:45
  11.0 15.6 %collective-permute-start.2 = (bf16[128,768]{1,0:T(8,128)(2,1)S(1)}, bf16[128,768]{1,0:T(8,128)(2,1)S(1)}, u32[]{:S(2)}, u32[]{:S(2)}) collective-permute-start(bf16[128,768]{1,0:T(8,128)(2,1)S(1)} %get-tuple-element.84), channel_id=1, source_target_pairs={{3,0},{0,1},{1,2},{2,3},{7,4},{4,5},{5,6},{6,7},{11,8},{8,9},{9,10... | collective-permute-start | bytes 589832 | tf_op jit(solution)/shard_map/ppermute | solution.py:45
  14.4 35.0 %all-to-all-start = ((bf16[32,2,16,384]{3,2,1,0:T(8,128)(2,1)}), bf16[32,2,16,384]{3,2,1,0:T(8,128)(2,1)S(1)}, u32[]{:S(2)}, u32[]{:S(2)}) async-start(bf16[32,2,16,384]{3,2,1,0:T(8,128)(2,1)} %outgoing_rows.1), calls=%async_computation | async-start | bytes 1572864 | tf_op jit(solution)/shard_map/all_to_all | solution.py:648
  26.9 9.0 %collective-permute-start.7 = (bf16[128,768]{1,0:T(8,128)(2,1)S(1)}, bf16[128,768]{1,0:T(8,128)(2,1)S(1)}, u32[]{:S(2)}, u32[]{:S(2)}) collective-permute-start(bf16[128,768]{1,0:T(8,128)(2,1)S(1)} %first_norm.1.block_ref.first_ref), channel_id=1, source_target_pairs={{2,0},{3,1},{0,2},{1,3},{6,4},{7,5},{4,6},{5,7},{10,8},{11,9},{8,1... | collective-permute-start | bytes 589832 | tf_op jit(solution)/shard_map/ppermute | solution.py:45
  27.7 11.1 %collective-permute-start.5 = (bf16[128,768]{1,0:T(8,128)(2,1)S(1)}, bf16[128,768]{1,0:T(8,128)(2,1)S(1)}, u32[]{:S(2)}, u32[]{:S(2)}) collective-permute-start(bf16[128,768]{1,0:T(8,128)(2,1)S(1)} %first_norm.1.block_ref.first_ref), channel_id=1, source_target_pairs={{3,0},{0,1},{1,2},{2,3},{7,4},{4,5},{5,6},{6,7},{11,8},{8,9},{9,10... | collective-permute-start | bytes 589832 | tf_op jit(solution)/shard_map/ppermute | solution.py:45
  30.1 10.8 %collective-permute-start.3 = (bf16[128,768]{1,0:T(8,128)(2,1)S(1)}, bf16[128,768]{1,0:T(8,128)(2,1)S(1)}, u32[]{:S(2)}, u32[]{:S(2)}) collective-permute-start(bf16[128,768]{1,0:T(8,128)(2,1)S(1)} %first_norm.1.block_ref.first_ref), channel_id=1, source_target_pairs={{1,0},{2,1},{3,2},{0,3},{5,4},{6,5},{7,6},{4,7},{9,8},{10,9},{11,1... | collective-permute-start | bytes 589832 | tf_op jit(solution)/shard_map/ppermute | solution.py:45
  36.6 9.1 %collective-permute-start.8 = (bf16[128,768]{1,0:T(8,128)(2,1)S(1)}, bf16[128,768]{1,0:T(8,128)(2,1)S(1)}, u32[]{:S(2)}, u32[]{:S(2)}) collective-permute-start(bf16[128,768]{1,0:T(8,128)(2,1)S(1)} %feed.5), channel_id=1, source_target_pairs={{2,0},{3,1},{0,2},{1,3},{6,4},{7,5},{4,6},{5,7},{10,8},{11,9},{8,1... | collective-permute-start | bytes 589832 | tf_op jit(solution)/shard_map/ppermute | solution.py:45
  39.5 7.8 %collective-permute-start.6 = (bf16[128,768]{1,0:T(8,128)(2,1)S(1)}, bf16[128,768]{1,0:T(8,128)(2,1)S(1)}, u32[]{:S(2)}, u32[]{:S(2)}) collective-permute-start(bf16[128,768]{1,0:T(8,128)(2,1)S(1)} %feed.4), channel_id=1, source_target_pairs={{1,0},{2,1},{3,2},{0,3},{5,4},{6,5},{7,6},{4,7},{9,8},{10,9},{11,1... | collective-permute-start | bytes 589832 | tf_op jit(solution)/shard_map/ppermute | solution.py:45
  41.5 7.0 %collective-permute-start.4 = (bf16[128,768]{1,0:T(8,128)(2,1)S(1)}, bf16[128,768]{1,0:T(8,128)(2,1)S(1)}, u32[]{:S(2)}, u32[]{:S(2)}) collective-permute-start(bf16[128,768]{1,0:T(8,128)(2,1)S(1)} %feed.3), channel_id=1, source_target_pairs={{3,0},{0,1},{1,2},{2,3},{7,4},{4,5},{5,6},{6,7},{11,8},{8,9},{9,10... | collective-permute-start | bytes 589832 | tf_op jit(solution)/shard_map/ppermute | solution.py:45
  49.4 28.6 %copy-start.1 = (bf16[768,192]{0,1:T(8,128)(2,1)S(1)}, bf16[768,192]{0,1:T(8,128)(2,1)}, u32[]{:S(2)}) copy-start(bf16[768,192]{0,1:T(8,128)(2,1)} %param.23) | copy-start | bytes 884740
  49.4 28.6 %copy-start.2 = (bf16[768,192]{0,1:T(8,128)(2,1)S(1)}, bf16[768,192]{0,1:T(8,128)(2,1)}, u32[]{:S(2)}) copy-start(bf16[768,192]{0,1:T(8,128)(2,1)} %param.24) | copy-start | bytes 884740
  49.4 28.6 %copy-start.6 = (bf16[256,192]{0,1:T(8,128)(2,1)S(1)}, bf16[256,192]{0,1:T(8,128)(2,1)}, u32[]{:S(2)}) copy-start(bf16[256,192]{0,1:T(8,128)(2,1)} %param.25) | copy-start | bytes 294916
  49.4 3.4 %collective-permute-start.12 = (bf16[32,2,16,384]{3,2,1,0:T(8,128)(2,1)S(1)}, bf16[32,2,16,384]{3,2,1,0:T(8,128)(2,1)S(1)}, u32[]{:S(2)}, u32[]{:S(2)}) collective-permute-start(bf16[32,2,16,384]{3,2,1,0:T(8,128)(2,1)S(1)} %all-to-all-done.received_hbm), channel_id=1, source_target_pairs={{4,0},{0,4},{5,1},{1,5},{6,2},{2,6},{7,3},{3,7},{12,8},{8,12},{13,... | collective-permute-start | bytes 2359304 | tf_op jit(solution)/shard_map/ppermute | solution.py:45
  49.5 6.7 %collective-permute-start.10 = (bf16[1,768]{1,0:T(2,128)(2,1)S(1)}, bf16[1,768]{1,0:T(2,128)(2,1)S(1)}, u32[]{:S(2)}, u32[]{:S(2)}) collective-permute-start(bf16[1,768]{1,0:T(2,128)(2,1)S(1)} %pooled_row.1.own_ref), channel_id=1, source_target_pairs={{3,0},{0,1},{1,2},{2,3},{7,4},{4,5},{5,6},{6,7},{11,8},{8,9},{9,10... | collective-permute-start | bytes 4616 | tf_op jit(solution)/shard_map/ppermute | solution.py:45
  49.6 6.7 %collective-permute-start.11 = (bf16[1,768]{1,0:T(2,128)(2,1)S(1)}, bf16[1,768]{1,0:T(2,128)(2,1)S(1)}, u32[]{:S(2)}, u32[]{:S(2)}) collective-permute-start(bf16[1,768]{1,0:T(2,128)(2,1)S(1)} %pooled_row.1.own_ref), channel_id=1, source_target_pairs={{2,0},{3,1},{0,2},{1,3},{6,4},{7,5},{4,6},{5,7},{10,8},{11,9},{8,1... | collective-permute-start | bytes 4616 | tf_op jit(solution)/shard_map/ppermute | solution.py:45
  51.7 4.6 %collective-permute-start.9 = (bf16[1,768]{1,0:T(2,128)(2,1)S(1)}, bf16[1,768]{1,0:T(2,128)(2,1)S(1)}, u32[]{:S(2)}, u32[]{:S(2)}) collective-permute-start(bf16[1,768]{1,0:T(2,128)(2,1)S(1)} %pooled_row.1.own_ref), channel_id=1, source_target_pairs={{1,0},{2,1},{3,2},{0,3},{5,4},{6,5},{7,6},{4,7},{9,8},{10,9},{11,1... | collective-permute-start | bytes 4616 | tf_op jit(solution)/shard_map/ppermute | solution.py:45
  57.0 20.8 %all-to-all-start.1 = ((bf16[32,4,768]{2,1,0:T(4,128)(2,1)}), bf16[32,4,768]{2,1,0:T(4,128)(2,1)S(1)}, u32[]{:S(2)}, u32[]{:S(2)}) async-start(bf16[32,4,768]{2,1,0:T(4,128)(2,1)} %spread_rows.1), calls=%async_computation.1 | async-start | bytes 393216 | tf_op jit(solution)/shard_map/all_to_all | solution.py:664
  66.8 6.2 %collective-permute-start.13 = (bf16[256,384]{1,0:T(8,128)(2,1)S(1)}, bf16[256,384]{1,0:T(8,128)(2,1)S(1)}, u32[]{:S(2)}, u32[]{:S(2)}) collective-permute-start(bf16[256,384]{1,0:T(8,128)(2,1)S(1)} %get-tuple-element.63.refs_4_), channel_id=1, source_target_pairs={{0,1},{1,0},{2,3},{3,2},{4,5},{5,4},{6,7},{7,6},{8,9},{9,8},{10,11... | collective-permute-start | bytes 589832 | tf_op jit(solution)/shard_map/ppermute | solution.py:40
  77.8 2.9 %collective-permute-start.14 = (bf16[128,768]{1,0:T(8,128)(2,1)S(1)}, bf16[128,768]{1,0:T(8,128)(2,1)S(1)}, u32[]{:S(2)}, u32[]{:S(2)}) collective-permute-start(bf16[128,768]{1,0:T(8,128)(2,1)S(1)} %reshape.54.refs_1_), channel_id=1, source_target_pairs={{4,0},{0,4},{5,1},{1,5},{6,2},{2,6},{7,3},{3,7},{12,8},{8,12},{13,... | collective-permute-start | bytes 589832 | tf_op jit(solution)/shard_map/ppermute | solution.py:45
  82.9 1.9 %collective-permute-start.15 = (bf16[32,16,384]{2,1,0:T(8,128)(2,1)S(1)}, bf16[32,16,384]{2,1,0:T(8,128)(2,1)S(1)}, u32[]{:S(2)}, u32[]{:S(2)}) collective-permute-start(bf16[32,16,384]{2,1,0:T(8,128)(2,1)S(1)} %get-tuple-element.77), channel_id=1, source_target_pairs={{4,0},{0,4},{5,1},{1,5},{6,2},{2,6},{7,3},{3,7},{12,8},{8,12},{13,... | collective-permute-start | bytes 1179656 | tf_op jit(solution)/shard_map/ppermute | solution.py:45
  106.1 5.5 %collective-permute-start.16 = (f32[4,192]{1,0:T(4,128)S(1)}, f32[4,192]{1,0:T(4,128)S(1)}, u32[]{:S(2)}, u32[]{:S(2)}) collective-permute-start(f32[4,192]{1,0:T(4,128)S(1)} %get-tuple-element.79), channel_id=1, source_target_pairs={{2,0},{3,1},{0,2},{1,3},{6,4},{7,5},{4,6},{5,7},{10,8},{11,9},{8,1... | collective-permute-start | bytes 9224 | tf_op jit(solution)/shard_map/ppermute | solution.py:45
  108.8 3.6 %collective-permute-start.17 = (f32[4,192]{1,0:T(4,128)S(1)}, f32[4,192]{1,0:T(4,128)S(1)}, u32[]{:S(2)}, u32[]{:S(2)}) collective-permute-start(f32[4,192]{1,0:T(4,128)S(1)} %get-tuple-element.80), channel_id=1, source_target_pairs={{1,0},{2,1},{3,2},{0,3},{5,4},{6,5},{7,6},{4,7},{9,8},{10,9},{11,1... | collective-permute-start | bytes 9224 | tf_op jit(solution)/shard_map/ppermute | solution.py:45
  109.7 4.8 %collective-permute-start.18 = (f32[4,192]{1,0:T(4,128)S(1)}, f32[4,192]{1,0:T(4,128)S(1)}, u32[]{:S(2)}, u32[]{:S(2)}) collective-permute-start(f32[4,192]{1,0:T(4,128)S(1)} %get-tuple-element.81), channel_id=1, source_target_pairs={{3,0},{0,1},{1,2},{2,3},{7,4},{4,5},{5,6},{6,7},{11,8},{8,9},{9,10... | collective-permute-start | bytes 9224 | tf_op jit(solution)/shard_map/ppermute | solution.py:45
  (11 other events, 37.9 us)

commit v5 on v4

--- a/solution.py
+++ b/solution.py
@@ -427,7 +427,7 @@
     copies[4].wait()
     table_ref[...] = jnp.where(row_text >= 0, placed, hist_ref[...].astype(F32)).astype(BF)
     copies[5].wait()
-    upstream_ref[...] = up_ref[...].astype(F32).T
+    upstream_ref[...] = up_ref[...]
     for copy in copies[6:]:
         copy.wait()
 
@@ -443,7 +443,7 @@
             jax.ShapeDtypeStruct((2, count, texts), BF),
             jax.ShapeDtypeStruct(w_self.shape, BF),
             jax.ShapeDtypeStruct(w_neigh.shape, BF),
-            jax.ShapeDtypeStruct(upstream.shape[::-1], F32),
+            jax.ShapeDtypeStruct(upstream.shape, BF),
         ),
         in_specs=scalars() + whole(1) + far_off(8),
         out_specs=tuple(whole(7)),
@@ -486,7 +486,7 @@
     cdf = 0.5 * (1.0 + lax.erf(pre_act * math.sqrt(0.5)))
     density = jnp.exp(-0.5 * pre_act * pre_act) * (1.0 / math.sqrt(2.0 * math.pi))
     act_ref[...] = pre_act * cdf
-    grad_pre = (upstream_ref[...] * (cdf + pre_act * density)).astype(BF)
+    grad_pre = (upstream_ref[...].astype(F32).T * (cdf + pre_act * density)).astype(BF)
     chips = weights_ref.shape[0]
     for k, rows in enumerate((table, agg_rows)):
         part = slice(k * quarter, (k + 1) * quarter)

time: 116 us -> 116 us (level)
  no operation moved by 1% of the time
where the time goes in v5:
time: 116 us; the launch traced here: 115 us
  starting transfers between devices  43.6 us (38%)
  waiting for transfers between devices  21.8 us (19%)
  blocking collectives  20.2 us (17%)
  Pallas kernels  19.2 us (17%)
  local copies, waits for them, and re-layouts  4.91 us (4%)
  matrix products  3.34 us (3%)
    ppermute x18, starting transfers between devices, pull(): lax.ppermute(value, axis, [((i + shift) % count, i) for i in range(count)])  21.5 us
    all_to_all x1, blocking collectives, local(): lax.all_to_all(parts, ('x', 'z'), split_axis=0, concat_axis=0, tiled=True)  20.2 us
    ppermute x18, waiting for transfers between devices, pull(): lax.ppermute(value, axis, [((i + shift) % count, i) for i in range(count)])  11.9 us
    all_to_all x1, starting transfers between devices, local(): lax.all_to_all(outgoing, ('x', 'z'), split_axis=0, concat_axis=0, tiled=T...  11.2 us
    all_to_all x1, starting transfers between devices, local(): lax.all_to_all(rows, ('x', 'z'), split_axis=0, concat_axis=0, tiled=True)  9.79 us
    ppermute x1, waiting for transfers between devices, swap(): return lax.ppermute(value, 'y', [(i, i ^ 1) for i in range(NY)])  5.1 us
    all_to_all x1, waiting for transfers between devices, local(): lax.all_to_all(rows, ('x', 'z'), split_axis=0, concat_axis=0, tiled=True)  4.82 us
    unnamed x28, local copies, waits for them, and re-layouts  2.96 us
  transfers between devices with their start and end apart: 21, of which 9 were waited for; matrix products, arithmetic and copies ran while one was open for 1% of the time, Pallas kernels for 13%

profile of v5, /device:TPU:32, one launch (start us, length us, event | category | flops | bytes accessed | tf_op | source)
XLA Modules:
  0.0 115.0 jit_solution(15232859268294861845)
XLA Ops:
  1.8 1.8 %convolution_convert_fusion.1 = bf16[512,576]{0,1:T(8,128)(2,1)S(1)} fusion(bf16[512,768]{1,0:T(8,128)(2,1)} %param.13, bf16[768,576]{0,1:T(8,128)(2,1)S(1)} %bitcast.54), kind=kOutput, calls=%fused_computation.3 | convolution fusion | flops 453279744 | bytes 2260992 | tf_op jit(solution)/shard_map/dot_general | solution.py:28
  6.6 3.3 %collective-permute-start = (bf16[128,768]{1,0:T(8,128)(2,1)S(1)}, bf16[128,768]{1,0:T(8,128)(2,1)S(1)}, u32[]{:S(2)}, u32[]{:S(2)}) collective-permute-start(bf16[128,768]{1,0:T(8,128)(2,1)S(1)} %get-tuple-element.86), channel_id=1, source_target_pairs={{2,0},{3,1},{0,2},{1,3},{6,4},{7,5},{4,6},{5,7},{10,8},{11,9},{8,1... | collective-permute-start | bytes 589832 | tf_op jit(solution)/shard_map/ppermute | solution.py:45
  12.4 2.0 %outgoing_rows.1 = bf16[32,2,16,384]{3,2,1,0:T(8,128)(2,1)} custom-call(s32[7]{0:T(128)S(1)} %pad_add_fusion.refs_0_.place_ref, s32[1,256]{1,0:T(1,128)S(1)} %bitcast.61, s32[1024,1]{1,0:T(8,128)S(1)} %reshape.55.wanted_ref, bf16[256,768]{1,0:T(8,128)(2,1)S(1)} %copy-done.5), custom_call_target="tpu_custom_call" | custom-call | flops 2000000000 | bytes 6000000 | tf_op jit(solution)/shard_map/outgoing_rows/pallas_call | solution.py:267
  14.4 11.2 %all-to-all-start = ((bf16[32,2,16,384]{3,2,1,0:T(8,128)(2,1)}), bf16[32,2,16,384]{3,2,1,0:T(8,128)(2,1)S(1)}, u32[]{:S(2)}, u32[]{:S(2)}) async-start(bf16[32,2,16,384]{3,2,1,0:T(8,128)(2,1)} %outgoing_rows.1), calls=%async_computation | async-start | bytes 1572864 | tf_op jit(solution)/shard_map/all_to_all | solution.py:648
  27.7 2.4 %collective-permute-start.5 = (bf16[128,768]{1,0:T(8,128)(2,1)S(1)}, bf16[128,768]{1,0:T(8,128)(2,1)S(1)}, u32[]{:S(2)}, u32[]{:S(2)}) collective-permute-start(bf16[128,768]{1,0:T(8,128)(2,1)S(1)} %first_norm.1.block_ref.first_ref), channel_id=1, source_target_pairs={{3,0},{0,1},{1,2},{2,3},{7,4},{4,5},{5,6},{6,7},{11,8},{8,9},{9,10... | collective-permute-start | bytes 589832 | tf_op jit(solution)/shard_map/ppermute | solution.py:45
  31.0 1.3 %feed_first.1 = (f32[128,768]{1,0:T(8,128)S(1)}, bf16[768,768]{1,0:T(8,128)(2,1)S(1)}, bf16[768,768]{1,0:T(8,128)(2,1)S(1)}) custom-call(bf16[128,768]{1,0:T(8,128)(2,1)S(1)} %first_norm.1.block_ref.first_ref, bf16[768,768]{1,0:T(8,128)(2,1)S(1)} %copy-done.3, bf16[768,768]{1,0:T(8,128)(2,1)S(1)} %copy-done.4), custom_call_target="tpu_custom_call" | custom-call | flops 8000000000 | bytes 9000000 | tf_op jit(solution)/shard_map/feed_first/pallas_call | solution.py:141
  32.3 1.9 %link_counts.1.counts_hbm = bf16[1280,256]{1,0:T(8,128)(2,1)S(1)} custom-call(s32[7]{0:T(128)S(1)} %pad_add_fusion.refs_0_.place_ref, s32[10,256]{1,0:T(8,128)S(1)} %bitcast.60), custom_call_target="tpu_custom_call" | custom-call | flops 4000000000 | bytes 2000000 | tf_op jit(solution)/shard_map/link_counts/pallas_call | solution.py:299
  34.2 1.7 %collective-permute-done.7.block_ref = bf16[128,768]{1,0:T(8,128)(2,1)S(1)} collective-permute-done((bf16[128,768]{1,0:T(8,128)(2,1)S(1)}, bf16[128,768]{1,0:T(8,128)(2,1)S(1)}, u32[]{:S(2)}, u32[]{:S(2)}) %collective-permute-start.7) | collective-permute-done | bytes 196640 | tf_op jit(solution)/shard_map/ppermute | solution.py:45
  37.6 1.2 %collective-permute-done.5.block_ref = bf16[128,768]{1,0:T(8,128)(2,1)S(1)} collective-permute-done((bf16[128,768]{1,0:T(8,128)(2,1)S(1)}, bf16[128,768]{1,0:T(8,128)(2,1)S(1)}, u32[]{:S(2)}, u32[]{:S(2)}) %collective-permute-start.5) | collective-permute-done | bytes 196640 | tf_op jit(solution)/shard_map/ppermute | solution.py:45
  39.5 1.4 %collective-permute-start.6 = (bf16[128,768]{1,0:T(8,128)(2,1)S(1)}, bf16[128,768]{1,0:T(8,128)(2,1)S(1)}, u32[]{:S(2)}, u32[]{:S(2)}) collective-permute-start(bf16[128,768]{1,0:T(8,128)(2,1)S(1)} %feed.4), channel_id=1, source_target_pairs={{1,0},{2,1},{3,2},{0,3},{5,4},{6,5},{7,6},{4,7},{9,8},{10,9},{11,1... | collective-permute-start | bytes 589832 | tf_op jit(solution)/shard_map/ppermute | solution.py:45
  42.5 3.2 %collective-permute-done.8.across_ref = bf16[128,768]{1,0:T(8,128)(2,1)S(1)} collective-permute-done((bf16[128,768]{1,0:T(8,128)(2,1)S(1)}, bf16[128,768]{1,0:T(8,128)(2,1)S(1)}, u32[]{:S(2)}, u32[]{:S(2)}) %collective-permute-start.8) | collective-permute-done | bytes 196640 | tf_op jit(solution)/shard_map/ppermute | solution.py:45
  45.7 1.6 %collective-permute-done.6.far_ref = bf16[128,768]{1,0:T(8,128)(2,1)S(1)} collective-permute-done((bf16[128,768]{1,0:T(8,128)(2,1)S(1)}, bf16[128,768]{1,0:T(8,128)(2,1)S(1)}, u32[]{:S(2)}, u32[]{:S(2)}) %collective-permute-start.6) | collective-permute-done | bytes 196640 | tf_op jit(solution)/shard_map/ppermute | solution.py:45
  47.3 1.2 %collective-permute-done.4.near_ref = bf16[128,768]{1,0:T(8,128)(2,1)S(1)} collective-permute-done((bf16[128,768]{1,0:T(8,128)(2,1)S(1)}, bf16[128,768]{1,0:T(8,128)(2,1)S(1)}, u32[]{:S(2)}, u32[]{:S(2)}) %collective-permute-start.4) | collective-permute-done | bytes 196640 | tf_op jit(solution)/shard_map/ppermute | solution.py:45
  49.6 2.1 %collective-permute-start.11 = (bf16[1,768]{1,0:T(2,128)(2,1)S(1)}, bf16[1,768]{1,0:T(2,128)(2,1)S(1)}, u32[]{:S(2)}, u32[]{:S(2)}) collective-permute-start(bf16[1,768]{1,0:T(2,128)(2,1)S(1)} %pooled_row.1.own_ref), channel_id=1, source_target_pairs={{2,0},{3,1},{0,2},{1,3},{6,4},{7,5},{4,6},{5,7},{10,8},{11,9},{8,1... | collective-permute-start | bytes 4616 | tf_op jit(solution)/shard_map/ppermute | solution.py:45
  53.9 2.3 %halo_sums.1 = (bf16[256,384]{1,0:T(8,128)(2,1)S(1)}, bf16[2,256,256]{2,1,0:T(8,128)(2,1)S(1)}) custom-call(s32[7]{0:T(128)S(1)} %pad_add_fusion.refs_0_.place_ref, s32[1,256]{1,0:T(1,128)S(1)} %bitcast.62, bf16[1280,256]{1,0:T(8,128)(2,1)S(1)} %copy-done.10, bf16[256,768]{1,0:T(8,128)(2,1)S(1)} %copy-done.5, ...), custom_call_target="tpu_custom_call" | custom-call | flops 1000000000 | bytes 5000000 | tf_op jit(solution)/shard_map/halo_sums/pallas_call | solution.py:365
  57.0 9.8 %all-to-all-start.1 = ((bf16[32,4,768]{2,1,0:T(4,128)(2,1)}), bf16[32,4,768]{2,1,0:T(4,128)(2,1)S(1)}, u32[]{:S(2)}, u32[]{:S(2)}) async-start(bf16[32,4,768]{2,1,0:T(4,128)(2,1)} %spread_rows.1), calls=%async_computation.1 | async-start | bytes 393216 | tf_op jit(solution)/shard_map/all_to_all | solution.py:664
  67.9 5.1 %collective-permute-done.13.refs_5_ = bf16[256,384]{1,0:T(8,128)(2,1)S(1)} collective-permute-done((bf16[256,384]{1,0:T(8,128)(2,1)S(1)}, bf16[256,384]{1,0:T(8,128)(2,1)S(1)}, u32[]{:S(2)}, u32[]{:S(2)}) %collective-permute-start.13) | collective-permute-done | bytes 196640 | tf_op jit(solution)/shard_map/ppermute | solution.py:40
  73.0 4.8 %all-to-all-done.1 = bf16[32,4,768]{2,1,0:T(4,128)(2,1)S(1)} async-done(((bf16[32,4,768]{2,1,0:T(4,128)(2,1)}), bf16[32,4,768]{2,1,0:T(4,128)(2,1)S(1)}, u32[]{:S(2)}, u32[]{:S(2)}) %all-to-all-start.1) | async-done | bytes 196640 | tf_op jit(solution)/shard_map/all_to_all | solution.py:664
  78.0 2.7 %sage_head.1 = (bf16[256,768]{1,0:T(8,128)(2,1)S(1)}, f32[256,768]{1,0:T(8,128)S(1)}, bf16[2,256,128]{2,1,0:T(8,128)(2,1)S(1)}, bf16[2,256,256]{2,1,0:T(8,128)(2...) custom-call(s32[7]{0:T(128)S(1)} %pad_add_fusion.refs_0_.place_ref, ...), custom_call_target="tpu_custom_call" | custom-call | flops 3000000000 | bytes 4000000 | tf_op jit(solution)/shard_map/sage_head/pallas_call | solution.py:437
  80.6 2.2 %sage.1 = (f32[256,192]{1,0:T(8,128)S(1)}, f32[32,24,384]{2,1,0:T(8,128)S(1)}, f32[32,8,384]{2,1,0:T(8,128)S(1)}, bf16[32,16,384]{2,1,0:T(8,128)(2,1)S(1)}) custom-call(s32[7]{0:T(128)S(1)} %pad_add_fusion.refs_0_.place_ref, bf16[128,768]{1,0:T(8,128)(2,1)S(1)} %collective-permute-done.14.refs_1_, bf16[256,768]{1,0:T(8,128)(2,1)S(1)} %get-tuple-element.65.refs_2_, ...), custom_call_target="tpu_custom_call" | custom-call | flops 2000000000 | bytes 8000000 | tf_op jit(solution)/shard_map/sage/pallas_call | solution.py:516
  83.3 1.4 %sage_tail.1 = (bf16[192,256]{1,0:T(8,128)(2,1)}, f32[32,16,384]{2,1,0:T(8,128)S(1)}) custom-call(s32[7]{0:T(128)S(1)} %pad_add_fusion.refs_0_.place_ref, f32[256,192]{1,0:T(8,128)S(1)} %get-tuple-element.72.act_ref, f32[32,24,384]{2,1,0:T(8,128)S(1)} %get-tuple-element.73.weights_ref, f32[32,8,384]{2,1,0:T(8,128)S(1)} %get-tuple-element.74.terms_ref), custom_call_target="tpu_custom_call" | custom-call | flops 3000000000 | bytes 4000000 | tf_op jit(solution)/shard_map/sage_tail/pallas_call | solution.py:538
  84.8 20.2 %all_to_all.15.refs_1_.parts_ref = bf16[32,16,384]{2,1,0:T(8,128)(2,1)S(1)} all-to-all(bf16[32,16,384]{2,1,0:T(8,128)(2,1)S(1)} %combine.1), channel_id=1, replica_groups=mesh['x'=4,'z'=8,'c'=2,'y'=4] {'x','z'}, dimensions={0} | all-to-all | bytes 786432 | tf_op jit(solution)/shard_map/all_to_all | solution.py:676
  106.0 2.7 %collective-permute-start.16 = (f32[4,192]{1,0:T(4,128)S(1)}, f32[4,192]{1,0:T(4,128)S(1)}, u32[]{:S(2)}, u32[]{:S(2)}) collective-permute-start(f32[4,192]{1,0:T(4,128)S(1)} %get-tuple-element.79), channel_id=1, source_target_pairs={{2,0},{3,1},{0,2},{1,3},{6,4},{7,5},{4,6},{5,7},{10,8},{11,9},{8,1... | collective-permute-start | bytes 9224 | tf_op jit(solution)/shard_map/ppermute | solution.py:45
  112.3 2.1 %collective-permute-done.18 = f32[4,192]{1,0:T(4,128)S(1)} collective-permute-done((f32[4,192]{1,0:T(4,128)S(1)}, f32[4,192]{1,0:T(4,128)S(1)}, u32[]{:S(2)}, u32[]{:S(2)}) %collective-permute-start.18) | collective-permute-done | bytes 3104 | tf_op jit(solution)/shard_map/ppermute | solution.py:45
  (79 shorter events, 24.3 us)
Async XLA Ops:
  6.6 19.9 %collective-permute-start = (bf16[128,768]{1,0:T(8,128)(2,1)S(1)}, bf16[128,768]{1,0:T(8,128)(2,1)S(1)}, u32[]{:S(2)}, u32[]{:S(2)}) collective-permute-start(bf16[128,768]{1,0:T(8,128)(2,1)S(1)} %get-tuple-element.86), channel_id=1, source_target_pairs={{2,0},{3,1},{0,2},{1,3},{6,4},{7,5},{4,6},{5,7},{10,8},{11,9},{8,1... | collective-permute-start | bytes 589832 | tf_op jit(solution)/shard_map/ppermute | solution.py:45
  9.9 16.7 %collective-permute-start.1 = (bf16[128,768]{1,0:T(8,128)(2,1)S(1)}, bf16[128,768]{1,0:T(8,128)(2,1)S(1)}, u32[]{:S(2)}, u32[]{:S(2)}) collective-permute-start(bf16[128,768]{1,0:T(8,128)(2,1)S(1)} %get-tuple-element.85), channel_id=1, source_target_pairs={{1,0},{2,1},{3,2},{0,3},{5,4},{6,5},{7,6},{4,7},{9,8},{10,9},{11,1... | collective-permute-start | bytes 589832 | tf_op jit(solution)/shard_map/ppermute | solution.py:45
  11.0 15.6 %collective-permute-start.2 = (bf16[128,768]{1,0:T(8,128)(2,1)S(1)}, bf16[128,768]{1,0:T(8,128)(2,1)S(1)}, u32[]{:S(2)}, u32[]{:S(2)}) collective-permute-start(bf16[128,768]{1,0:T(8,128)(2,1)S(1)} %get-tuple-element.84), channel_id=1, source_target_pairs={{3,0},{0,1},{1,2},{2,3},{7,4},{4,5},{5,6},{6,7},{11,8},{8,9},{9,10... | collective-permute-start | bytes 589832 | tf_op jit(solution)/shard_map/ppermute | solution.py:45
  14.4 35.0 %all-to-all-start = ((bf16[32,2,16,384]{3,2,1,0:T(8,128)(2,1)}), bf16[32,2,16,384]{3,2,1,0:T(8,128)(2,1)S(1)}, u32[]{:S(2)}, u32[]{:S(2)}) async-start(bf16[32,2,16,384]{3,2,1,0:T(8,128)(2,1)} %outgoing_rows.1), calls=%async_computation | async-start | bytes 1572864 | tf_op jit(solution)/shard_map/all_to_all | solution.py:648
  26.9 9.0 %collective-permute-start.7 = (bf16[128,768]{1,0:T(8,128)(2,1)S(1)}, bf16[128,768]{1,0:T(8,128)(2,1)S(1)}, u32[]{:S(2)}, u32[]{:S(2)}) collective-permute-start(bf16[128,768]{1,0:T(8,128)(2,1)S(1)} %first_norm.1.block_ref.first_ref), channel_id=1, source_target_pairs={{2,0},{3,1},{0,2},{1,3},{6,4},{7,5},{4,6},{5,7},{10,8},{11,9},{8,1... | collective-permute-start | bytes 589832 | tf_op jit(solution)/shard_map/ppermute | solution.py:45
  27.7 11.1 %collective-permute-start.5 = (bf16[128,768]{1,0:T(8,128)(2,1)S(1)}, bf16[128,768]{1,0:T(8,128)(2,1)S(1)}, u32[]{:S(2)}, u32[]{:S(2)}) collective-permute-start(bf16[128,768]{1,0:T(8,128)(2,1)S(1)} %first_norm.1.block_ref.first_ref), channel_id=1, source_target_pairs={{3,0},{0,1},{1,2},{2,3},{7,4},{4,5},{5,6},{6,7},{11,8},{8,9},{9,10... | collective-permute-start | bytes 589832 | tf_op jit(solution)/shard_map/ppermute | solution.py:45
  30.1 10.8 %collective-permute-start.3 = (bf16[128,768]{1,0:T(8,128)(2,1)S(1)}, bf16[128,768]{1,0:T(8,128)(2,1)S(1)}, u32[]{:S(2)}, u32[]{:S(2)}) collective-permute-start(bf16[128,768]{1,0:T(8,128)(2,1)S(1)} %first_norm.1.block_ref.first_ref), channel_id=1, source_target_pairs={{1,0},{2,1},{3,2},{0,3},{5,4},{6,5},{7,6},{4,7},{9,8},{10,9},{11,1... | collective-permute-start | bytes 589832 | tf_op jit(solution)/shard_map/ppermute | solution.py:45
  36.6 9.1 %collective-permute-start.8 = (bf16[128,768]{1,0:T(8,128)(2,1)S(1)}, bf16[128,768]{1,0:T(8,128)(2,1)S(1)}, u32[]{:S(2)}, u32[]{:S(2)}) collective-permute-start(bf16[128,768]{1,0:T(8,128)(2,1)S(1)} %feed.5), channel_id=1, source_target_pairs={{2,0},{3,1},{0,2},{1,3},{6,4},{7,5},{4,6},{5,7},{10,8},{11,9},{8,1... | collective-permute-start | bytes 589832 | tf_op jit(solution)/shard_map/ppermute | solution.py:45
  39.5 7.8 %collective-permute-start.6 = (bf16[128,768]{1,0:T(8,128)(2,1)S(1)}, bf16[128,768]{1,0:T(8,128)(2,1)S(1)}, u32[]{:S(2)}, u32[]{:S(2)}) collective-permute-start(bf16[128,768]{1,0:T(8,128)(2,1)S(1)} %feed.4), channel_id=1, source_target_pairs={{1,0},{2,1},{3,2},{0,3},{5,4},{6,5},{7,6},{4,7},{9,8},{10,9},{11,1... | collective-permute-start | bytes 589832 | tf_op jit(solution)/shard_map/ppermute | solution.py:45
  41.5 7.0 %collective-permute-start.4 = (bf16[128,768]{1,0:T(8,128)(2,1)S(1)}, bf16[128,768]{1,0:T(8,128)(2,1)S(1)}, u32[]{:S(2)}, u32[]{:S(2)}) collective-permute-start(bf16[128,768]{1,0:T(8,128)(2,1)S(1)} %feed.3), channel_id=1, source_target_pairs={{3,0},{0,1},{1,2},{2,3},{7,4},{4,5},{5,6},{6,7},{11,8},{8,9},{9,10... | collective-permute-start | bytes 589832 | tf_op jit(solution)/shard_map/ppermute | solution.py:45
  49.4 28.6 %copy-start.1 = (bf16[768,192]{0,1:T(8,128)(2,1)S(1)}, bf16[768,192]{0,1:T(8,128)(2,1)}, u32[]{:S(2)}) copy-start(bf16[768,192]{0,1:T(8,128)(2,1)} %param.23) | copy-start | bytes 884740
  49.4 28.6 %copy-start.2 = (bf16[768,192]{0,1:T(8,128)(2,1)S(1)}, bf16[768,192]{0,1:T(8,128)(2,1)}, u32[]{:S(2)}) copy-start(bf16[768,192]{0,1:T(8,128)(2,1)} %param.24) | copy-start | bytes 884740
  49.4 28.6 %copy-start.6 = (bf16[256,192]{0,1:T(8,128)(2,1)S(1)}, bf16[256,192]{0,1:T(8,128)(2,1)}, u32[]{:S(2)}) copy-start(bf16[256,192]{0,1:T(8,128)(2,1)} %param.25) | copy-start | bytes 294916
  49.4 3.4 %collective-permute-start.12 = (bf16[32,2,16,384]{3,2,1,0:T(8,128)(2,1)S(1)}, bf16[32,2,16,384]{3,2,1,0:T(8,128)(2,1)S(1)}, u32[]{:S(2)}, u32[]{:S(2)}) collective-permute-start(bf16[32,2,16,384]{3,2,1,0:T(8,128)(2,1)S(1)} %all-to-all-done.received_hbm), channel_id=1, source_target_pairs={{4,0},{0,4},{5,1},{1,5},{6,2},{2,6},{7,3},{3,7},{12,8},{8,12},{13,... | collective-permute-start | bytes 2359304 | tf_op jit(solution)/shard_map/ppermute | solution.py:45
  49.5 6.7 %collective-permute-start.10 = (bf16[1,768]{1,0:T(2,128)(2,1)S(1)}, bf16[1,768]{1,0:T(2,128)(2,1)S(1)}, u32[]{:S(2)}, u32[]{:S(2)}) collective-permute-start(bf16[1,768]{1,0:T(2,128)(2,1)S(1)} %pooled_row.1.own_ref), channel_id=1, source_target_pairs={{3,0},{0,1},{1,2},{2,3},{7,4},{4,5},{5,6},{6,7},{11,8},{8,9},{9,10... | collective-permute-start | bytes 4616 | tf_op jit(solution)/shard_map/ppermute | solution.py:45
  49.6 6.7 %collective-permute-start.11 = (bf16[1,768]{1,0:T(2,128)(2,1)S(1)}, bf16[1,768]{1,0:T(2,128)(2,1)S(1)}, u32[]{:S(2)}, u32[]{:S(2)}) collective-permute-start(bf16[1,768]{1,0:T(2,128)(2,1)S(1)} %pooled_row.1.own_ref), channel_id=1, source_target_pairs={{2,0},{3,1},{0,2},{1,3},{6,4},{7,5},{4,6},{5,7},{10,8},{11,9},{8,1... | collective-permute-start | bytes 4616 | tf_op jit(solution)/shard_map/ppermute | solution.py:45
  51.7 4.6 %collective-permute-start.9 = (bf16[1,768]{1,0:T(2,128)(2,1)S(1)}, bf16[1,768]{1,0:T(2,128)(2,1)S(1)}, u32[]{:S(2)}, u32[]{:S(2)}) collective-permute-start(bf16[1,768]{1,0:T(2,128)(2,1)S(1)} %pooled_row.1.own_ref), channel_id=1, source_target_pairs={{1,0},{2,1},{3,2},{0,3},{5,4},{6,5},{7,6},{4,7},{9,8},{10,9},{11,1... | collective-permute-start | bytes 4616 | tf_op jit(solution)/shard_map/ppermute | solution.py:45
  57.0 20.8 %all-to-all-start.1 = ((bf16[32,4,768]{2,1,0:T(4,128)(2,1)}), bf16[32,4,768]{2,1,0:T(4,128)(2,1)S(1)}, u32[]{:S(2)}, u32[]{:S(2)}) async-start(bf16[32,4,768]{2,1,0:T(4,128)(2,1)} %spread_rows.1), calls=%async_computation.1 | async-start | bytes 393216 | tf_op jit(solution)/shard_map/all_to_all | solution.py:664
  66.8 6.2 %collective-permute-start.13 = (bf16[256,384]{1,0:T(8,128)(2,1)S(1)}, bf16[256,384]{1,0:T(8,128)(2,1)S(1)}, u32[]{:S(2)}, u32[]{:S(2)}) collective-permute-start(bf16[256,384]{1,0:T(8,128)(2,1)S(1)} %get-tuple-element.63.refs_4_), channel_id=1, source_target_pairs={{0,1},{1,0},{2,3},{3,2},{4,5},{5,4},{6,7},{7,6},{8,9},{9,8},{10,11... | collective-permute-start | bytes 589832 | tf_op jit(solution)/shard_map/ppermute | solution.py:40
  77.8 2.8 %collective-permute-start.14 = (bf16[128,768]{1,0:T(8,128)(2,1)S(1)}, bf16[128,768]{1,0:T(8,128)(2,1)S(1)}, u32[]{:S(2)}, u32[]{:S(2)}) collective-permute-start(bf16[128,768]{1,0:T(8,128)(2,1)S(1)} %reshape.54.refs_1_), channel_id=1, source_target_pairs={{4,0},{0,4},{5,1},{1,5},{6,2},{2,6},{7,3},{3,7},{12,8},{8,12},{13,... | collective-permute-start | bytes 589832 | tf_op jit(solution)/shard_map/ppermute | solution.py:45
  82.8 1.9 %collective-permute-start.15 = (bf16[32,16,384]{2,1,0:T(8,128)(2,1)S(1)}, bf16[32,16,384]{2,1,0:T(8,128)(2,1)S(1)}, u32[]{:S(2)}, u32[]{:S(2)}) collective-permute-start(bf16[32,16,384]{2,1,0:T(8,128)(2,1)S(1)} %get-tuple-element.77), channel_id=1, source_target_pairs={{4,0},{0,4},{5,1},{1,5},{6,2},{2,6},{7,3},{3,7},{12,8},{8,12},{13,... | collective-permute-start | bytes 1179656 | tf_op jit(solution)/shard_map/ppermute | solution.py:45
  106.0 5.5 %collective-permute-start.16 = (f32[4,192]{1,0:T(4,128)S(1)}, f32[4,192]{1,0:T(4,128)S(1)}, u32[]{:S(2)}, u32[]{:S(2)}) collective-permute-start(f32[4,192]{1,0:T(4,128)S(1)} %get-tuple-element.79), channel_id=1, source_target_pairs={{2,0},{3,1},{0,2},{1,3},{6,4},{7,5},{4,6},{5,7},{10,8},{11,9},{8,1... | collective-permute-start | bytes 9224 | tf_op jit(solution)/shard_map/ppermute | solution.py:45
  108.7 3.6 %collective-permute-start.17 = (f32[4,192]{1,0:T(4,128)S(1)}, f32[4,192]{1,0:T(4,128)S(1)}, u32[]{:S(2)}, u32[]{:S(2)}) collective-permute-start(f32[4,192]{1,0:T(4,128)S(1)} %get-tuple-element.80), channel_id=1, source_target_pairs={{1,0},{2,1},{3,2},{0,3},{5,4},{6,5},{7,6},{4,7},{9,8},{10,9},{11,1... | collective-permute-start | bytes 9224 | tf_op jit(solution)/shard_map/ppermute | solution.py:45
  109.6 4.8 %collective-permute-start.18 = (f32[4,192]{1,0:T(4,128)S(1)}, f32[4,192]{1,0:T(4,128)S(1)}, u32[]{:S(2)}, u32[]{:S(2)}) collective-permute-start(f32[4,192]{1,0:T(4,128)S(1)} %get-tuple-element.81), channel_id=1, source_target_pairs={{3,0},{0,1},{1,2},{2,3},{7,4},{4,5},{5,6},{6,7},{11,8},{8,9},{9,10... | collective-permute-start | bytes 9224 | tf_op jit(solution)/shard_map/ppermute | solution.py:45
  (11 other events, 37.9 us)
